TPU v7x, 32 devices: a whole 2x2x4 slice. The times are simulated.
32 devices in a mesh: dp: 4 (over y, x), ctx: 8 (over z, core).
Axes of the slice: x: 2, y: 2, z: 4, core: 2. Of those that a mesh axis runs over, the one named last changes fastest.
Arguments:
- inputs: bfloat16 [1024, 8, 1088], P('ctx', 'dp'), may hold values from -6 to 6
- segments: int32 [8, 1024], P('dp', 'ctx'), may hold values from 0 to 3, as said below
- ln1_gain: float32 [1088], replicated, may hold values from 0.1 to 1.9
- ln1_bias: float32 [1088], replicated, may hold values from -3 to 3
- qkv_weight: bfloat16 [1088, 3264], P('ctx', 'dp'), may hold values from -0.1875 to 0.1875
- query_bias: float32 [1088], replicated, may hold values from -3 to 3
- value_bias: float32 [1088], replicated, may hold values from -3 to 3
- proj_weight: bfloat16 [1088, 1088], P('ctx', 'dp'), may hold values from -0.5 to 0.5
- proj_bias: float32 [1088], replicated, may hold values from -3 to 3
- ln2_gain: float32 [1088], replicated, may hold values from 0.1 to 1.9
- ln2_bias: float32 [1088], replicated, may hold values from -3 to 3
- fc_weight: bfloat16 [1088, 4352], P(None, ('dp', 'ctx')), may hold values from -0.1875 to 0.1875
- fc_bias: bfloat16 [4352], P(('dp', 'ctx')), may hold values from -3 to 3
- out_weight: bfloat16 [4352, 1088], P(('dp', 'ctx')), may hold values from -0.09375 to 0.09375
- out_bias: float32 [1088], replicated, may hold values from -3 to 3
- cotangent: bfloat16 [1024, 8, 1088], P('ctx', 'dp'), may hold values from -6 to 6
Outputs:
- output: bfloat16 [1024, 8, 1088], P('ctx', 'dp')
- input_grad: bfloat16 [1024, 8, 1088], P('ctx', 'dp')
- ln1_gain_grad: float32 [1088], replicated
- ln1_bias_grad: float32 [1088], replicated
- qkv_weight_grad: float32 [1088, 3264], P('ctx', 'dp')
- query_bias_grad: float32 [1088], replicated
- value_bias_grad: float32 [1088], replicated
- proj_weight_grad: float32 [1088, 1088], P('ctx', 'dp')
- proj_bias_grad: float32 [1088], replicated
- ln2_gain_grad: float32 [1088], replicated
- ln2_bias_grad: float32 [1088], replicated
- fc_weight_grad: float32 [1088, 4352], P(None, ('dp', 'ctx'))
- fc_bias_grad: float32 [4352], P(('dp', 'ctx'))
- out_weight_grad: float32 [4352, 1088], P(('dp', 'ctx'))
- out_bias_grad: float32 [1088], replicated
Inputs may be any that keep to these rules, and one draw needn't show every extreme that they name: `segments`: segment numbers start at 0 in every sequence and never fall along it. In every aligned run of 2 sequences, one sequence is a single document.
All inputs are finite; a program needn't handle non-finite values.
Results may differ from a plain program's by a relative error of at most 0.02.
Values may be sent and summed in bfloat16 or wider, within the bound.
A program may use at most 320 MiB of HBM per device.

v0:
```python
import math

import jax
import jax.numpy as jnp
from jax import lax
from jax.sharding import PartitionSpec as P

HEADS = 17
HEAD_DIM = 64
FF = 4352
MICRO = 2


EPSILON = 1e-05
MASKED = -1e30


def passed_along(value, axis, steps):
    count = lax.axis_size(axis)
    leading, last = (max(0, -steps), min(count, count - steps))
    return lax.ppermute(value, axis, [(source, source + steps) for source in range(leading, last)])


def from_behind(block, axis, distance):
    devices = range(lax.axis_size(axis))
    route = [((i - distance) % len(devices), i) for i in devices]
    return lax.ppermute(block, axis, route)


def normalize(values, gain_row, shift_row):
    center = values - jnp.mean(values, -1, keepdims=True)
    spread = jnp.mean(center * center, -1, keepdims=True)
    return center * lax.rsqrt(spread + EPSILON) * gain_row + shift_row


def gelu_tanh(values):
    return jax.nn.gelu(values, approximate=True)


def project(operand, weight):
    return jnp.einsum("rsd,dn->rsn", operand, weight, preferred_element_type=jnp.float32)


def project_back(operand, weight):
    return jnp.einsum("rsn,dn->rsd", operand, weight, preferred_element_type=jnp.float32)


def outer_sum(operand, gradient):
    return jnp.einsum("rsd,rsn->dn", operand, gradient, preferred_element_type=jnp.float32)


def column_sum(gradient):
    return jnp.sum(gradient.astype(jnp.float32), (0, 1))


def gather_rows(attn_pair):
    return (
        lax.all_gather(attn_pair[0], "ctx", axis=0, tiled=True),
        lax.all_gather(attn_pair[1], "ctx", axis=0, tiled=True),
    )


def gather_columns(attn_pair):
    return (
        lax.all_gather(attn_pair[0], "dp", axis=1, tiled=True),
        lax.all_gather(attn_pair[1], "dp", axis=1, tiled=True),
    )


def scatter_rows(attn_pair):
    return (
        lax.psum_scatter(
            attn_pair[0].astype(jnp.bfloat16), "ctx", scatter_dimension=0, tiled=True
        ).astype(jnp.float32),
        lax.psum_scatter(
            attn_pair[1].astype(jnp.bfloat16), "ctx", scatter_dimension=0, tiled=True
        ).astype(jnp.float32),
    )


def scatter_columns(attn_pair):
    return (
        lax.psum_scatter(
            attn_pair[0].astype(jnp.bfloat16), "dp", scatter_dimension=1, tiled=True
        ).astype(jnp.float32),
        lax.psum_scatter(
            attn_pair[1].astype(jnp.bfloat16), "dp", scatter_dimension=1, tiled=True
        ).astype(jnp.float32),
    )


def fetch_weights(qkv_weight, proj_weight, fc_weight, fc_bias, out_weight):
    attn_pair = gather_columns(gather_rows((qkv_weight, proj_weight)))
    mlp_triple = (
        lax.all_gather(fc_weight, ("dp", "ctx"), axis=1, tiled=True),
        lax.all_gather(fc_bias, ("dp", "ctx"), axis=0, tiled=True),
        lax.all_gather(out_weight, ("dp", "ctx"), axis=0, tiled=True),
    )
    return tuple(attn_pair) + tuple(mlp_triple)


def masked_scores(queries, key_rows, key_segments, key_first, query_segments, query_pos):
    key_count, seq_count, model_width = key_rows.shape
    head_count, head_size = (queries.shape[2], queries.shape[3])
    keys_split = key_rows.reshape(key_count, seq_count, head_count, head_size)
    scores = jnp.einsum(
        "qshe,kshe->shqk", queries, keys_split, preferred_element_type=jnp.float32
    ) * head_size ** (-0.5)
    key_pos = key_first + jnp.arange(key_count, dtype=jnp.int32)
    causal = key_pos[None, :] <= query_pos[:, None]
    key_docs = jnp.transpose(key_segments.astype(jnp.float32))
    same_doc = query_segments[:, None, :, None] == key_docs[:, None, None, :]
    allowed = causal[None, None] & same_doc
    return (jnp.where(allowed, scores, MASKED), allowed)


def split_blocks(arrived):
    piece_rows = arrived[0].shape[0]
    block_rows = math.gcd(piece_rows, 512)
    blocks = tuple(
        (
            member.reshape((piece_rows // block_rows, block_rows) + member.shape[1:])
            for member in arrived
        )
    )
    offsets = block_rows * jnp.arange(piece_rows // block_rows, dtype=jnp.int32)
    return blocks + (offsets,)


def layer_step(weights_full, vectors, inputs_mb, cotan_mb, segments_mb):
    w_qkv, w_proj, w_fc, b_fc, w_out = weights_full
    ln1_gain, ln1_bias, query_bias, value_bias, proj_bias, ln2_gain, ln2_bias, out_bias = vectors
    seq_rows, seq_count, model_width = inputs_mb.shape
    cycle_size = lax.axis_size("ctx")
    cycle_index = lax.axis_index("ctx")
    query_pos = cycle_index * seq_rows + jnp.arange(seq_rows, dtype=jnp.int32)
    score_scale = HEAD_DIM ** (-0.5)
    inputs_f = inputs_mb.astype(jnp.float32)
    normed_f, ln1_back = jax.vjp(normalize, inputs_f, ln1_gain, ln1_bias)
    normed = normed_f.astype(jnp.bfloat16)
    qkv_bias = jnp.concatenate([query_bias, jnp.zeros_like(query_bias), value_bias])
    joined = project(normed, w_qkv) + qkv_bias
    queries = (
        joined[..., :model_width].astype(jnp.bfloat16).reshape(seq_rows, seq_count, HEADS, HEAD_DIM)
    )
    key_rows = joined[..., model_width : 2 * model_width].astype(jnp.bfloat16)
    value_rows = joined[..., 2 * model_width :].astype(jnp.bfloat16)
    query_segments = segments_mb.astype(jnp.float32)
    key_segments = jnp.transpose(segments_mb).astype(jnp.bfloat16)
    start_max = jnp.full((seq_count, HEADS, seq_rows), MASKED, jnp.float32)
    start_total = jnp.zeros((seq_count, HEADS, seq_rows), jnp.float32)

    def block_step(current, element):
        key_block, seg_block, offset = element
        scores, allowed = masked_scores(
            queries, key_block, seg_block, offset, query_segments, query_pos
        )
        row_max, row_total = current
        new_max = jnp.maximum(row_max, jnp.max(scores, -1))
        powers = jnp.where(allowed, jnp.exp(scores - new_max[..., None]), 0.0)
        row_total = row_total * jnp.exp(row_max - new_max) + jnp.sum(powers, -1)
        return ((new_max, row_total), None)

    row_max, row_total = lax.scan(
        block_step,
        (start_max, start_total),
        split_blocks(
            (
                lax.all_gather(key_rows, "ctx", axis=0, tiled=True),
                lax.all_gather(key_segments, "ctx", axis=0, tiled=True),
            )
        ),
    )[0]

    def probabilities(scores, allowed):
        return jnp.where(allowed, jnp.exp(scores - row_max[..., None]) / row_total[..., None], 0.0)

    zero_heads = jnp.zeros((seq_rows, seq_count, HEADS, HEAD_DIM), jnp.float32)

    def block_step(current, element):
        key_block, value_block, seg_block, offset = element
        scores, allowed = masked_scores(
            queries, key_block, seg_block, offset, query_segments, query_pos
        )
        prob_f = probabilities(scores, allowed)
        prob_low = prob_f.astype(jnp.bfloat16)
        residue = (prob_f - prob_low.astype(jnp.float32)).astype(jnp.bfloat16)
        value_split = value_block.reshape(value_block.shape[0], seq_count, HEADS, HEAD_DIM)
        summed, remainder = current
        summed = summed + jnp.einsum(
            "shqk,kshe->qshe", prob_low, value_split, preferred_element_type=jnp.float32
        )
        remainder = remainder + jnp.einsum(
            "shqk,kshe->qshe", residue, value_split, preferred_element_type=jnp.float32
        )
        return ((summed, remainder), None)

    summed, remainder = lax.scan(
        block_step,
        (zero_heads, zero_heads),
        split_blocks(
            (
                lax.all_gather(key_rows, "ctx", axis=0, tiled=True),
                lax.all_gather(value_rows, "ctx", axis=0, tiled=True),
                lax.all_gather(key_segments, "ctx", axis=0, tiled=True),
            )
        ),
    )[0]
    attended = summed.reshape(seq_rows, seq_count, model_width).astype(jnp.bfloat16)
    exact_out = summed + remainder
    resid = inputs_f + project(attended, w_proj) + proj_bias
    hidden_f, ln2_back = jax.vjp(normalize, resid, ln2_gain, ln2_bias)
    hidden_in = hidden_f.astype(jnp.bfloat16)
    pre_fc = project(hidden_in, w_fc) + b_fc.astype(jnp.float32)
    activated_f, gelu_back = jax.vjp(gelu_tanh, pre_fc)
    activated = activated_f.astype(jnp.bfloat16)
    output_mb = (resid + project(activated, w_out) + out_bias).astype(jnp.bfloat16)
    out_bias_grad = column_sum(cotan_mb)
    out_weight_grad = outer_sum(activated, cotan_mb)
    d_activated = project_back(cotan_mb, w_out)
    d_pre_fc = gelu_back(d_activated)[0].astype(jnp.bfloat16)
    fc_bias_grad = column_sum(d_pre_fc)
    fc_weight_grad = outer_sum(hidden_in, d_pre_fc)
    d_hidden = project_back(d_pre_fc, w_fc)
    d_resid_part, ln2_gain_grad, ln2_bias_grad = ln2_back(d_hidden)
    d_resid = cotan_mb.astype(jnp.float32) + d_resid_part
    d_branch = d_resid.astype(jnp.bfloat16)
    proj_bias_grad = column_sum(d_branch)
    proj_weight_grad = outer_sum(attended, d_branch)
    d_att = project_back(d_branch, w_proj).astype(jnp.bfloat16)
    d_att_heads = d_att.reshape(seq_rows, seq_count, HEADS, HEAD_DIM)
    row_delta = jnp.transpose(jnp.sum(d_att_heads.astype(jnp.float32) * exact_out, -1), (1, 2, 0))

    def cycle_step(turn, running):
        key_block, value_block, seg_block, key_grad, value_grad, query_grad = running
        holder_index = (cycle_index - turn) % cycle_size
        scores, allowed = masked_scores(
            queries, key_block, seg_block, holder_index * seq_rows, query_segments, query_pos
        )
        prob_f = probabilities(scores, allowed)
        key_split = key_block.reshape(seq_rows, seq_count, HEADS, HEAD_DIM)
        value_split = value_block.reshape(seq_rows, seq_count, HEADS, HEAD_DIM)
        d_prob = jnp.einsum(
            "qshe,kshe->shqk", d_att_heads, value_split, preferred_element_type=jnp.float32
        )
        d_raw = (prob_f * (d_prob - row_delta[..., None]) * score_scale).astype(jnp.bfloat16)
        query_grad = query_grad + jnp.einsum(
            "shqk,kshe->qshe", d_raw, key_split, preferred_element_type=jnp.float32
        ).reshape(seq_rows, seq_count, model_width)
        key_grad = key_grad + jnp.einsum(
            "shqk,qshe->kshe", d_raw, queries, preferred_element_type=jnp.float32
        ).reshape(seq_rows, seq_count, model_width)
        value_grad = value_grad + jnp.einsum(
            "shqk,qshe->kshe",
            prob_f.astype(jnp.bfloat16),
            d_att_heads,
            preferred_element_type=jnp.float32,
        ).reshape(seq_rows, seq_count, model_width)
        key_block, value_block, seg_block = passed_along(
            (key_block, value_block, seg_block), "ctx", 1
        )
        key_grad, value_grad = (
            from_behind(key_grad.astype(jnp.bfloat16), "ctx", 1).astype(key_grad.dtype),
            from_behind(value_grad.astype(jnp.bfloat16), "ctx", 1).astype(value_grad.dtype),
        )
        return (key_block, value_block, seg_block, key_grad, value_grad, query_grad)

    zero_rows = jnp.zeros((seq_rows, seq_count, model_width), jnp.float32)
    finished = lax.fori_loop(
        0,
        cycle_size,
        cycle_step,
        (key_rows, value_rows, key_segments, zero_rows, zero_rows, zero_rows),
    )
    d_joined = jnp.concatenate([finished[5], finished[3], finished[4]], -1).astype(jnp.bfloat16)
    query_bias_grad = column_sum(d_joined[..., :model_width])
    value_bias_grad = column_sum(d_joined[..., 2 * model_width :])
    qkv_weight_grad = outer_sum(normed, d_joined)
    d_normed = project_back(d_joined, w_qkv)
    d_input_part, ln1_gain_grad, ln1_bias_grad = ln1_back(d_normed)
    input_grad_mb = (d_resid + d_input_part).astype(jnp.bfloat16)
    gradients = (
        ln1_gain_grad,
        ln1_bias_grad,
        qkv_weight_grad,
        query_bias_grad,
        value_bias_grad,
        proj_weight_grad,
        proj_bias_grad,
        ln2_gain_grad,
        ln2_bias_grad,
        fc_weight_grad,
        fc_bias_grad,
        out_weight_grad,
        out_bias_grad,
    )
    return (output_mb, input_grad_mb, gradients)


def local(
    inputs,
    segments,
    ln1_gain,
    ln1_bias,
    qkv_weight,
    query_bias,
    value_bias,
    proj_weight,
    proj_bias,
    ln2_gain,
    ln2_bias,
    fc_weight,
    fc_bias,
    out_weight,
    out_bias,
    cotangent,
):
    seq_rows, local_seqs, model_width = inputs.shape
    batch_seqs = local_seqs // MICRO
    vectors = (ln1_gain, ln1_bias, query_bias, value_bias, proj_bias, ln2_gain, ln2_bias, out_bias)
    inputs_split = jnp.moveaxis(inputs.reshape(seq_rows, MICRO, batch_seqs, model_width), 1, 0)
    cotan_split = jnp.moveaxis(cotangent.reshape(seq_rows, MICRO, batch_seqs, model_width), 1, 0)
    segments_split = segments.reshape(MICRO, batch_seqs, seq_rows)

    def run_batch(totals, element):
        inputs_mb, cotan_mb, segments_mb = element
        weights_full = fetch_weights(qkv_weight, proj_weight, fc_weight, fc_bias, out_weight)
        output_mb, input_grad_mb, gradients = layer_step(
            weights_full, vectors, inputs_mb, cotan_mb, segments_mb
        )
        totals = tuple((summed + addend for summed, addend in zip(totals, gradients)))
        return (totals, (output_mb, input_grad_mb))

    def zero_vector(length_rows):
        return jnp.zeros((length_rows,), jnp.float32)

    zero_totals = (
        zero_vector(model_width),
        zero_vector(model_width),
        jnp.zeros((model_width, 3 * model_width), jnp.float32),
        zero_vector(model_width),
        zero_vector(model_width),
        jnp.zeros((model_width, model_width), jnp.float32),
        zero_vector(model_width),
        zero_vector(model_width),
        zero_vector(model_width),
        jnp.zeros((model_width, FF), jnp.float32),
        zero_vector(FF),
        jnp.zeros((FF, model_width), jnp.float32),
        zero_vector(model_width),
    )
    totals, (outputs, input_grads) = lax.scan(
        run_batch, zero_totals, (inputs_split, cotan_split, segments_split)
    )
    (
        ln1_gain_grad,
        ln1_bias_grad,
        qkv_grad,
        query_bias_grad,
        value_bias_grad,
        proj_grad,
        proj_bias_grad,
        ln2_gain_grad,
        ln2_bias_grad,
        fc_grad,
        fc_bias_grad,
        out_grad,
        out_bias_grad,
    ) = totals
    vector_sums = lax.psum(
        (
            ln1_gain_grad,
            ln1_bias_grad,
            query_bias_grad,
            value_bias_grad,
            proj_bias_grad,
            ln2_gain_grad,
            ln2_bias_grad,
            out_bias_grad,
        ),
        ("dp", "ctx"),
    )
    qkv_grad, proj_grad = scatter_rows(scatter_columns((qkv_grad, proj_grad)))
    fc_grad, fc_bias_grad, out_grad = (
        lax.psum_scatter(fc_grad, ("dp", "ctx"), scatter_dimension=1, tiled=True),
        lax.psum_scatter(fc_bias_grad, ("dp", "ctx"), scatter_dimension=0, tiled=True),
        lax.psum_scatter(out_grad, ("dp", "ctx"), scatter_dimension=0, tiled=True),
    )
    output = jnp.moveaxis(outputs, 0, 1).reshape(seq_rows, local_seqs, model_width)
    input_grad = jnp.moveaxis(input_grads, 0, 1).reshape(seq_rows, local_seqs, model_width)
    return (
        output,
        input_grad,
        vector_sums[0],
        vector_sums[1],
        qkv_grad,
        vector_sums[2],
        vector_sums[3],
        proj_grad,
        vector_sums[4],
        vector_sums[5],
        vector_sums[6],
        fc_grad,
        fc_bias_grad,
        out_grad,
        vector_sums[7],
    )


def solution(mesh):
    return jax.shard_map(
        local,
        mesh=mesh,
        in_specs=(
            P("ctx", "dp", None),
            P("dp", "ctx"),
            P(),
            P(),
            P("ctx", "dp"),
            P(),
            P(),
            P("ctx", "dp"),
            P(),
            P(),
            P(),
            P(None, ("dp", "ctx")),
            P(("dp", "ctx")),
            P(("dp", "ctx"), None),
            P(),
            P("ctx", "dp", None),
        ),
        out_specs=(
            P("ctx", "dp", None),
            P("ctx", "dp", None),
            P(),
            P(),
            P("ctx", "dp"),
            P(),
            P(),
            P("ctx", "dp"),
            P(),
            P(),
            P(),
            P(None, ("dp", "ctx")),
            P(("dp", "ctx")),
            P(("dp", "ctx"), None),
            P(),
        ),
        check_vma=False,
    )
```

profile of v0, /device:TPU:0, one launch (start us, length us, event | category | flops | bytes accessed | tf_op | source)
XLA Modules:
  0.0 2068.6 jit_solution(9062763358178012316)
XLA Ops:
  8.2 1334.9 %while.132 = (s32[]{:T(128)}, f32[1088]{0:T(1024)}, f32[1088]{0:T(1024)}, f32[1088,3264]{1,0:T(8,128)}, f32[1088]{0:T(1024)}, /*index=5*/f32[1088]{0:T(1024)}, f...) while((s32[]{:T(128)}, f32[1088]{0:T(1024)}, ...), condition=%wide.region_27.28_spmd.clone, body=%wide.region_0.27_spmd.clone.sunk | while | flops 11754915840 | bytes 619384768 | solution.py:352
  9.2 32.4 %all-gather.12.cloned.1.call-done = bf16[1088,816]{1,0:T(8,128)(2,1)} async-done(((bf16[136,816]{1,0:T(8,128)(2,1)}), bf16[1088,816]{1,0:T(8,128)(2,1)}) %all-gather.12.cloned.1.call-update) | async-done | bytes 1775632 | tf_op jit(solution)/shard_map/while/body/eval_jaxpr/all_gather | solution.py:58
  46.1 79.5 %all-gather.14.cloned.1.call-done = bf16[1088,3264]{0,1:T(8,128)(2,1)} async-done(((bf16[1088,816]{0,1:T(8,128)(2,1)}), bf16[1088,3264]{0,1:T(8,128)(2,1)}) %all-gather.14.cloned.1.call-update) | async-done | bytes 7102480 | tf_op jit(solution)/shard_map/while/body/eval_jaxpr/all_gather | solution.py:65
  125.6 5.4 fusion.187
  132.7 18.6 all_gather.81
  153.9 12.1 all-gather.3
  166.3 41.4 %all-reduce.12 = bf16[4352]{0:T(1024)(128)(2,1)S(1)} all-reduce(bf16[4352]{0:T(1024)(128)(2,1)S(1)} %dynamic-update-slice.3), channel_id=1, replica_groups=mesh['dp'=4,'ctx'=8] {'dp','ctx'}, use_global_device_ids=true, to_apply=%add | all-reduce | flops 4352 | bytes 17408 | tf_op jit(solution)/shard_map/while
  213.5 18.2 while.133
  231.8 30.1 %while.134 = (s32[]{:T(128)}, f32[128,1,17,64]{0,3,2,1:T(8,128)}, f32[128,1,17,64]{0,3,2,1:T(8,128)}, bf16[2,512,1,1088]{1,3,2,0:T(8,128)(2,1)}, s32[2]{0:T(128)...) while((s32[]{:T(128)}, f32[128,1,17,64]{0,3,2,1:T(8,128)}, ...), condition=%wide.region_8.8_spmd.clone, body=%wide.region_7.7_spmd.clone.sunk | while | flops 439714944 | bytes 41660100 | solution.py:198
  239.5 5.2 fusion.205
  253.7 5.3 fusion.205
  265.9 62.5 %all-gather.22.cloned.1.call-done = bf16[1088,4352]{0,1:T(8,128)(2,1)} async-done(((bf16[1088,136]{0,1:T(8,128)(2,1)}), bf16[1088,4352]{0,1:T(8,128)(2,1)}) %all-gather.22.cloned.1.call-update) | async-done | bytes 9469968 | tf_op jit(solution)/shard_map/while/body/eval_jaxpr/all_gather | solution.py:95
  328.4 7.3 convolution_add_fusion.13
  335.6 79.0 %all-gather.24.cloned.1.call-done = bf16[4352,1088]{1,0:T(8,128)(2,1)} async-done(((bf16[136,1088]{1,0:T(8,128)(2,1)}), bf16[4352,1088]{1,0:T(8,128)(2,1)}) %all-gather.24.cloned.1.call-update) | async-done | bytes 9469968 | tf_op jit(solution)/shard_map/while/body/eval_jaxpr/all_gather | solution.py:97
  414.7 7.0 convert_reduce_fusion.12
  430.5 183.4 %while.135 = (s32[]{:T(128)}, bf16[128,1,1088]{0,2,1:T(8,128)(2,1)}, bf16[128,1,1088]{0,2,1:T(8,128)(2,1)S(1)}, bf16[128,1]{0,1:T(2,128)(2,1)S(1)}, f32[128,1,10...) while((s32[]{:T(128)}, bf16[128,1,1088]{0,2,1:T(8,128)(2,1)}, ...), condition=%wide.region_15.15_spmd.clone, body=%wide.region_14.14_spmd.clone.sunk | while | flops 182485392 | bytes 20397332 | solution.py:269
  446.4 5.3 collective-permute-done.3
  468.7 5.8 collective-permute-done.3
  491.4 5.3 collective-permute-done.3
  514.1 5.3 collective-permute-done.3
  536.4 5.8 collective-permute-done.3
  559.1 5.3 collective-permute-done.3
  581.9 5.3 collective-permute-done.3
  604.2 5.8 collective-permute-done.3
  615.0 6.3 fusion.192
  622.5 9.8 convolution_add_fusion.16
  636.6 6.5 convolution_add_fusion.14
  643.2 13.1 convolution_add_fusion.17
  659.1 8.2 fusion.194
  669.5 26.9 %all-gather.12.cloned.1.call-done = bf16[1088,816]{1,0:T(8,128)(2,1)} async-done(((bf16[136,816]{1,0:T(8,128)(2,1)}), bf16[1088,816]{1,0:T(8,128)(2,1)}) %all-gather.12.cloned.1.call-update) | async-done | bytes 1775632 | tf_op jit(solution)/shard_map/while/body/eval_jaxpr/all_gather | solution.py:58
  701.0 79.5 %all-gather.14.cloned.1.call-done = bf16[1088,3264]{0,1:T(8,128)(2,1)} async-done(((bf16[1088,816]{0,1:T(8,128)(2,1)}), bf16[1088,3264]{0,1:T(8,128)(2,1)}) %all-gather.14.cloned.1.call-update) | async-done | bytes 7102480 | tf_op jit(solution)/shard_map/while/body/eval_jaxpr/all_gather | solution.py:65
  780.5 5.4 fusion.187
  787.7 18.9 all_gather.81
  809.2 11.8 all-gather.3
  821.3 41.7 %all-reduce.12 = bf16[4352]{0:T(1024)(128)(2,1)S(1)} all-reduce(bf16[4352]{0:T(1024)(128)(2,1)S(1)} %dynamic-update-slice.3), channel_id=1, replica_groups=mesh['dp'=4,'ctx'=8] {'dp','ctx'}, use_global_device_ids=true, to_apply=%add | all-reduce | flops 4352 | bytes 17408 | tf_op jit(solution)/shard_map/while
  869.4 18.2 while.133
  887.6 29.7 %while.134 = (s32[]{:T(128)}, f32[128,1,17,64]{0,3,2,1:T(8,128)}, f32[128,1,17,64]{0,3,2,1:T(8,128)}, bf16[2,512,1,1088]{1,3,2,0:T(8,128)(2,1)}, s32[2]{0:T(128)...) while((s32[]{:T(128)}, f32[128,1,17,64]{0,3,2,1:T(8,128)}, ...), condition=%wide.region_8.8_spmd.clone, body=%wide.region_7.7_spmd.clone.sunk | while | flops 439714944 | bytes 41660100 | solution.py:198
  909.5 5.3 fusion.205
  921.3 62.1 %all-gather.22.cloned.1.call-done = bf16[1088,4352]{0,1:T(8,128)(2,1)} async-done(((bf16[1088,136]{0,1:T(8,128)(2,1)}), bf16[1088,4352]{0,1:T(8,128)(2,1)}) %all-gather.22.cloned.1.call-update) | async-done | bytes 9469968 | tf_op jit(solution)/shard_map/while/body/eval_jaxpr/all_gather | solution.py:95
  983.4 7.3 convolution_add_fusion.13
  990.7 78.9 %all-gather.24.cloned.1.call-done = bf16[4352,1088]{1,0:T(8,128)(2,1)} async-done(((bf16[136,1088]{1,0:T(8,128)(2,1)}), bf16[4352,1088]{1,0:T(8,128)(2,1)}) %all-gather.24.cloned.1.call-update) | async-done | bytes 9469968 | tf_op jit(solution)/shard_map/while/body/eval_jaxpr/all_gather | solution.py:97
  1069.6 7.0 convert_reduce_fusion.12
  1085.4 183.4 %while.135 = (s32[]{:T(128)}, bf16[128,1,1088]{0,2,1:T(8,128)(2,1)}, bf16[128,1,1088]{0,2,1:T(8,128)(2,1)S(1)}, bf16[128,1]{0,1:T(2,128)(2,1)S(1)}, f32[128,1,10...) while((s32[]{:T(128)}, bf16[128,1,1088]{0,2,1:T(8,128)(2,1)}, ...), condition=%wide.region_15.15_spmd.clone, body=%wide.region_14.14_spmd.clone.sunk | while | flops 182485392 | bytes 20397332 | solution.py:269
  1101.3 5.3 collective-permute-done.3
  1123.6 5.8 collective-permute-done.3
  1146.3 5.3 collective-permute-done.3
  1169.1 5.3 collective-permute-done.3
  1191.4 5.8 collective-permute-done.3
  1214.1 5.3 collective-permute-done.3
  1236.8 5.3 collective-permute-done.3
  1259.1 5.7 collective-permute-done.3
  1269.9 6.3 fusion.192
  1277.5 15.4 convolution_add_fusion.16
  1293.0 5.6 convolution_add_fusion.15
  1298.7 6.5 convolution_add_fusion.14
  1305.4 21.5 %convolution_add_fusion.17 = f32[4352,1088]{0,1:T(8,128)} fusion(f32[4352,1088]{0,1:T(8,128)} %get-tuple-element.2259, pred[]{:T(512)S(6)} %compare.14, bf16[2,128,1,1088]{1,3,2,0:T(8,128)(2,1)} %get-tuple-element.2320, s32[]{:T(128)S(6)} %copy.140, f32[128,4352]{1,0:T(8,128)} %copy-done.11), kind=kOutput, calls=%fused_computation.62.clone.1 | convolution fusion | flops 1226637312 | bytes 40386564 | tf_op jit(solution)/shard_map/while/body/eval_jaxpr/rsd,rsn->dn/dot_general | solution.py:49
  1329.7 8.2 fusion.194
  1343.1 8.8 convert_element_type.367
  1357.9 189.7 %all-reduce.15.cloned.1.call-done = (bf16[1088,3264]{1,0:T(8,128)(2,1)}, bf16[1088,1088]{1,0:T(8,128)(2,1)}) async-done(((bf16[1088,3264]{1,0:T(8,128)(2,1)}, bf16[1088,1088]{1,0:T(8,128)(2,1)}), (bf16[1088,3264]{1,0:T(8,128)(2,1)}, bf16[1088,1088]{1,0:T(8,128)(2,1)})) %all-reduce.15.cloned.1.call-update) | async-done | bytes 9469968
  1554.8 21.4 %copy.60 = f32[1088,4352]{0,1:T(8,128)} copy(f32[1088,4352]{1,0:T(8,128)} %get-tuple-element.947) | data formatting | bytes 37879808 | tf_op jit(solution)/shard_map/while | solution.py:352
  1576.3 21.5 %copy.61 = f32[4352,1088]{1,0:T(8,128)} copy(f32[4352,1088]{0,1:T(8,128)} %get-tuple-element.949) | data formatting | bytes 37879808 | tf_op jit(solution)/shard_map/while | solution.py:352
  1598.6 43.3 %all-reduce.9 = (f32[1088]{0:T(1024)}, f32[1088]{0:T(1024)}, f32[1088]{0:T(1024)}, f32[1088]{0:T(1024)}, f32[1088]{0:T(1024)}, /*index=5*/f32[1088]{0:T(1024)}, ...) all-reduce(f32[1088]{0:T(1024)S(1)} %copy-done.55, ...), channel_id=1, replica_groups=mesh['dp'=4,'ctx'=8] {'dp','ctx'}, use_global_device_ids=true, to_apply=%region_28.29 | all-reduce | flops 13056 | bytes 104448 | tf_op jit(solution)/shard_map/psum | solution.py:370
  1646.0 195.7 %reduce-scatter.19.cloned.1.call-done = f32[1088,136]{0,1:T(8,128)} async-done(((f32[1088,4352]{0,1:T(8,128)}), f32[1088,136]{0,1:T(8,128)}) %reduce-scatter.19.cloned.1.call-update) | async-done | bytes 591888
  1841.7 219.3 %reduce-scatter.21.cloned.1.call-done = f32[136,1088]{1,0:T(8,128)} async-done(((f32[4352,1088]{1,0:T(8,128)}), f32[136,1088]{1,0:T(8,128)}) %reduce-scatter.21.cloned.1.call-update) | async-done | bytes 591888
  (968 shorter events, 445.0 us)
Async XLA Ops:
  8.4 33.2 %all-gather.12.cloned.1.call-start = ((), (), s32[]{:S(2)}) async-start(), calls=%async_computation.9 | async-start | bytes 2193408 | tf_op jit(solution)/shard_map/while/body/eval_jaxpr/all_gather | solution.py:58
  9.2 116.5 %all-gather.14.cloned.1.call-start = ((), (), s32[]{:S(2)}) async-start(), calls=%async_computation.10 | async-start | bytes 9400320 | tf_op jit(solution)/shard_map/while/body/eval_jaxpr/all_gather | solution.py:65
  45.6 162.8 %all-gather.16.cloned.1.call-start = ((), (), s32[]{:S(2)}) async-start(), calls=%async_computation.11 | async-start | bytes 2506752 | tf_op jit(solution)/shard_map/while/body/eval_jaxpr/all_gather | solution.py:169
  132.0 78.3 %all-gather.20.cloned.1.call-start = ((), (), s32[]{:S(2)}) async-start(), calls=%async_computation.13 | async-start | bytes 2506752 | tf_op jit(solution)/shard_map/while/body/eval_jaxpr/all_gather | solution.py:204
  132.6 130.4 %all-gather.18.cloned.1.call-start = ((), (), s32[]{:S(2)}) async-start(), calls=%async_computation.12 | async-start | bytes 3133440 | tf_op jit(solution)/shard_map/while/body/eval_jaxpr/all_gather | solution.py:66
  152.5 175.9 %all-gather.22.cloned.1.call-start = ((), (), s32[]{:S(2)}) async-start(), calls=%async_computation.14 | async-start | bytes 10340352 | tf_op jit(solution)/shard_map/while/body/eval_jaxpr/all_gather | solution.py:95
  153.0 261.6 %all-gather.24.cloned.1.call-start = ((), (), s32[]{:S(2)}) async-start(), calls=%async_computation.15 | async-start | bytes 10340352 | tf_op jit(solution)/shard_map/while/body/eval_jaxpr/all_gather | solution.py:97
  431.5 24.2 %collective-permute-start = (bf16[128,1,1088]{0,2,1:T(8,128)(2,1)S(1)}, bf16[128,1,1088]{0,2,1:T(8,128)(2,1)}, u32[]{:S(2)}, u32[]{:S(2)}) collective-permute-start(bf16[128,1,1088]{0,2,1:T(8,128)(2,1)S(1)} %copy.109), channel_id=1, source_target_pairs={{0,1},{1,2},{2,3},{3,4},{4,5},{5,6},{6,7},{8,9},{9,10},{10,11},{11... | collective-permute-start | bytes 835592 | tf_op jit(solution)/shard_map/while/body/eval_jaxpr/while/body/eval_jaxpr/ppermute | solution.py:21
  434.4 21.3 %collective-permute-start.1 = (bf16[128,1,1088]{0,2,1:T(8,128)(2,1)S(1)}, bf16[128,1,1088]{0,2,1:T(8,128)(2,1)S(1)}, u32[]{:S(2)}, u32[]{:S(2)}) collective-permute-start(bf16[128,1,1088]{0,2,1:T(8,128)(2,1)S(1)} %copy.110), channel_id=1, source_target_pairs={{0,1},{1,2},{2,3},{3,4},{4,5},{5,6},{6,7},{8,9},{9,10},{10,11},{11... | collective-permute-start | bytes 835592 | tf_op jit(solution)/shard_map/while/body/eval_jaxpr/while/body/eval_jaxpr/ppermute | solution.py:21
  436.9 18.8 collective-permute-start.2
  456.6 21.8 %collective-permute-start = (bf16[128,1,1088]{0,2,1:T(8,128)(2,1)S(1)}, bf16[128,1,1088]{0,2,1:T(8,128)(2,1)}, u32[]{:S(2)}, u32[]{:S(2)}) collective-permute-start(bf16[128,1,1088]{0,2,1:T(8,128)(2,1)S(1)} %copy.109), channel_id=1, source_target_pairs={{0,1},{1,2},{2,3},{3,4},{4,5},{5,6},{6,7},{8,9},{9,10},{10,11},{11... | collective-permute-start | bytes 835592 | tf_op jit(solution)/shard_map/while/body/eval_jaxpr/while/body/eval_jaxpr/ppermute | solution.py:21
  458.7 19.8 collective-permute-start.1
  460.0 18.4 collective-permute-start.2
  479.4 21.3 %collective-permute-start = (bf16[128,1,1088]{0,2,1:T(8,128)(2,1)S(1)}, bf16[128,1,1088]{0,2,1:T(8,128)(2,1)}, u32[]{:S(2)}, u32[]{:S(2)}) collective-permute-start(bf16[128,1,1088]{0,2,1:T(8,128)(2,1)S(1)} %copy.109), channel_id=1, source_target_pairs={{0,1},{1,2},{2,3},{3,4},{4,5},{5,6},{6,7},{8,9},{9,10},{10,11},{11... | collective-permute-start | bytes 835592 | tf_op jit(solution)/shard_map/while/body/eval_jaxpr/while/body/eval_jaxpr/ppermute | solution.py:21
  481.4 19.3 collective-permute-start.1
  501.7 21.7 %collective-permute-start = (bf16[128,1,1088]{0,2,1:T(8,128)(2,1)S(1)}, bf16[128,1,1088]{0,2,1:T(8,128)(2,1)}, u32[]{:S(2)}, u32[]{:S(2)}) collective-permute-start(bf16[128,1,1088]{0,2,1:T(8,128)(2,1)S(1)} %copy.109), channel_id=1, source_target_pairs={{0,1},{1,2},{2,3},{3,4},{4,5},{5,6},{6,7},{8,9},{9,10},{10,11},{11... | collective-permute-start | bytes 835592 | tf_op jit(solution)/shard_map/while/body/eval_jaxpr/while/body/eval_jaxpr/ppermute | solution.py:21
  503.7 19.7 collective-permute-start.1
  505.0 18.4 collective-permute-start.2
  524.4 21.8 %collective-permute-start = (bf16[128,1,1088]{0,2,1:T(8,128)(2,1)S(1)}, bf16[128,1,1088]{0,2,1:T(8,128)(2,1)}, u32[]{:S(2)}, u32[]{:S(2)}) collective-permute-start(bf16[128,1,1088]{0,2,1:T(8,128)(2,1)S(1)} %copy.109), channel_id=1, source_target_pairs={{0,1},{1,2},{2,3},{3,4},{4,5},{5,6},{6,7},{8,9},{9,10},{10,11},{11... | collective-permute-start | bytes 835592 | tf_op jit(solution)/shard_map/while/body/eval_jaxpr/while/body/eval_jaxpr/ppermute | solution.py:21
  526.4 19.8 collective-permute-start.1
  527.7 18.4 collective-permute-start.2
  547.2 21.3 %collective-permute-start = (bf16[128,1,1088]{0,2,1:T(8,128)(2,1)S(1)}, bf16[128,1,1088]{0,2,1:T(8,128)(2,1)}, u32[]{:S(2)}, u32[]{:S(2)}) collective-permute-start(bf16[128,1,1088]{0,2,1:T(8,128)(2,1)S(1)} %copy.109), channel_id=1, source_target_pairs={{0,1},{1,2},{2,3},{3,4},{4,5},{5,6},{6,7},{8,9},{9,10},{10,11},{11... | collective-permute-start | bytes 835592 | tf_op jit(solution)/shard_map/while/body/eval_jaxpr/while/body/eval_jaxpr/ppermute | solution.py:21
  549.2 19.3 collective-permute-start.1
  550.5 17.9 collective-permute-start.2
  569.4 21.7 %collective-permute-start = (bf16[128,1,1088]{0,2,1:T(8,128)(2,1)S(1)}, bf16[128,1,1088]{0,2,1:T(8,128)(2,1)}, u32[]{:S(2)}, u32[]{:S(2)}) collective-permute-start(bf16[128,1,1088]{0,2,1:T(8,128)(2,1)S(1)} %copy.109), channel_id=1, source_target_pairs={{0,1},{1,2},{2,3},{3,4},{4,5},{5,6},{6,7},{8,9},{9,10},{10,11},{11... | collective-permute-start | bytes 835592 | tf_op jit(solution)/shard_map/while/body/eval_jaxpr/while/body/eval_jaxpr/ppermute | solution.py:21
  571.5 19.7 collective-permute-start.1
  572.8 18.4 collective-permute-start.2
  592.1 21.8 %collective-permute-start = (bf16[128,1,1088]{0,2,1:T(8,128)(2,1)S(1)}, bf16[128,1,1088]{0,2,1:T(8,128)(2,1)}, u32[]{:S(2)}, u32[]{:S(2)}) collective-permute-start(bf16[128,1,1088]{0,2,1:T(8,128)(2,1)S(1)} %copy.109), channel_id=1, source_target_pairs={{0,1},{1,2},{2,3},{3,4},{4,5},{5,6},{6,7},{8,9},{9,10},{10,11},{11... | collective-permute-start | bytes 835592 | tf_op jit(solution)/shard_map/while/body/eval_jaxpr/while/body/eval_jaxpr/ppermute | solution.py:21
  594.2 19.8 collective-permute-start.1
  595.5 18.4 collective-permute-start.2
  668.7 27.7 %all-gather.12.cloned.1.call-start = ((), (), s32[]{:S(2)}) async-start(), calls=%async_computation.9 | async-start | bytes 2193408 | tf_op jit(solution)/shard_map/while/body/eval_jaxpr/all_gather | solution.py:58
  669.5 111.0 %all-gather.14.cloned.1.call-start = ((), (), s32[]{:S(2)}) async-start(), calls=%async_computation.10 | async-start | bytes 9400320 | tf_op jit(solution)/shard_map/while/body/eval_jaxpr/all_gather | solution.py:65
  700.4 163.9 %all-gather.16.cloned.1.call-start = ((), (), s32[]{:S(2)}) async-start(), calls=%async_computation.11 | async-start | bytes 2506752 | tf_op jit(solution)/shard_map/while/body/eval_jaxpr/all_gather | solution.py:169
  786.9 79.4 %all-gather.20.cloned.1.call-start = ((), (), s32[]{:S(2)}) async-start(), calls=%async_computation.13 | async-start | bytes 2506752 | tf_op jit(solution)/shard_map/while/body/eval_jaxpr/all_gather | solution.py:204
  787.6 130.9 %all-gather.18.cloned.1.call-start = ((), (), s32[]{:S(2)}) async-start(), calls=%async_computation.12 | async-start | bytes 3133440 | tf_op jit(solution)/shard_map/while/body/eval_jaxpr/all_gather | solution.py:66
  807.7 175.7 %all-gather.22.cloned.1.call-start = ((), (), s32[]{:S(2)}) async-start(), calls=%async_computation.14 | async-start | bytes 10340352 | tf_op jit(solution)/shard_map/while/body/eval_jaxpr/all_gather | solution.py:95
  808.5 261.1 %all-gather.24.cloned.1.call-start = ((), (), s32[]{:S(2)}) async-start(), calls=%async_computation.15 | async-start | bytes 10340352 | tf_op jit(solution)/shard_map/while/body/eval_jaxpr/all_gather | solution.py:97
  1086.4 24.2 %collective-permute-start = (bf16[128,1,1088]{0,2,1:T(8,128)(2,1)S(1)}, bf16[128,1,1088]{0,2,1:T(8,128)(2,1)}, u32[]{:S(2)}, u32[]{:S(2)}) collective-permute-start(bf16[128,1,1088]{0,2,1:T(8,128)(2,1)S(1)} %copy.109), channel_id=1, source_target_pairs={{0,1},{1,2},{2,3},{3,4},{4,5},{5,6},{6,7},{8,9},{9,10},{10,11},{11... | collective-permute-start | bytes 835592 | tf_op jit(solution)/shard_map/while/body/eval_jaxpr/while/body/eval_jaxpr/ppermute | solution.py:21
  1089.3 21.3 %collective-permute-start.1 = (bf16[128,1,1088]{0,2,1:T(8,128)(2,1)S(1)}, bf16[128,1,1088]{0,2,1:T(8,128)(2,1)S(1)}, u32[]{:S(2)}, u32[]{:S(2)}) collective-permute-start(bf16[128,1,1088]{0,2,1:T(8,128)(2,1)S(1)} %copy.110), channel_id=1, source_target_pairs={{0,1},{1,2},{2,3},{3,4},{4,5},{5,6},{6,7},{8,9},{9,10},{10,11},{11... | collective-permute-start | bytes 835592 | tf_op jit(solution)/shard_map/while/body/eval_jaxpr/while/body/eval_jaxpr/ppermute | solution.py:21
  1091.8 18.8 collective-permute-start.2
  1111.6 21.8 %collective-permute-start = (bf16[128,1,1088]{0,2,1:T(8,128)(2,1)S(1)}, bf16[128,1,1088]{0,2,1:T(8,128)(2,1)}, u32[]{:S(2)}, u32[]{:S(2)}) collective-permute-start(bf16[128,1,1088]{0,2,1:T(8,128)(2,1)S(1)} %copy.109), channel_id=1, source_target_pairs={{0,1},{1,2},{2,3},{3,4},{4,5},{5,6},{6,7},{8,9},{9,10},{10,11},{11... | collective-permute-start | bytes 835592 | tf_op jit(solution)/shard_map/while/body/eval_jaxpr/while/body/eval_jaxpr/ppermute | solution.py:21
  1113.6 19.8 collective-permute-start.1
  1114.9 18.4 collective-permute-start.2
  1134.3 21.3 %collective-permute-start = (bf16[128,1,1088]{0,2,1:T(8,128)(2,1)S(1)}, bf16[128,1,1088]{0,2,1:T(8,128)(2,1)}, u32[]{:S(2)}, u32[]{:S(2)}) collective-permute-start(bf16[128,1,1088]{0,2,1:T(8,128)(2,1)S(1)} %copy.109), channel_id=1, source_target_pairs={{0,1},{1,2},{2,3},{3,4},{4,5},{5,6},{6,7},{8,9},{9,10},{10,11},{11... | collective-permute-start | bytes 835592 | tf_op jit(solution)/shard_map/while/body/eval_jaxpr/while/body/eval_jaxpr/ppermute | solution.py:21
  1136.4 19.3 collective-permute-start.1
  1156.6 21.7 %collective-permute-start = (bf16[128,1,1088]{0,2,1:T(8,128)(2,1)S(1)}, bf16[128,1,1088]{0,2,1:T(8,128)(2,1)}, u32[]{:S(2)}, u32[]{:S(2)}) collective-permute-start(bf16[128,1,1088]{0,2,1:T(8,128)(2,1)S(1)} %copy.109), channel_id=1, source_target_pairs={{0,1},{1,2},{2,3},{3,4},{4,5},{5,6},{6,7},{8,9},{9,10},{10,11},{11... | collective-permute-start | bytes 835592 | tf_op jit(solution)/shard_map/while/body/eval_jaxpr/while/body/eval_jaxpr/ppermute | solution.py:21
  1158.6 19.7 collective-permute-start.1
  1160.0 18.4 collective-permute-start.2
  1179.3 21.8 %collective-permute-start = (bf16[128,1,1088]{0,2,1:T(8,128)(2,1)S(1)}, bf16[128,1,1088]{0,2,1:T(8,128)(2,1)}, u32[]{:S(2)}, u32[]{:S(2)}) collective-permute-start(bf16[128,1,1088]{0,2,1:T(8,128)(2,1)S(1)} %copy.109), channel_id=1, source_target_pairs={{0,1},{1,2},{2,3},{3,4},{4,5},{5,6},{6,7},{8,9},{9,10},{10,11},{11... | collective-permute-start | bytes 835592 | tf_op jit(solution)/shard_map/while/body/eval_jaxpr/while/body/eval_jaxpr/ppermute | solution.py:21
  1181.4 19.8 collective-permute-start.1
  1182.7 18.4 collective-permute-start.2
  1202.1 21.3 %collective-permute-start = (bf16[128,1,1088]{0,2,1:T(8,128)(2,1)S(1)}, bf16[128,1,1088]{0,2,1:T(8,128)(2,1)}, u32[]{:S(2)}, u32[]{:S(2)}) collective-permute-start(bf16[128,1,1088]{0,2,1:T(8,128)(2,1)S(1)} %copy.109), channel_id=1, source_target_pairs={{0,1},{1,2},{2,3},{3,4},{4,5},{5,6},{6,7},{8,9},{9,10},{10,11},{11... | collective-permute-start | bytes 835592 | tf_op jit(solution)/shard_map/while/body/eval_jaxpr/while/body/eval_jaxpr/ppermute | solution.py:21
  1204.1 19.3 collective-permute-start.1
  1224.4 21.7 %collective-permute-start = (bf16[128,1,1088]{0,2,1:T(8,128)(2,1)S(1)}, bf16[128,1,1088]{0,2,1:T(8,128)(2,1)}, u32[]{:S(2)}, u32[]{:S(2)}) collective-permute-start(bf16[128,1,1088]{0,2,1:T(8,128)(2,1)S(1)} %copy.109), channel_id=1, source_target_pairs={{0,1},{1,2},{2,3},{3,4},{4,5},{5,6},{6,7},{8,9},{9,10},{10,11},{11... | collective-permute-start | bytes 835592 | tf_op jit(solution)/shard_map/while/body/eval_jaxpr/while/body/eval_jaxpr/ppermute | solution.py:21
  1226.4 19.7 collective-permute-start.1
  1227.7 18.4 collective-permute-start.2
  1247.1 21.8 %collective-permute-start = (bf16[128,1,1088]{0,2,1:T(8,128)(2,1)S(1)}, bf16[128,1,1088]{0,2,1:T(8,128)(2,1)}, u32[]{:S(2)}, u32[]{:S(2)}) collective-permute-start(bf16[128,1,1088]{0,2,1:T(8,128)(2,1)S(1)} %copy.109), channel_id=1, source_target_pairs={{0,1},{1,2},{2,3},{3,4},{4,5},{5,6},{6,7},{8,9},{9,10},{10,11},{11... | collective-permute-start | bytes 835592 | tf_op jit(solution)/shard_map/while/body/eval_jaxpr/while/body/eval_jaxpr/ppermute | solution.py:21
  1249.1 19.8 collective-permute-start.1
  1250.4 18.4 collective-permute-start.2
  1343.1 204.6 %all-reduce.15.cloned.1.call-start = ((), (), s32[]{:S(2)}) async-start(), calls=%async_computation.8 | async-start | bytes 19496960
  1356.1 286.5 %reduce-scatter.17.cloned.1.call-start = ((), (), s32[]{:S(2)}) async-start(), calls=%async_computation.5 | async-start | bytes 940032
  1550.2 94.0 %reduce-scatter.15.cloned.1.call-start = ((), (), s32[]{:S(2)}) async-start(), calls=%async_computation.4 | async-start | bytes 2193408
  1554.7 287.0 %reduce-scatter.19.cloned.1.call-start = ((), (), s32[]{:S(2)}) async-start(), calls=%async_computation.6 | async-start | bytes 20680704
  1576.3 484.8 %reduce-scatter.21.cloned.1.call-start = ((), (), s32[]{:S(2)}) async-start(), calls=%async_computation.7 | async-start | bytes 20680704
  (184 other events, 4233.4 us)
Sparse Core Ops, SparseCore 0:
  11.0 30.5 all-gather.11
  45.7 79.8 all-gather.13
  132.2 34.6 all-gather.15
  168.4 31.0 all-gather.19
  201.8 38.6 all-gather.17
  243.6 84.6 all-gather.21
  331.6 83.0 all-gather.23
  671.3 25.1 all-gather.11
  700.5 79.8 all-gather.13
  787.0 34.7 all-gather.15
  823.5 31.0 all-gather.19
  857.0 38.5 all-gather.17
  898.9 84.4 all-gather.21
  986.5 83.0 all-gather.23
Sparse Core Ops, SparseCore 1:
  1356.2 191.4 all-reduce.14
  1550.3 32.7 reduce-scatter.16
  1585.4 36.1 reduce-scatter.14
  1629.6 212.0 reduce-scatter.18
  1848.7 212.3 reduce-scatter.20
where the time goes:
time: 2080 us; the launch traced here: 2070 us
  waiting for transfers between devices  1230 us (59%)
  matrix products  301 us (14%)
  blocking collectives  188 us (9%)
  other arithmetic  114 us (5%)
  local copies, waits for them, and re-layouts  107 us (5%)
  starting transfers between devices  100 us (5%)
    unnamed x10, waiting for transfers between devices  605 us
    all_gather x2, waiting for transfers between devices, gather_columns(): lax.all_gather(attn_pair[0], 'dp', axis=1, tiled=True)  159 us
    all_gather x2, waiting for transfers between devices, fetch_weights(): lax.all_gather(out_weight, ('dp', 'ctx'), axis=0, tiled=True)  158 us
    all_gather x2, waiting for transfers between devices, fetch_weights(): lax.all_gather(fc_weight, ('dp', 'ctx'), axis=1, tiled=True)  125 us
    ppermute x32, waiting for transfers between devices, from_behind(): return lax.ppermute(block, axis, route)  119 us
    ppermute x48, starting transfers between devices, passed_along(): lax.ppermute(value, axis, [(source, source + steps) for source in range(l...  84.2 us
    while x2, blocking collectives  83.1 us
    dot_general x8, matrix products, outer_sum(): jnp.einsum('rsd,rsn->dn', operand, gradient, preferred_element_type=jnp.f...  82.6 us
  transfers between devices with their start and end apart: 99, of which 43 were waited for; matrix products, arithmetic and copies ran while one was open for 15% of the time, Pallas kernels for 0%

commit v1 on v0

v1 whole, which is shorter than its diff:
```python
import functools

import jax
import jax.numpy as jnp
from jax import lax
from jax.experimental import pallas as pl
from jax.experimental.pallas import tpu as pltpu
from jax.sharding import Mesh
from jax.sharding import PartitionSpec as P

HEADS = 17
HEAD_DIM = 64
EPSILON = 1e-05
MASKED = -1e30
SCALE = HEAD_DIM ** (-0.5)
GROUP = ("dp", "z")
EVERY = ("dp", "z", "core")
BF16 = jnp.bfloat16
F32 = jnp.float32
VMEM_BYTES = 48 * 1024 * 1024


def swapped(value):
    return lax.ppermute(value, "core", [(0, 1), (1, 0)])


def normalize(values, gain_row, shift_row):
    center = values - jnp.mean(values, -1, keepdims=True)
    spread = jnp.mean(center * center, -1, keepdims=True)
    return center * lax.rsqrt(spread + EPSILON) * gain_row + shift_row


def gelu_tanh(values):
    return jax.nn.gelu(values, approximate=True)


def contract(spec, left, right):
    return jnp.einsum(spec, left, right, preferred_element_type=F32)


def dot_over(left, right, left_dim, right_dim):
    return lax.dot_general(
        left, right, (((left_dim,), (right_dim,)), ((), ())), preferred_element_type=F32
    )


def scaled(block):
    return (block.astype(F32) * SCALE).astype(BF16)


def forward_kernel(z_ref, q_ref, k_ref, v_ref, row_ref, col_ref, out_ref, lse_ref, bias):
    keys, queries = bias.shape

    @pl.when(pl.program_id(0) == 0)
    def _():
        key_pos = lax.broadcasted_iota(jnp.int32, (keys, queries), 0)
        query_pos = z_ref[0] * queries + lax.broadcasted_iota(jnp.int32, (keys, queries), 1)
        docs = row_ref[z_ref[0]]
        same = col_ref[...].reshape(keys, 1) == docs
        bias[...] = jnp.where((key_pos <= query_pos) & same, 0.0, MASKED)

    scores = dot_over(k_ref[...], scaled(q_ref[...]), 0, 0) + bias[...]
    row_max = jnp.max(scores, 0, keepdims=True)
    powers = jnp.exp(scores - row_max)
    total = jnp.sum(powers, 0, keepdims=True)
    out = dot_over(v_ref[...], powers.astype(BF16), 1, 0) / total
    out_ref[...] = out.astype(BF16)
    lse_ref[0] = row_max + jnp.log(total)


def backward_kernel(
    z_ref, q_own, k_own, v_own, q_ref, k_ref, v_ref, do_ref, lse_ref, delta_ref,
    row_ref, col_ref, grad_ref, bias, dq, dk, dv,
):
    blocks, rows, _ = bias.shape
    z = z_ref[0]

    @pl.when(pl.program_id(0) == 0)
    def _():
        for j in range(blocks):

            @pl.when(j < z)
            def _():
                bias[j] = jnp.where(col_ref[j] == row_ref[z], 0.0, MASKED)

            @pl.when(j > z)
            def _():
                bias[j] = jnp.where(col_ref[z] == row_ref[j], 0.0, MASKED)

            @pl.when(j == z)
            def _():
                key_pos = lax.broadcasted_iota(jnp.int32, (rows, rows), 0)
                query_pos = lax.broadcasted_iota(jnp.int32, (rows, rows), 1)
                same = col_ref[z] == row_ref[z]
                bias[j] = jnp.where((key_pos <= query_pos) & same, 0.0, MASKED)

    query = scaled(q_own[...])
    key = k_own[...]
    value = v_own[...]
    d_out = do_ref[z]
    lse = lse_ref[z, 0]
    delta = delta_ref[z, 0]

    def pair(key_t, value_t, query_t, d_out_t, lse_row, delta_row, bias_block):
        scores = dot_over(key_t, query_t, 0, 0) + bias_block
        prob = jnp.exp(scores - lse_row)
        d_prob = dot_over(value_t, d_out_t, 0, 0)
        d_raw = (prob * (d_prob - delta_row)).astype(BF16)
        return prob.astype(BF16), d_raw

    prob, d_raw = pair(key, value, query, d_out, lse, delta, bias[z])
    dq[...] = dot_over(key, d_raw, 1, 0)
    dk[...] = dot_over(query, d_raw, 1, 1)
    dv[...] = dot_over(d_out, prob, 1, 1)

    for j in range(blocks):
        here = slice(j * rows, (j + 1) * rows)

        @pl.when(j < z)
        def _():
            key_j = k_ref[:, here]
            _, raw_j = pair(key_j, v_ref[:, here], query, d_out, lse, delta, bias[j])
            dq[...] += dot_over(key_j, raw_j, 1, 0)

        @pl.when(j > z)
        def _():
            query_j = scaled(q_ref[:, here])
            d_out_j = do_ref[j]
            prob_j, raw_j = pair(key, value, query_j, d_out_j, lse_ref[j, 0], delta_ref[j, 0], bias[j])
            dk[...] += dot_over(query_j, raw_j, 1, 1)
            dv[...] += dot_over(d_out_j, prob_j, 1, 1)

    grad_ref[0] = (dq[...] * SCALE).astype(BF16)
    grad_ref[1] = dk[...].astype(BF16)
    grad_ref[2] = dv[...].astype(BF16)


def whole_block(array):
    return pl.BlockSpec(array.shape, lambda h, z: (0,) * array.ndim)


def head_specs(rows, length):
    own = [
        pl.BlockSpec((HEAD_DIM, rows), functools.partial(lambda p, h, z: (p * HEADS + h, z[0]), p))
        for p in range(3)
    ]
    full = [
        pl.BlockSpec((HEAD_DIM, length), functools.partial(lambda p, h, z: (p * HEADS + h, 0), p))
        for p in range(3)
    ]
    return own, full


def attend(z_index, joined_t, seg_rows, seg_cols, rows):
    length = joined_t.shape[1]
    own, full = head_specs(rows, length)
    return pl.pallas_call(
        forward_kernel,
        grid_spec=pltpu.PrefetchScalarGridSpec(
            num_scalar_prefetch=1,
            grid=(HEADS,),
            in_specs=[own[0], full[1], full[2], whole_block(seg_rows), whole_block(seg_cols)],
            out_specs=[
                pl.BlockSpec((HEAD_DIM, rows), lambda h, z: (h, 0)),
                pl.BlockSpec((1, 1, rows), lambda h, z: (h, 0, 0)),
            ],
            scratch_shapes=[pltpu.VMEM((length, rows), F32)],
        ),
        out_shape=[
            jax.ShapeDtypeStruct((HEADS * HEAD_DIM, rows), BF16),
            jax.ShapeDtypeStruct((HEADS, 1, rows), F32),
        ],
        compiler_params=pltpu.CompilerParams(vmem_limit_bytes=VMEM_BYTES),
        cost_estimate=pl.CostEstimate(
            flops=4 * HEADS * HEAD_DIM * rows * length,
            bytes_accessed=4 * HEADS * HEAD_DIM * length,
            transcendentals=HEADS * rows * length,
        ),
        name="attend",
    )(z_index, joined_t, joined_t, joined_t, seg_rows, seg_cols)


def attend_back(z_index, joined_t, d_att_all, lse_all, delta_all, seg_rows, seg_cols, rows):
    length = joined_t.shape[1]
    blocks = length // rows
    own, full = head_specs(rows, length)
    row_spec = pl.BlockSpec((blocks, 1, 1, rows), lambda h, z: (0, h, 0, 0))
    return pl.pallas_call(
        backward_kernel,
        grid_spec=pltpu.PrefetchScalarGridSpec(
            num_scalar_prefetch=1,
            grid=(HEADS,),
            in_specs=own
            + full
            + [
                pl.BlockSpec((blocks, HEAD_DIM, rows), lambda h, z: (0, h, 0)),
                row_spec,
                row_spec,
                whole_block(seg_rows),
                whole_block(seg_cols),
            ],
            out_specs=pl.BlockSpec((3, HEAD_DIM, rows), lambda h, z: (0, h, 0)),
            scratch_shapes=[pltpu.VMEM((blocks, rows, rows), F32)]
            + [pltpu.VMEM((HEAD_DIM, rows), F32)] * 3,
        ),
        out_shape=jax.ShapeDtypeStruct((3, HEADS * HEAD_DIM, rows), BF16),
        compiler_params=pltpu.CompilerParams(vmem_limit_bytes=VMEM_BYTES),
        cost_estimate=pl.CostEstimate(
            flops=8 * HEADS * HEAD_DIM * rows * length,
            bytes_accessed=8 * HEADS * HEAD_DIM * length,
            transcendentals=HEADS * rows * length,
        ),
        name="attend_back",
    )(z_index, *([joined_t] * 6), d_att_all, lse_all, delta_all, seg_rows, seg_cols)


def local(
    inputs,
    segments,
    ln1_gain,
    ln1_bias,
    qkv_weight,
    query_bias,
    value_bias,
    proj_weight,
    proj_bias,
    ln2_gain,
    ln2_bias,
    fc_weight,
    fc_bias,
    out_weight,
    out_bias,
    cotangent,
):
    part, seqs, width = inputs.shape
    dp, nz = lax.axis_size("dp"), lax.axis_size("z")
    z, core = lax.axis_index("z"), lax.axis_index("core")
    rows = 2 * part
    shard_rows, qkv_cols = qkv_weight.shape
    proj_cols = proj_weight.shape[1]
    units = fc_weight.shape[1]
    first = core == 0

    seg_row = jnp.pad(segments.reshape(1, seqs * part).astype(BF16), ((0, 7), (0, width - seqs * part)))
    packed = jnp.concatenate(
        [inputs[:, 0], inputs[:, 1], cotangent[:, 0], cotangent[:, 1], seg_row], 0
    )
    arrived = swapped(packed)
    low_part = jnp.where(first, packed, arrived)
    high_part = jnp.where(first, arrived, packed)

    def chip_rows(slot):
        here = slice(slot * part, (slot + 1) * part)
        return jnp.concatenate([low_part[here], high_part[here]], 0)

    def own_other(slot):
        zero, one = chip_rows(slot), chip_rows(slot + 1)
        return jnp.where(first, zero, one), jnp.where(first, one, zero)

    x_own, x_other = own_other(0)
    g_own, g_other = own_other(2)
    segs = [
        jnp.concatenate(
            [low_part[4 * part, i * part : (i + 1) * part], high_part[4 * part, i * part : (i + 1) * part]]
        )
        for i in range(2)
    ]
    seg_own = jnp.pad(jnp.where(first, segs[0], segs[1]).reshape(1, rows), ((0, 7), (0, width - rows)))

    bias_row = jnp.pad(fc_bias.reshape(1, units), ((0, 7), (0, qkv_cols + proj_cols - units)))
    pair_block = jnp.concatenate([jnp.concatenate([qkv_weight, proj_weight], 1), bias_row], 0)
    pair_half = lax.all_gather(pair_block, GROUP, axis=0, tiled=False)
    seq_all = lax.all_gather(jnp.concatenate([x_own, seg_own], 0), "z", axis=0, tiled=False)
    w_fc = lax.all_gather(fc_weight.T, GROUP, axis=0, tiled=True)
    w_out = lax.all_gather(out_weight, GROUP, axis=0, tiled=True)
    b_fc = pair_half[:, shard_rows, :units].reshape(-1).astype(F32)
    pair_mine = pair_half[:, :shard_rows]
    pair_other = swapped(pair_mine)
    pair_full = jnp.stack(
        [jnp.where(first, pair_mine, pair_other), jnp.where(first, pair_other, pair_mine)]
    ).reshape(2, dp, nz, shard_rows, qkv_cols + proj_cols)
    pair_full = jnp.transpose(pair_full, (2, 0, 3, 1, 4)).reshape(width, dp, qkv_cols + proj_cols)
    w_qkv = pair_full[..., :qkv_cols].reshape(width, dp * qkv_cols)
    w_proj = pair_full[..., qkv_cols:].reshape(width, dp * proj_cols)

    x_all = seq_all[:, :rows].reshape(nz * rows, width)
    docs = seq_all[:, rows, :rows].astype(F32)
    seg_rows, seg_cols = docs.reshape(nz, 1, rows), docs.reshape(nz, rows, 1)
    z_index = z.astype(jnp.int32).reshape(1)

    h1_all = normalize(x_all.astype(F32), ln1_gain, ln1_bias).astype(BF16)
    qkv_bias = jnp.concatenate([query_bias, jnp.zeros_like(query_bias), value_bias])
    joined_t = (contract("dn,rd->nr", w_qkv, h1_all) + qkv_bias[:, None]).astype(BF16)
    att_t, lse = attend(z_index, joined_t, seg_rows, seg_cols, rows)
    lse_all = lax.all_gather(lse, "z", axis=0, tiled=False)
    att_other_t = swapped(att_t)

    x_f = x_own.astype(F32)
    resid = x_f + contract("dr,dn->rn", att_t, w_proj) + proj_bias
    h2_f, ln2_back = jax.vjp(normalize, resid, ln2_gain, ln2_bias)
    h2 = h2_f.astype(BF16)
    h2_other = swapped(h2)

    def hidden(rows_in, gradient):
        pre = contract("rd,nd->rn", rows_in, w_fc) + b_fc
        act, gelu_back = jax.vjp(gelu_tanh, pre)
        d_pre = gelu_back(contract("rd,nd->rn", gradient, w_out))[0]
        return act.astype(BF16), d_pre.astype(BF16)

    act, d_pre = hidden(h2, g_own)
    act_other, d_pre_other = hidden(h2_other, g_other)
    d_h2_sent = swapped(contract("rn,nd->rd", d_pre_other, w_fc).astype(BF16))
    y_sent = swapped(contract("rn,nd->rd", act_other, w_out).astype(BF16))
    d_h2 = contract("rn,nd->rd", d_pre, w_fc) + d_h2_sent.astype(F32)
    output = (resid + contract("rn,nd->rd", act, w_out) + y_sent.astype(F32) + out_bias).astype(BF16)

    def scattered(blocks):
        return lax.psum_scatter(blocks.astype(BF16), GROUP, scatter_dimension=0, tiled=True)

    out_grad = scattered(
        contract("rn,rd->nd", act, g_own) + contract("rn,rd->nd", act_other, g_other)
    )
    fc_grad = scattered(
        contract("rn,rd->nd", d_pre, h2) + contract("rn,rd->nd", d_pre_other, h2_other)
    )
    d_resid_part, ln2_gain_grad, ln2_bias_grad = ln2_back(d_h2)
    d_resid = g_own.astype(F32) + d_resid_part
    d_branch = d_resid.astype(BF16)
    d_branch_other = swapped(d_branch)
    d_att_t = contract("rn,dn->dr", d_branch, w_proj).astype(BF16)
    products = d_att_t.astype(F32) * att_t.astype(F32)
    delta = jnp.sum(products.reshape(HEADS, HEAD_DIM, rows), 1, keepdims=True)
    d_att_all = lax.all_gather(d_att_t, "z", axis=0, tiled=False)
    delta_all = lax.all_gather(delta, "z", axis=0, tiled=False)

    fc_bias_part = jnp.sum(d_pre.astype(F32), 0) + jnp.sum(d_pre_other.astype(F32), 0)
    early = jnp.concatenate(
        [
            jnp.sum(g_own.astype(F32), 0),
            jnp.sum(d_branch.astype(F32), 0),
            ln2_gain_grad,
            ln2_bias_grad,
            fc_bias_part,
        ]
    ).reshape(1, -1)
    early_all = lax.all_gather(early, EVERY, axis=0, tiled=True)
    early_sum = jnp.sum(early_all[:, : 4 * width], 0).reshape(4, width)
    fc_parts = early_all[:, 4 * width :].reshape(dp * nz, 2, dp * nz, units)
    fc_parts = lax.dynamic_index_in_dim(fc_parts, core, 1, keepdims=False)
    place = lax.axis_index("dp") * nz + z
    fc_bias_grad = jnp.sum(lax.dynamic_index_in_dim(fc_parts, place, 1, keepdims=False), 0)

    grads_t = attend_back(z_index, joined_t, d_att_all, lse_all, delta_all, seg_rows, seg_cols, rows)
    dj_t = grads_t.reshape(3 * width, rows)
    dj_other_t = swapped(dj_t)

    def my_columns(block):
        split = block.reshape(block.shape[0], nz, 2, shard_rows)
        return jnp.where(first, split[:, :, 0], split[:, :, 1]).reshape(block.shape[0], -1)

    def my_rows(block_t):
        split = block_t.reshape(nz, 2, shard_rows, block_t.shape[1])
        return jnp.where(first, split[:, 0], split[:, 1]).reshape(-1, block_t.shape[1])

    h1_own = normalize(x_f, ln1_gain, ln1_bias).astype(BF16)
    h1_other = normalize(x_other.astype(F32), ln1_gain, ln1_bias).astype(BF16)
    h1_mine, h1_mine_other = my_columns(h1_own), my_columns(h1_other)
    att_mine, att_mine_other = my_rows(att_t), my_rows(att_other_t)
    pair_parts = []
    for i in range(dp):
        take = slice(i * qkv_cols, (i + 1) * qkv_cols)
        qkv_part = contract("ra,nr->an", h1_mine, dj_t[take]) + contract(
            "ra,nr->an", h1_mine_other, dj_other_t[take]
        )
        take = slice(i * proj_cols, (i + 1) * proj_cols)
        proj_part = contract("ar,rn->an", att_mine, d_branch[:, take]) + contract(
            "ar,rn->an", att_mine_other, d_branch_other[:, take]
        )
        pair_parts.append(jnp.concatenate([qkv_part.astype(BF16), proj_part.astype(BF16)], 1))
    pair_grad = scattered(jnp.concatenate(pair_parts, 0))

    _, ln1_back = jax.vjp(normalize, x_f, ln1_gain, ln1_bias)
    d_normed = contract("nr,dn->rd", dj_t, w_qkv)
    d_input_part, ln1_gain_grad, ln1_bias_grad = ln1_back(d_normed)
    input_grad = (d_resid + d_input_part).astype(BF16)
    dj_sums = jnp.sum(dj_t.astype(F32), 1)
    late = jnp.concatenate(
        [ln1_gain_grad, ln1_bias_grad, dj_sums[:width], dj_sums[2 * width :]]
    ).reshape(1, -1)
    late_sum = jnp.sum(lax.all_gather(late, EVERY, axis=0, tiled=True), 0).reshape(4, width)

    def placed(block):
        mine = jnp.where(first, block[:part], block[part:])
        sent = swapped(jnp.where(first, block[part:], block[:part]))
        return jnp.stack([jnp.where(first, mine, sent), jnp.where(first, sent, mine)], 1)

    return (
        placed(output),
        placed(input_grad),
        late_sum[0],
        late_sum[1],
        pair_grad[:, :qkv_cols].astype(F32),
        late_sum[2],
        late_sum[3],
        pair_grad[:, qkv_cols:].astype(F32),
        early_sum[1],
        early_sum[2],
        early_sum[3],
        fc_grad.astype(F32).T,
        fc_bias_grad,
        out_grad.astype(F32),
        early_sum[0],
    )


def solution(mesh):
    dp, ctx = mesh.shape["dp"], mesh.shape["ctx"]
    split = Mesh(mesh.devices.reshape(dp, ctx // 2, 2), EVERY)
    ctx_axes = ("z", "core")
    tokens = P(ctx_axes, "dp", None)
    pair = P(ctx_axes, "dp")
    columns, units, unit_rows = P(None, EVERY), P(EVERY), P(EVERY, None)
    return jax.shard_map(
        local,
        mesh=split,
        in_specs=(
            tokens, P("dp", ctx_axes), P(), P(), pair, P(), P(), pair,
            P(), P(), P(), columns, units, unit_rows, P(), tokens,
        ),
        out_specs=(
            tokens, tokens, P(), P(), pair, P(), P(), pair,
            P(), P(), P(), columns, units, unit_rows, P(),
        ),
        check_vma=False,
    )
```

time: 2080 us -> 885 us (0.43)
  waiting for transfers between devices: 1230 us -> 474 us
  matrix products: 301 us -> 93.6 us
  starting transfers between devices: 100 us -> 2.76 us
  blocking collectives: 188 us -> 115 us
  local copies, waits for them, and re-layouts: 107 us -> 55 us
  Pallas kernels: 0 us -> 47.3 us
  other arithmetic: 114 us -> 75.4 us
    unnamed x10 -> x11, waiting for transfers between devices: 605 us -> 273 us
    all_gather x14 -> x5, waiting for transfers between devices: 501 us -> 199 us  [the longest x1 76.4 us: local(): w_fc = lax.all_gather(fc_weight.T, GROUP, axis=0, tiled=True)]
    dot_general x120 -> x32, matrix products: 301 us -> 93.6 us  [contract(): return jnp.einsum(spec, left, right, preferred_element_type=F32)]
    ppermute x80 -> x10, waiting for transfers between devices: 119 us -> 2.66 us  [swapped(): return lax.ppermute(value, 'core', [(0, 1), (1, 0)])]
    ppermute x80 -> x10, starting transfers between devices: 99.5 us -> 2.21 us  [swapped(): return lax.ppermute(value, 'core', [(0, 1), (1, 0)])]
    while x2 -> x0, blocking collectives: 83.1 us -> none
    while x340 -> x0, local copies, waits for them, and re-layouts: 65.1 us -> none  [the longest x2 42.9 us: local(): lax.scan(run_batch, zero_totals, (inputs_split, cotan_split, segments_spl...]
    convert_element_type x82 -> x10, other arithmetic: 75.3 us -> 11.6 us  [the longest x1 2.37 us: local(): h1_all = normalize(x_all.astype(F32), ln1_gain, ln1_bias).astype(BF16)]
  transfers between devices with their start and end apart: 99 -> 18, of which waited for: 43 -> 6; matrix products, arithmetic and copies ran while one was open for 15% -> 22% of each run, Pallas kernels for 0% -> 5%
where the time goes in v1:
time: 885 us; the launch traced here: 879 us
  waiting for transfers between devices  474 us (54%)
  blocking collectives  115 us (13%)
  matrix products  93.6 us (11%)
  other arithmetic  75.4 us (9%)
  local copies, waits for them, and re-layouts  55 us (6%)
  Pallas kernels  47.3 us (5%)
  between operations  16.1 us (2%)
    unnamed x11, waiting for transfers between devices  273 us
    dot_general x32, matrix products, contract(): return jnp.einsum(spec, left, right, preferred_element_type=F32)  93.6 us
    all_gather x1, waiting for transfers between devices, local(): w_fc = lax.all_gather(fc_weight.T, GROUP, axis=0, tiled=True)  76.4 us
    all_gather x1, waiting for transfers between devices, local(): pair_half = lax.all_gather(pair_block, GROUP, axis=0, tiled=False)  75.4 us
    all_gather x1, waiting for transfers between devices, local(): lax.all_gather(jnp.concatenate([x_own, seg_own], 0), 'z', axis=0, tiled=F...  46.8 us
    all_gather x1, blocking collectives, local(): early_all = lax.all_gather(early, EVERY, axis=0, tiled=True)  46.2 us
    all_gather x1, blocking collectives, local(): lax.all_gather(late, EVERY, axis=0, tiled=True)  41 us
    pallas_call x1, Pallas kernels, attend_back(): pl.pallas_call(backward_kernel, grid_spec=pltpu.PrefetchScalarGridSpec(nu...  30.5 us
  transfers between devices with their start and end apart: 18, of which 6 were waited for; matrix products, arithmetic and copies ran while one was open for 22% of the time, Pallas kernels for 5%

profile of v1, /device:TPU:0, one launch (start us, length us, event | category | flops | bytes accessed | tf_op | source)
XLA Modules:
  0.0 879.2 jit_solution(7170231049575834918)
XLA Ops:
  7.9 1.8 fusion.56
  11.7 1.0 bitcast_dynamic-update-slice_fusion.2
  13.0 1.4 copy.101
  14.9 2.6 collective-permute-done
  17.5 2.4 copy.102
  20.8 1.5 convert_reduce_fusion.5
  22.4 1.1 copy.105
  24.3 75.4 %all-gather.20.cloned.1.call-done = bf16[2304,1088]{1,0:T(8,128)(2,1)} async-done(((bf16[144,1088]{1,0:T(8,128)(2,1)}), bf16[2304,1088]{1,0:T(8,128)(2,1)}) %all-gather.20.cloned.1.call-update) | async-done | bytes 5013520 | tf_op jit(solution)/shard_map/all_gather | solution.py:272
  99.7 5.1 slice.280
  105.3 46.8 %all-gather.22.cloned.1.call-done = bf16[1056,1088]{1,0:T(8,128)(2,1)} async-done(((bf16[264,1088]{1,0:T(8,128)(2,1)}), bf16[1056,1088]{1,0:T(8,128)(2,1)}) %all-gather.22.cloned.1.call-update) | async-done | bytes 2297872 | tf_op jit(solution)/shard_map/all_gather | solution.py:273
  153.2 2.1 convert_reduce_fusion
  156.2 2.4 fusion.10
  158.5 8.9 %broadcast_select_fusion.1 = (bf16[16,136,1088]{2,1,0:T(8,128)(2,1)}, bf16[16,136,1088]{2,1,0:T(8,128)(2,1)}) fusion(bf16[16,136,1088]{2,1,0:T(8,128)(2,1)} %collective-permute-done.1, pred[]{:T(512)S(6)} %eq.3, bf16[16,144,1088]{2,1,0:T(8,128)(2,1)} %bitcast.119), kind=kLoop, calls=%fused_computation.18 | loop fusion | flops 4734976 | bytes 18939904 | tf_op jit(solution)/shard_map/jit(_where)/select_n | solution.py:280
  167.4 8.9 %pad_maximum_fusion = bf16[2,4,4,136,1088]{4,3,0,2,1:T(8,128)(2,1)} fusion(bf16[1,4,4,136,1088]{4,3,0,2,1:T(8,128)(2,1)} %bitcast.117, bf16[1,4,4,136,1088]{4,3,0,2,1:T(8,128)(2,1)} %bitcast.116), kind=kLoop, calls=%fused_computation.5 | loop fusion | flops 4734976 | bytes 18939904 | tf_op jit(solution)/shard_map/stack | solution.py:279
  176.4 5.4 slice.281
  181.8 7.0 slice.282
  188.7 4.6 copy.107
  193.4 11.1 %copy.104 = bf16[1088,4,816]{0,2,1:T(8,128)(2,1)} copy(bf16[1088,4,816]{2,0,1:T(8,128)(2,1)} %slice.282) | data formatting | bytes 14204928 | tf_op jit(solution)/shard_map/slice | solution.py:283
  204.5 13.9 %add_convert_fusion.q_ref.k_ref.v_ref.q_own.k_own.v_own = bf16[3264,1024]{1,0:T(8,128)(2,1)} fusion(bf16[1088,3264]{0,1:T(8,128)(2,1)} %bitcast.121, bf16[1024,1088]{1,0:T(8,128)(2,1)} %bitcast.147, f32[3264]{0:T(1024)S(1)} %concatenate.93), kind=kOutput, calls=%fused_computation.2 | convolution fusion | flops 7279607808 | bytes 16028416 | tf_op jit(solution)/shard_map/dn,rd->nr/dot_general | solution.py:38
  218.4 16.8 %attend.1 = (bf16[1088,256]{1,0:T(8,128)(2,1)S(1)}, f32[17,1,256]{2,1,0:T(1,128)S(1)}) custom-call(s32[1]{0:T(128)} %bitcast.4.z_ref, bf16[3264,1024]{1,0:T(8,128)(2,1)} %add_convert_fusion.q_ref.k_ref.v_ref.q_own.k_own.v_own, bf16[3264,1024]{1,0:T(8,128)(2,1)} %add_convert_fusion.q_ref.k_ref.v_ref.q_own.k_own.v_own, ...), custom_call_target="tpu_custom_call" | custom-call | flops 1140850688 | bytes 4456448 | tf_op jit(solution)/shard_map/attend/pallas_call | solution.py:157
  236.4 1.2 add_convert_fusion.9
  237.5 5.6 fusion.88
  244.2 76.4 %all-gather.16.cloned.1.call-done = bf16[2176,1088]{1,0:T(8,128)(2,1)} async-done(((bf16[136,1088]{1,0:T(8,128)(2,1)}), bf16[2176,1088]{1,0:T(8,128)(2,1)}) %all-gather.16.cloned.1.call-update) | async-done | bytes 4734992 | tf_op jit(solution)/shard_map/all_gather | solution.py:274
  320.6 4.5 convolution_add_fusion.2
  325.2 3.9 convert_reduce_fusion.2
  329.1 2.1 convolution_convert_fusion.1
  331.4 4.9 convert_reduce_fusion.3
  336.3 2.6 multiply_reduce_fusion
  340.8 2.2 convert_multiply_fusion
  343.4 3.8 fusion.76
  347.3 4.4 fusion.1
  354.4 13.6 %all-gather.3 = f32[68,1,256]{2,1,0:T(1,128)S(1)} all-gather(f32[17,1,256]{2,1,0:T(1,128)S(1)} %get-tuple-element.18), channel_id=5, replica_groups=mesh['dp'=4,'z'=4,'core'=2] {'z'}, dimensions={0}, use_global_device_ids=true | all-gather | bytes 87040 | tf_op jit(solution)/shard_map/all_gather | solution.py:295
  368.8 2.9 fusion.89
  371.6 5.7 convolution_convert_fusion.2
  377.4 4.9 fusion
  382.4 1.2 slice_select_fusion
  384.1 2.2 fusion.59
  386.3 5.6 add_convert_fusion.8
  393.6 2.1 fusion.62
  395.7 1.3 reduce_sum.230
  397.1 14.2 %all-gather.7 = f32[4,17,256]{2,1,0:T(8,128)S(1)} all-gather(f32[1,17,256]{2,1,0:T(8,128)S(1)} %bitcast.151), channel_id=6, replica_groups=mesh['dp'=4,'z'=4,'core'=2] {'z'}, dimensions={0}, use_global_device_ids=true | all-gather | bytes 87040 | tf_op jit(solution)/shard_map/all_gather | solution.py:334
  411.4 2.1 fusion.65
  413.5 2.1 fusion.68
  415.6 1.2 fusion.34
  417.8 1.6 fusion.33
  420.4 1.5 fusion.32
  422.8 1.2 fusion.31
  425.0 1.6 copy-done
  426.6 30.5 %attend_back.1 = bf16[3,1088,256]{2,1,0:T(8,128)(2,1)S(1)} custom-call(s32[1]{0:T(128)} %bitcast.4.z_ref, bf16[3264,1024]{1,0:T(8,128)(2,1)} %add_convert_fusion.q_ref.k_ref.v_ref.q_own.k_own.v_own, bf16[3264,1024]{1,0:T(8,128)(2,1)} %add_convert_fusion.q_ref.k_ref.v_ref.q_own.k_own.v_own, ...), custom_call_target="tpu_custom_call" | custom-call | flops 2281701376 | bytes 8912896 | tf_op jit(solution)/shard_map/attend_back/pallas_call | solution.py:188
  457.3 7.5 fusion.77
  470.3 23.2 %fusion.4 = bf16[2176,1088]{1,0:T(8,128)(2,1)} fusion(bf16[544,272]{1,0:T(8,128)(2,1)S(1)} %copy-done.46, bf16[544,816]{1,0:T(8,128)(2,1)S(1)} %add_convert_fusion.1, bf16[544,272]{1,0:T(8,128)(2,1)S(1)} %copy-done.47, bf16[544,816]{1,0:T(8,128)(2,1)S(1)} %add_convert_fusion.2, bf16[544,272]{1,0:T(8,128)(2,1)S(1)} %copy-done.48, ...), kind=kLoop, calls=%fused_computation.11 | loop fusion | flops 37879808 | bytes 9469952 | tf_op jit(solution)/shard_map/concatenate | solution.py:380
  493.5 46.2 %all-gather.9 = f32[32,1,6528]{2,1,0:T(1,128)S(1)} all-gather(f32[1,1,6528]{2,1,0:T(1,128)S(1)} %reshape.392), channel_id=8, replica_groups=mesh['dp'=4,'z'=4,'core'=2] {'dp','z','core'}, dimensions={0}, use_global_device_ids=true | all-gather | bytes 861696 | tf_op jit(solution)/shard_map/all_gather | solution.py:346
  539.9 1.5 reshape.378
  541.4 1.7 dynamic-slice_reduce_fusion
  543.7 1.2 select_bitcast_fusion.3
  545.8 1.7 fusion.40
  549.2 41.0 %all-gather.8 = f32[32,1,4352]{2,1,0:T(1,128)S(1)} all-gather(f32[1,1,4352]{2,1,0:T(1,128)S(1)} %reshape.390), channel_id=7, replica_groups=mesh['dp'=4,'z'=4,'core'=2] {'dp','z','core'}, dimensions={0}, use_global_device_ids=true | all-gather | bytes 574464 | tf_op jit(solution)/shard_map/all_gather | solution.py:390
  591.2 1.1 select_bitcast_fusion.1
  593.2 1.8 convert_element_type.231
  595.0 82.8 %reduce-scatter.7.cloned.1.call-done = bf16[136,1088]{1,0:T(8,128)(2,1)} async-done(((bf16[2176,1088]{1,0:T(8,128)(2,1)}), bf16[136,1088]{1,0:T(8,128)(2,1)}) %reduce-scatter.7.cloned.1.call-update) | async-done | bytes 295952
  677.8 1.8 convert_bitcast_fusion
  679.6 189.1 %all-reduce.8.cloned.1.call-done = bf16[2176,1088]{1,0:T(8,128)(2,1)} async-done(((bf16[2176,1088]{1,0:T(8,128)(2,1)}), bf16[2176,1088]{1,0:T(8,128)(2,1)}) %all-reduce.8.cloned.1.call-update) | async-done | bytes 4734992
  868.7 1.8 dynamic-slice_convert_fusion
  870.5 1.7 dynamic-slice_convert_fusion.1
  (246 shorter events, 31.3 us)
Async XLA Ops:
  7.2 5.5 copy-start.52
  7.2 92.5 %all-gather.20.cloned.1.call-start = ((), (), s32[]{:S(2)}) async-start(), calls=%async_computation.4 | async-start | bytes 5640192 | tf_op jit(solution)/shard_map/all_gather | solution.py:272
  9.8 142.3 %all-gather.22.cloned.1.call-start = ((), (), s32[]{:S(2)}) async-start(), calls=%async_computation.5 | async-start | bytes 3041280 | tf_op jit(solution)/shard_map/all_gather | solution.py:273
  14.4 3.2 collective-permute-start
  20.8 84.3 %copy-start.26 = (bf16[128,1088]{0,1:T(8,128)(2,1)}, bf16[128,1088]{0,1:T(8,128)(2,1)S(1)}, u32[]{:S(2)}) copy-start(bf16[128,1088]{0,1:T(8,128)(2,1)S(1)} %get-tuple-element.45) | copy-start | bytes 835588
  20.8 84.3 %copy-start.29 = (bf16[128,1088]{0,1:T(8,128)(2,1)}, bf16[128,1088]{0,1:T(8,128)(2,1)S(1)}, u32[]{:S(2)}) copy-start(bf16[128,1088]{0,1:T(8,128)(2,1)S(1)} %get-tuple-element.46) | copy-start | bytes 835588
  20.8 84.3 %copy-start.32 = (bf16[128,1088]{0,1:T(8,128)(2,1)}, bf16[128,1088]{0,1:T(8,128)(2,1)S(1)}, u32[]{:S(2)}) copy-start(bf16[128,1088]{0,1:T(8,128)(2,1)S(1)} %get-tuple-element.86) | copy-start | bytes 835588
  20.8 84.3 %copy-start.35 = (bf16[128,1088]{0,1:T(8,128)(2,1)}, bf16[128,1088]{0,1:T(8,128)(2,1)S(1)}, u32[]{:S(2)}) copy-start(bf16[128,1088]{0,1:T(8,128)(2,1)S(1)} %get-tuple-element.87) | copy-start | bytes 835588
  22.3 212.9 %copy-start.8 = (bf16[256,1088]{0,1:T(8,128)(2,1)}, bf16[256,1088]{0,1:T(8,128)(2,1)S(1)}, u32[]{:S(2)}) copy-start(bf16[256,1088]{0,1:T(8,128)(2,1)S(1)} %get-tuple-element.60) | copy-start | bytes 1671172
  23.5 214.0 %all-gather.18.cloned.1.call-start = ((), (), s32[]{:S(2)}) async-start(), calls=%async_computation.3 | async-start | bytes 5326848 | tf_op jit(solution)/shard_map/all_gather | solution.py:275
  24.2 296.4 %all-gather.16.cloned.1.call-start = ((), (), s32[]{:S(2)}) async-start(), calls=%async_computation.2 | async-start | bytes 5326848 | tf_op jit(solution)/shard_map/all_gather | solution.py:274
  99.7 5.2 copy-start.57
  99.7 5.2 copy-start.58
  104.8 53.7 %collective-permute-start.1 = (bf16[16,136,1088]{2,1,0:T(8,128)(2,1)}, bf16[16,136,1088]{2,1,0:T(8,128)(2,1)}, u32[]{:S(2)}, u32[]{:S(2)}) collective-permute-start(bf16[16,136,1088]{2,1,0:T(8,128)(2,1)} %slice.280), channel_id=1, source_target_pairs={{0,1},{1,0},{2,3},{3,2},{4,5},{5,4},{6,7},{7,6},{8,9},{9,8},{10,11... | collective-permute-start | bytes 14204936 | tf_op jit(solution)/shard_map/ppermute | solution.py:24
  104.9 320.1 %all-gather.24.cloned.1.call-start = ((), (), s32[]{:S(2)}) async-start(), calls=%async_computation.6 | async-start | bytes 2785280 | tf_op jit(solution)/shard_map/all_gather | solution.py:333
  105.3 132.2 %copy-start.4 = (bf16[256,1088]{0,1:T(8,128)(2,1)}, bf16[256,1088]{0,1:T(8,128)(2,1)S(1)}, u32[]{:S(2)}) copy-start(bf16[256,1088]{0,1:T(8,128)(2,1)S(1)} %get-tuple-element.34) | copy-start | bytes 1671172
  152.1 3.2 copy-start.1
  153.2 3.0 copy-start.53
  153.2 3.0 copy-start.55
  218.4 16.8 %copy-start.24 = (bf16[1088,4,272]{0,2,1:T(8,128)(2,1)S(1)}, bf16[1088,4,272]{0,2,1:T(8,128)(2,1)}, u32[]{:S(2)}) copy-start(bf16[1088,4,272]{0,2,1:T(8,128)(2,1)} %copy.107) | copy-start | bytes 7102468
  218.4 16.8 %copy-start.60 = (f32[1088]{0:T(1024)S(1)}, f32[1088]{0:T(1024)}, u32[]{:S(2)}) copy-start(f32[1088]{0:T(1024)} %param.24) | copy-start | bytes 13060
  236.2 102.8 %copy-start.2 = (f32[256,1088]{0,1:T(8,128)}, f32[256,1088]{0,1:T(8,128)S(1)}, u32[]{:S(2)}) copy-start(f32[256,1088]{0,1:T(8,128)S(1)} %get-tuple-element.76) | copy-start | bytes 3342340
  237.5 83.1 %collective-permute-start.2 = (bf16[256,1088]{0,1:T(8,128)(2,1)}, bf16[256,1088]{0,1:T(8,128)(2,1)}, u32[]{:S(2)}, u32[]{:S(2)}) collective-permute-start(bf16[256,1088]{0,1:T(8,128)(2,1)} %add_convert_fusion.9), channel_id=1, source_target_pairs={{0,1},{1,0},{2,3},{3,2},{4,5},{5,4},{6,7},{7,6},{8,9},{9,8},{10,11... | collective-permute-start | bytes 1671176 | tf_op jit(solution)/shard_map/ppermute | solution.py:24
  244.2 81.0 %copy-start.27 = (bf16[128,1088]{0,1:T(8,128)(2,1)S(1)}, bf16[128,1088]{0,1:T(8,128)(2,1)}, u32[]{:S(2)}) copy-start(bf16[128,1088]{0,1:T(8,128)(2,1)} %copy-done.26) | copy-start | bytes 835588
  244.2 81.0 %copy-start.30 = (bf16[128,1088]{0,1:T(8,128)(2,1)S(1)}, bf16[128,1088]{0,1:T(8,128)(2,1)}, u32[]{:S(2)}) copy-start(bf16[128,1088]{0,1:T(8,128)(2,1)} %copy-done.29) | copy-start | bytes 835588
  244.2 81.0 %copy-start.33 = (bf16[128,1088]{0,1:T(8,128)(2,1)S(1)}, bf16[128,1088]{0,1:T(8,128)(2,1)}, u32[]{:S(2)}) copy-start(bf16[128,1088]{0,1:T(8,128)(2,1)} %copy-done.32) | copy-start | bytes 835588
  244.2 81.0 %copy-start.36 = (bf16[128,1088]{0,1:T(8,128)(2,1)S(1)}, bf16[128,1088]{0,1:T(8,128)(2,1)}, u32[]{:S(2)}) copy-start(bf16[128,1088]{0,1:T(8,128)(2,1)} %copy-done.35) | copy-start | bytes 835588
  320.6 4.5 copy-start.59
  320.6 8.5 slice-start
  325.2 3.9 copy-start.41
  325.2 3.9 slice-start.1
  331.3 5.0 collective-permute-start.5
  336.3 2.6 copy-start.44
  340.2 2.8 copy-start.38
  343.1 250.1 %reduce-scatter.9.cloned.1.call-start = ((), (), s32[]{:S(2)}) async-start(), calls=%async_computation.9 | async-start | bytes 5326848
  343.3 3.9 copy-start.28
  343.3 3.9 copy-start.31
  343.4 3.9 copy-start.34
  343.4 3.9 copy-start.37
  343.4 3.9 copy-start.42
  351.7 326.0 %reduce-scatter.7.cloned.1.call-start = ((), (), s32[]{:S(2)}) async-start(), calls=%async_computation.8 | async-start | bytes 5326848
  353.6 15.2 %copy-start.45 = (bf16[256,2176]{1,0:T(8,128)(2,1)S(1)}, bf16[256,2176]{1,0:T(8,128)(2,1)}, u32[]{:S(2)}) copy-start(bf16[256,2176]{1,0:T(8,128)(2,1)} %copy-done.44) | copy-start | bytes 3342340
  353.9 28.5 %collective-permute-start.8 = (bf16[1088,256]{1,0:T(8,128)(2,1)S(1)}, bf16[1088,256]{1,0:T(8,128)(2,1)}, u32[]{:S(2)}, u32[]{:S(2)}) collective-permute-start(bf16[1088,256]{1,0:T(8,128)(2,1)S(1)} %get-tuple-element.17), channel_id=1, source_target_pairs={{0,1},{1,0},{2,3},{3,2},{4,5},{5,4},{6,7},{7,6},{8,9},{9,8},{10,11... | collective-permute-start | bytes 1671176 | tf_op jit(solution)/shard_map/ppermute | solution.py:24
  368.8 2.9 copy-start.43
  371.6 5.7 copy-start.51
  377.4 9.0 %collective-permute-start.3 = (bf16[256,1088]{0,1:T(8,128)(2,1)}, bf16[256,1088]{0,1:T(8,128)(2,1)}, u32[]{:S(2)}, u32[]{:S(2)}) collective-permute-start(bf16[256,1088]{0,1:T(8,128)(2,1)} %convolution_convert_fusion.2), channel_id=1, source_target_pairs={{0,1},{1,0},{2,3},{3,2},{4,5},{5,4},{6,7},{7,6},{8,9},{9,8},{10,11... | collective-permute-start | bytes 1671176 | tf_op jit(solution)/shard_map/ppermute | solution.py:24
  382.3 4.0 copy-start.3
  382.3 4.0 copy-start.61
  382.3 486.4 %all-reduce.8.cloned.1.call-start = ((), (), s32[]{:S(2)}) async-start(), calls=%async_computation.7 | async-start | bytes 10027008
  383.6 32.1 %collective-permute-start.9 = (bf16[256,1088]{0,1:T(8,128)(2,1)}, bf16[256,1088]{0,1:T(8,128)(2,1)}, u32[]{:S(2)}, u32[]{:S(2)}) collective-permute-start(bf16[256,1088]{0,1:T(8,128)(2,1)} %copy-done.38), channel_id=1, source_target_pairs={{0,1},{1,0},{2,3},{3,2},{4,5},{5,4},{6,7},{7,6},{8,9},{9,8},{10,11... | collective-permute-start | bytes 1671176 | tf_op jit(solution)/shard_map/ppermute | solution.py:24
  386.3 7.2 copy-start.11
  393.6 22.1 %copy-start.14 = (f32[544,272]{0,1:T(8,128)S(1)}, f32[544,272]{0,1:T(8,128)}, u32[]{:S(2)}) copy-start(f32[544,272]{0,1:T(8,128)} %fusion.59) | copy-start | bytes 1775620
  395.7 148.0 %collective-permute-start.4 = (bf16[128,1088]{0,1:T(8,128)(2,1)}, bf16[128,1088]{0,1:T(8,128)(2,1)}, u32[]{:S(2)}, u32[]{:S(2)}) collective-permute-start(bf16[128,1088]{0,1:T(8,128)(2,1)} %broadcast_select_fusion.10), channel_id=1, source_target_pairs={{0,1},{1,0},{2,3},{3,2},{4,5},{5,4},{6,7},{7,6},{8,9},{9,8},{10,11... | collective-permute-start | bytes 835592 | tf_op jit(solution)/shard_map/ppermute | solution.py:24
  417.8 5.0 copy-start.15
  426.6 30.7 %copy-start.9 = (bf16[256,1088]{0,1:T(8,128)(2,1)S(1)}, bf16[256,1088]{0,1:T(8,128)(2,1)}, u32[]{:S(2)}) copy-start(bf16[256,1088]{0,1:T(8,128)(2,1)} %copy-done.8) | copy-start | bytes 1671172
  457.2 7.7 copy-start.17
  457.2 7.7 copy-start.19
  457.2 7.7 copy-start.21
  457.2 7.7 copy-start.23
  457.2 10.2 %collective-permute-start.7 = (bf16[3264,256]{1,0:T(8,128)(2,1)S(1)}, bf16[3264,256]{1,0:T(8,128)(2,1)S(1)}, u32[]{:S(2)}, u32[]{:S(2)}) collective-permute-start(bf16[3264,256]{1,0:T(8,128)(2,1)S(1)} %bitcast.100), channel_id=1, source_target_pairs={{0,1},{1,0},{2,3},{3,2},{4,5},{5,4},{6,7},{7,6},{8,9},{9,8},{10,11... | collective-permute-start | bytes 5013512 | tf_op jit(solution)/shard_map/ppermute | solution.py:24
  541.4 4.4 copy-start.13
  541.4 6.1 copy-start.7
  541.4 6.1 copy-start.10
  548.0 43.2 %collective-permute-start.6 = (bf16[128,1088]{0,1:T(8,128)(2,1)S(1)}, bf16[128,1088]{0,1:T(8,128)(2,1)S(1)}, u32[]{:S(2)}, u32[]{:S(2)}) collective-permute-start(bf16[128,1088]{0,1:T(8,128)(2,1)S(1)} %broadcast_select_fusion.8), channel_id=1, source_target_pairs={{0,1},{1,0},{2,3},{3,2},{4,5},{5,4},{6,7},{7,6},{8,9},{9,8},{10,11... | collective-permute-start | bytes 835592 | tf_op jit(solution)/shard_map/ppermute | solution.py:24
  (20 other events, 29.2 us)
Sparse Core Ops, SparseCore 0:
  11.4 88.3 all-gather.19
  101.9 50.1 all-gather.21
  154.8 81.6 all-gather.17
  239.1 81.4 all-gather.15
  343.2 48.0 all-gather.23
  396.5 137.8 reduce-scatter.8
  540.6 137.1 reduce-scatter.6
  683.7 185.0 all-reduce.7

commit v2 on v1

--- a/solution.py
+++ b/solution.py
@@ -24,6 +24,108 @@
     return lax.ppermute(value, "core", [(0, 1), (1, 0)])
 
 
+def exchanged(value, axis, bit):
+    return lax.ppermute(value, axis, [(i, i ^ bit) for i in range(lax.axis_size(axis))])
+
+
+def axis_bits(axis):
+    size = lax.axis_size(axis)
+    return [(axis, 1 << b) for b in reversed(range(size.bit_length() - 1))]
+
+
+def doubled(block, order):
+    bits = axis_bits("dp") + axis_bits("z")
+    held = block.reshape((1,) * len(bits) + block.shape)
+    for place in order:
+        held = jnp.concatenate([held, exchanged(held, *bits[place])], place)
+    return held.reshape((-1,) + block.shape)
+
+
+def halved(blocks, order):
+    bits = axis_bits("dp") + axis_bits("z")
+    block_shape = blocks.shape[1:]
+    held = blocks.astype(BF16).reshape((2,) * len(bits) + block_shape)
+    for place in order:
+        keep = lax.slice_in_dim(held, 0, 1, axis=place)
+        sent = exchanged(lax.slice_in_dim(held, 1, 2, axis=place), *bits[place])
+        held = (keep.astype(F32) + sent.astype(F32)).astype(BF16)
+    return held.reshape(block_shape)
+
+
+def along_z(block):
+    bits = axis_bits("z")
+    held = block.reshape((1,) * len(bits) + block.shape)
+    for place in range(len(bits)):
+        held = jnp.concatenate([held, exchanged(held, *bits[place])], place)
+    return held.reshape((-1,) + block.shape)
+
+
+def summed_everywhere(value):
+    for axis, bit in [("core", 1)] + axis_bits("z") + axis_bits("dp"):
+        value = value + exchanged(value, axis, bit)
+    return value
+
+
+def reorder_kernel(take_ref, low_mine, high_mine, low_other, high_other, out_ref):
+    rows, cut = out_ref.shape[1], low_mine.shape[1]
+    mine = pl.program_id(0) % 2 == take_ref[take_ref.shape[0] - 1]
+
+    def put(low_ref, high_ref):
+        out_ref[0, :cut] = low_ref[0]
+        out_ref[0, cut:] = high_ref[0, : rows - cut]
+
+    @pl.when(mine)
+    def _():
+        put(low_mine, high_mine)
+
+    @pl.when(jnp.logical_not(mine))
+    def _():
+        put(low_other, high_other)
+
+
+def reorder_weights(take, low_mine, high_mine, low_other, high_other, rows):
+    count, _, width = low_mine.shape
+
+    def taken(array):
+        return pl.BlockSpec((1,) + array.shape[1:], lambda i, t: (t[i // 2], 0, 0))
+
+    parts = (low_mine, high_mine, low_other, high_other)
+    return pl.pallas_call(
+        reorder_kernel,
+        grid_spec=pltpu.PrefetchScalarGridSpec(
+            num_scalar_prefetch=1,
+            grid=(2 * count,),
+            in_specs=[taken(array) for array in parts],
+            out_specs=pl.BlockSpec((1, rows, width), lambda i, t: (i, 0, 0)),
+        ),
+        out_shape=jax.ShapeDtypeStruct((2 * count, rows, width), BF16),
+        compiler_params=pltpu.CompilerParams(vmem_limit_bytes=VMEM_BYTES),
+        cost_estimate=pl.CostEstimate(flops=0, bytes_accessed=12 * count * rows * width, transcendentals=0),
+        name="reorder_weights",
+    )(take, *parts)
+
+
+def copy_kernel(take_ref, in_ref, out_ref):
+    out_ref[...] = in_ref[...]
+
+
+def reorder_blocks(take, blocks):
+    count, rows, width = blocks.shape
+    return pl.pallas_call(
+        copy_kernel,
+        grid_spec=pltpu.PrefetchScalarGridSpec(
+            num_scalar_prefetch=1,
+            grid=(count,),
+            in_specs=[pl.BlockSpec((1, rows, width), lambda i, t: (t[i], 0, 0))],
+            out_specs=pl.BlockSpec((1, rows, width), lambda i, t: (i, 0, 0)),
+        ),
+        out_shape=jax.ShapeDtypeStruct(blocks.shape, BF16),
+        compiler_params=pltpu.CompilerParams(vmem_limit_bytes=VMEM_BYTES),
+        cost_estimate=pl.CostEstimate(flops=0, bytes_accessed=4 * count * rows * width, transcendentals=0),
+        name="reorder_blocks",
+    )(take, blocks)
+
+
 def normalize(values, gain_row, shift_row):
     center = values - jnp.mean(values, -1, keepdims=True)
     spread = jnp.mean(center * center, -1, keepdims=True)
@@ -97,9 +199,9 @@
     query = scaled(q_own[...])
     key = k_own[...]
     value = v_own[...]
-    d_out = do_ref[z]
-    lse = lse_ref[z, 0]
-    delta = delta_ref[z, 0]
+    d_out = do_ref[0]
+    lse = lse_ref[0, 0]
+    delta = delta_ref[0, 0]
 
     def pair(key_t, value_t, query_t, d_out_t, lse_row, delta_row, bias_block):
         scores = dot_over(key_t, query_t, 0, 0) + bias_block
@@ -125,8 +227,11 @@
         @pl.when(j > z)
         def _():
             query_j = scaled(q_ref[:, here])
-            d_out_j = do_ref[j]
-            prob_j, raw_j = pair(key, value, query_j, d_out_j, lse_ref[j, 0], delta_ref[j, 0], bias[j])
+            slot = jnp.bitwise_xor(z, j)
+            d_out_j = do_ref[slot]
+            prob_j, raw_j = pair(
+                key, value, query_j, d_out_j, lse_ref[slot, 0], delta_ref[slot, 0], bias[j]
+            )
             dk[...] += dot_over(query_j, raw_j, 1, 1)
             dv[...] += dot_over(d_out_j, prob_j, 1, 1)
 
@@ -269,19 +374,33 @@
 
     bias_row = jnp.pad(fc_bias.reshape(1, units), ((0, 7), (0, qkv_cols + proj_cols - units)))
     pair_block = jnp.concatenate([jnp.concatenate([qkv_weight, proj_weight], 1), bias_row], 0)
-    pair_half = lax.all_gather(pair_block, GROUP, axis=0, tiled=False)
     seq_all = lax.all_gather(jnp.concatenate([x_own, seg_own], 0), "z", axis=0, tiled=False)
-    w_fc = lax.all_gather(fc_weight.T, GROUP, axis=0, tiled=True)
-    w_out = lax.all_gather(out_weight, GROUP, axis=0, tiled=True)
-    b_fc = pair_half[:, shard_rows, :units].reshape(-1).astype(F32)
-    pair_mine = pair_half[:, :shard_rows]
-    pair_other = swapped(pair_mine)
-    pair_full = jnp.stack(
-        [jnp.where(first, pair_mine, pair_other), jnp.where(first, pair_other, pair_mine)]
-    ).reshape(2, dp, nz, shard_rows, qkv_cols + proj_cols)
-    pair_full = jnp.transpose(pair_full, (2, 0, 3, 1, 4)).reshape(width, dp, qkv_cols + proj_cols)
-    w_qkv = pair_full[..., :qkv_cols].reshape(width, dp * qkv_cols)
-    w_proj = pair_full[..., qkv_cols:].reshape(width, dp * proj_cols)
+    dp_places = list(range(dp.bit_length() - 1))
+    z_places = [len(dp_places) + i for i in range(nz.bit_length() - 1)]
+    grow = z_places + dp_places, z_places + dp_places[::-1]
+    shrink = dp_places + z_places[::-1], dp_places[::-1] + z_places[::-1]
+    take = (
+        (jnp.arange(dp)[:, None] ^ lax.axis_index("dp")) * nz + (jnp.arange(nz)[None] ^ z)
+    ).reshape(-1).astype(jnp.int32)
+    cut = pair_block.shape[0] // 32 * 16
+    low_half = doubled(pair_block[:cut], grow[0])
+    high_half = doubled(pair_block[cut:], grow[1])
+    out_block, low_half, high_half = lax.optimization_barrier((out_weight, low_half, high_half))
+    w_out = doubled(out_block, grow[1]).reshape(-1, width)
+    fc_block, seq_all = lax.optimization_barrier((fc_weight.T, seq_all))
+    w_fc = lax.all_gather(fc_block, GROUP, axis=0, tiled=False)
+    w_fc = reorder_blocks(take, w_fc)
+    w_fc = w_fc.reshape(-1, width)
+    b_fc = high_half[:, shard_rows - cut, :units].reshape(-1).astype(F32)
+    w_pair = reorder_weights(
+        jnp.concatenate([take, core.astype(jnp.int32).reshape(1)]),
+        low_half,
+        high_half,
+        swapped(low_half),
+        swapped(high_half),
+        shard_rows,
+    ).reshape(dp, width, qkv_cols + proj_cols)
+    w_qkv, w_proj = w_pair[..., :qkv_cols], w_pair[..., qkv_cols:]
 
     x_all = seq_all[:, :rows].reshape(nz * rows, width)
     docs = seq_all[:, rows, :rows].astype(F32)
@@ -290,13 +409,14 @@
 
     h1_all = normalize(x_all.astype(F32), ln1_gain, ln1_bias).astype(BF16)
     qkv_bias = jnp.concatenate([query_bias, jnp.zeros_like(query_bias), value_bias])
-    joined_t = (contract("dn,rd->nr", w_qkv, h1_all) + qkv_bias[:, None]).astype(BF16)
+    joined_t = (contract("cdn,rd->cnr", w_qkv, h1_all).reshape(3 * width, -1) + qkv_bias[:, None]).astype(BF16)
     att_t, lse = attend(z_index, joined_t, seg_rows, seg_cols, rows)
-    lse_all = lax.all_gather(lse, "z", axis=0, tiled=False)
+    lse_all = along_z(lse)
     att_other_t = swapped(att_t)
 
     x_f = x_own.astype(F32)
-    resid = x_f + contract("dr,dn->rn", att_t, w_proj) + proj_bias
+    branch = [contract("dr,dn->rn", att_t, w_proj[i]) for i in range(dp)]
+    resid = x_f + jnp.concatenate(branch, 1) + proj_bias
     h2_f, ln2_back = jax.vjp(normalize, resid, ln2_gain, ln2_bias)
     h2 = h2_f.astype(BF16)
     h2_other = swapped(h2)
@@ -314,41 +434,33 @@
     d_h2 = contract("rn,nd->rd", d_pre, w_fc) + d_h2_sent.astype(F32)
     output = (resid + contract("rn,nd->rd", act, w_out) + y_sent.astype(F32) + out_bias).astype(BF16)
 
-    def scattered(blocks):
-        return lax.psum_scatter(blocks.astype(BF16), GROUP, scatter_dimension=0, tiled=True)
-
-    out_grad = scattered(
-        contract("rn,rd->nd", act, g_own) + contract("rn,rd->nd", act_other, g_other)
-    )
-    fc_grad = scattered(
-        contract("rn,rd->nd", d_pre, h2) + contract("rn,rd->nd", d_pre_other, h2_other)
-    )
+    out_parts = contract("rn,rd->nd", act, g_own) + contract("rn,rd->nd", act_other, g_other)
+    fc_parts = contract("rn,rd->nd", d_pre, h2) + contract("rn,rd->nd", d_pre_other, h2_other)
+    out_grad = halved(out_parts.reshape(dp * nz, units, width), shrink[0])
+    fc_grad = halved(fc_parts.reshape(dp * nz, units, width), shrink[1])
     d_resid_part, ln2_gain_grad, ln2_bias_grad = ln2_back(d_h2)
     d_resid = g_own.astype(F32) + d_resid_part
     d_branch = d_resid.astype(BF16)
     d_branch_other = swapped(d_branch)
-    d_att_t = contract("rn,dn->dr", d_branch, w_proj).astype(BF16)
+    d_att_t = sum(
+        contract("rn,dn->dr", d_branch[:, i * proj_cols : (i + 1) * proj_cols], w_proj[i])
+        for i in range(dp)
+    ).astype(BF16)
     products = d_att_t.astype(F32) * att_t.astype(F32)
     delta = jnp.sum(products.reshape(HEADS, HEAD_DIM, rows), 1, keepdims=True)
-    d_att_all = lax.all_gather(d_att_t, "z", axis=0, tiled=False)
-    delta_all = lax.all_gather(delta, "z", axis=0, tiled=False)
+    d_att_all, delta_all = along_z(d_att_t), along_z(delta)
 
     fc_bias_part = jnp.sum(d_pre.astype(F32), 0) + jnp.sum(d_pre_other.astype(F32), 0)
-    early = jnp.concatenate(
-        [
-            jnp.sum(g_own.astype(F32), 0),
-            jnp.sum(d_branch.astype(F32), 0),
-            ln2_gain_grad,
-            ln2_bias_grad,
-            fc_bias_part,
-        ]
-    ).reshape(1, -1)
-    early_all = lax.all_gather(early, EVERY, axis=0, tiled=True)
-    early_sum = jnp.sum(early_all[:, : 4 * width], 0).reshape(4, width)
-    fc_parts = early_all[:, 4 * width :].reshape(dp * nz, 2, dp * nz, units)
-    fc_parts = lax.dynamic_index_in_dim(fc_parts, core, 1, keepdims=False)
-    place = lax.axis_index("dp") * nz + z
-    fc_bias_grad = jnp.sum(lax.dynamic_index_in_dim(fc_parts, place, 1, keepdims=False), 0)
+    early_sum = summed_everywhere(
+        jnp.stack([jnp.sum(g_own.astype(F32), 0), jnp.sum(d_branch.astype(F32), 0), ln2_gain_grad, ln2_bias_grad])
+    )
+    fc_bias_grad = fc_bias_part.reshape((dp, nz, units))
+    for axis, dim in (("dp", 0), ("z", 1)):
+        for _, bit in axis_bits(axis):
+            keep = lax.slice_in_dim(fc_bias_grad, 0, bit, axis=dim)
+            sent = lax.slice_in_dim(fc_bias_grad, bit, 2 * bit, axis=dim)
+            fc_bias_grad = keep + exchanged(sent, axis, bit)
+    fc_bias_grad = fc_bias_grad.reshape(units)
 
     grads_t = attend_back(z_index, joined_t, d_att_all, lse_all, delta_all, seg_rows, seg_cols, rows)
     dj_t = grads_t.reshape(3 * width, rows)
@@ -368,26 +480,32 @@
     att_mine, att_mine_other = my_rows(att_t), my_rows(att_other_t)
     pair_parts = []
     for i in range(dp):
-        take = slice(i * qkv_cols, (i + 1) * qkv_cols)
-        qkv_part = contract("ra,nr->an", h1_mine, dj_t[take]) + contract(
-            "ra,nr->an", h1_mine_other, dj_other_t[take]
+        span = slice(i * qkv_cols, (i + 1) * qkv_cols)
+        qkv_part = contract("ra,nr->an", h1_mine, dj_t[span]) + contract(
+            "ra,nr->an", h1_mine_other, dj_other_t[span]
         )
-        take = slice(i * proj_cols, (i + 1) * proj_cols)
-        proj_part = contract("ar,rn->an", att_mine, d_branch[:, take]) + contract(
-            "ar,rn->an", att_mine_other, d_branch_other[:, take]
+        span = slice(i * proj_cols, (i + 1) * proj_cols)
+        proj_part = contract("ar,rn->an", att_mine, d_branch[:, span]) + contract(
+            "ar,rn->an", att_mine_other, d_branch_other[:, span]
         )
         pair_parts.append(jnp.concatenate([qkv_part.astype(BF16), proj_part.astype(BF16)], 1))
-    pair_grad = scattered(jnp.concatenate(pair_parts, 0))
+    pair_sent = reorder_blocks(
+        take, jnp.concatenate(pair_parts, 0).reshape(dp * nz, shard_rows, qkv_cols + proj_cols)
+    )
+    pair_grad = jnp.concatenate(
+        [halved(pair_sent[:, :cut], shrink[0]), halved(pair_sent[:, cut:], shrink[1])], 0
+    )
 
     _, ln1_back = jax.vjp(normalize, x_f, ln1_gain, ln1_bias)
-    d_normed = contract("nr,dn->rd", dj_t, w_qkv)
+    d_normed = sum(
+        contract("nr,dn->rd", dj_t[i * qkv_cols : (i + 1) * qkv_cols], w_qkv[i]) for i in range(dp)
+    )
     d_input_part, ln1_gain_grad, ln1_bias_grad = ln1_back(d_normed)
     input_grad = (d_resid + d_input_part).astype(BF16)
     dj_sums = jnp.sum(dj_t.astype(F32), 1)
-    late = jnp.concatenate(
-        [ln1_gain_grad, ln1_bias_grad, dj_sums[:width], dj_sums[2 * width :]]
-    ).reshape(1, -1)
-    late_sum = jnp.sum(lax.all_gather(late, EVERY, axis=0, tiled=True), 0).reshape(4, width)
+    late_sum = summed_everywhere(
+        jnp.stack([ln1_gain_grad, ln1_bias_grad, dj_sums[:width], dj_sums[2 * width :]])
+    )
 
     def placed(block):
         mine = jnp.where(first, block[:part], block[part:])

time: 885 us -> 696 us (0.79)
  waiting for transfers between devices: 474 us -> 257 us
  blocking collectives: 115 us -> 0 us
  starting transfers between devices: 2.76 us -> 61.3 us
  Pallas kernels: 47.3 us -> 87.9 us
  matrix products: 93.6 us -> 111 us
  other arithmetic: 75.4 us -> 90 us
  local copies, waits for them, and re-layouts: 55 us -> 66 us
    unnamed x11 -> x2, waiting for transfers between devices: 273 us -> 0.03 us
    ppermute x0 -> x48, waiting for transfers between devices: none -> 257 us  [exchanged(): lax.ppermute(value, axis, [(i, i ^ bit) for i in range(lax.axis_size(axis...]
    all_gather x4 -> x1, waiting for transfers between devices: 152 us -> 0.01 us  [local(): w_fc = lax.all_gather(fc_block, GROUP, axis=0, tiled=False)]
    all_gather x4 -> x0, blocking collectives: 115 us -> none  [the longest x1 46.2 us: local(): early_all = lax.all_gather(early, EVERY, axis=0, tiled=True)]
    ppermute x0 -> x48, starting transfers between devices: none -> 59.1 us  [exchanged(): lax.ppermute(value, axis, [(i, i ^ bit) for i in range(lax.axis_size(axis...]
    all_gather x1, waiting for transfers between devices: 46.8 us -> 0.01 us  [local(): lax.all_gather(jnp.concatenate([x_own, seg_own], 0), 'z', axis=0, tiled=F...]
    pallas_call x0 -> x3, Pallas kernels: none -> 40.6 us  [the longest x1 22.9 us: reorder_weights(): pl.pallas_call(reorder_kernel, grid_spec=pltpu.PrefetchScalarGridSpec(num...]
    concatenate x2 -> x20, other arithmetic: 25 us -> 51.4 us  [the longest x12 24.3 us: doubled(): held = jnp.concatenate([held, exchanged(held, *bits[place])], place)]
  transfers between devices with their start and end apart: 18 -> 61, of which waited for: 6 -> 32; matrix products, arithmetic and copies ran while one was open for 22% -> 35% of each run, Pallas kernels for 5% -> 13%
where the time goes in v2:
time: 696 us; the launch traced here: 689 us
  waiting for transfers between devices  257 us (37%)
  matrix products  111 us (16%)
  other arithmetic  90 us (13%)
  Pallas kernels  87.9 us (13%)
  local copies, waits for them, and re-layouts  66 us (9%)
  starting transfers between devices  61.3 us (9%)
  between operations  15.9 us (2%)
    ppermute x48, waiting for transfers between devices, exchanged(): lax.ppermute(value, axis, [(i, i ^ bit) for i in range(lax.axis_size(axis...  257 us
    dot_general x41, matrix products, contract(): return jnp.einsum(spec, left, right, preferred_element_type=F32)  111 us
    ppermute x48, starting transfers between devices, exchanged(): lax.ppermute(value, axis, [(i, i ^ bit) for i in range(lax.axis_size(axis...  59.1 us
    pallas_call x1, Pallas kernels, attend_back(): pl.pallas_call(backward_kernel, grid_spec=pltpu.PrefetchScalarGridSpec(nu...  30.8 us
    concatenate x12, other arithmetic, doubled(): held = jnp.concatenate([held, exchanged(held, *bits[place])], place)  24.3 us
    concatenate x1, other arithmetic, local(): jnp.concatenate(pair_parts, 0)  23.2 us
    pallas_call x1, Pallas kernels, reorder_weights(): pl.pallas_call(reorder_kernel, grid_spec=pltpu.PrefetchScalarGridSpec(num...  22.9 us
    pallas_call x2, Pallas kernels, reorder_blocks(): pl.pallas_call(copy_kernel, grid_spec=pltpu.PrefetchScalarGridSpec(num_sc...  17.7 us
  transfers between devices with their start and end apart: 61, of which 32 were waited for; matrix products, arithmetic and copies ran while one was open for 35% of the time, Pallas kernels for 13%

profile of v2, /device:TPU:0, one launch (start us, length us, event | category | flops | bytes accessed | tf_op | source)
XLA Modules:
  0.0 689.1 jit_solution(1174464373613831448)
XLA Ops:
  8.3 4.1 collective-permute-start.1
  15.7 8.5 %collective-permute-done.1 = bf16[1,1,1,1,64,1088]{5,4,3,2,1,0:T(8,128)(2,1)S(1)} collective-permute-done((bf16[1,1,1,1,64,1088]{5,4,3,2,1,0:T(8,128)(2,1)S(1)}, bf16[1,1,1,1,64,1088]{5,4,3,2,1,0:T(8,128)(2,1)S(1)}, u32[]{:S(2)}, u32[]{:S(2)}) %collective-permute-start.1) | collective-permute-done | bytes 139296 | tf_op jit(solution)/shard_map/ppermute | solution.py:28
  29.3 4.9 collective-permute-done.2
  37.1 4.5 collective-permute-done.6
  44.1 5.4 collective-permute-done.3
  52.1 2.4 copy.107
  57.4 4.9 collective-permute-done.7
  62.3 2.5 pad_maximum_fusion.9
  69.7 16.3 %collective-permute-done.4 = bf16[2,1,2,2,64,1088]{5,4,3,2,1,0:T(8,128)(2,1)} collective-permute-done((bf16[2,1,2,2,64,1088]{5,4,3,2,1,0:T(8,128)(2,1)}, bf16[2,1,2,2,64,1088]{5,4,3,2,1,0:T(8,128)(2,1)}, u32[]{:S(2)}, u32[]{:S(2)}) %collective-permute-start.4) | collective-permute-done | bytes 1114144 | tf_op jit(solution)/shard_map/ppermute | solution.py:28
  87.8 8.7 %collective-permute-done.8 = bf16[1,2,2,2,80,1088]{5,4,3,2,1,0:T(8,128)(2,1)} collective-permute-done((bf16[1,2,2,2,80,1088]{5,4,3,2,1,0:T(8,128)(2,1)}, bf16[1,2,2,2,80,1088]{5,4,3,2,1,0:T(8,128)(2,1)}, u32[]{:S(2)}, u32[]{:S(2)}) %collective-permute-start.8) | collective-permute-done | bytes 1392672 | tf_op jit(solution)/shard_map/ppermute | solution.py:28
  96.5 3.2 pad_maximum_fusion.5
  99.7 2.9 collective-permute-start.11
  102.8 28.4 %collective-permute-done.11 = bf16[1,1,1,1,136,1088]{5,4,3,2,1,0:T(8,128)(2,1)S(1)} collective-permute-done((bf16[1,1,1,1,136,1088]{5,4,3,2,1,0:T(8,128)(2,1)S(1)}, bf16[1,1,1,1,136,1088]{5,4,3,2,1,0:T(8,128)(2,1)S(1)}, u32[]{:S(2)}, u32[]{:S(2)}) %collective-permute-start.11) | collective-permute-done | bytes 295968 | tf_op jit(solution)/shard_map/ppermute | solution.py:28
  135.9 11.9 %collective-permute-done.12 = bf16[1,1,2,1,136,1088]{5,4,3,2,1,0:T(8,128)(2,1)} collective-permute-done((bf16[1,1,2,1,136,1088]{5,4,3,2,1,0:T(8,128)(2,1)}, bf16[1,1,2,1,136,1088]{5,4,3,2,1,0:T(8,128)(2,1)}, u32[]{:S(2)}, u32[]{:S(2)}) %collective-permute-start.12) | collective-permute-done | bytes 591904 | tf_op jit(solution)/shard_map/ppermute | solution.py:28
  147.8 2.4 pad_maximum_fusion.10
  154.0 2.5 fusion.7
  158.8 21.2 %collective-permute-done.13 = bf16[1,1,2,2,136,1088]{5,4,3,2,1,0:T(8,128)(2,1)} collective-permute-done((bf16[1,1,2,2,136,1088]{5,4,3,2,1,0:T(8,128)(2,1)}, bf16[1,1,2,2,136,1088]{5,4,3,2,1,0:T(8,128)(2,1)}, u32[]{:S(2)}, u32[]{:S(2)}) %collective-permute-start.13) | collective-permute-done | bytes 1183776 | tf_op jit(solution)/shard_map/ppermute | solution.py:28
  180.0 3.2 pad_maximum_fusion.6
  184.7 22.9 %reorder_weights.1 = bf16[32,136,1088]{2,1,0:T(8,128)(2,1)} custom-call(s32[17]{0:T(128)S(1)} %pad_add_fusion.take_ref, bf16[16,64,1088]{2,1,0:T(8,128)(2,1)S(1)} %bitcast.167, bf16[16,80,1088]{2,1,0:T(8,128)(2,1)} %bitcast.9.high_mine, bf16[16,64,1088]{2,1,0:T(8,128)(2,1)} %collective-permute-done.9.low_other, ...), custom_call_target="tpu_custom_call" | custom-call | bytes 28409856 | tf_op jit(solution)/shard_map/reorder_weights/pallas_call | solution.py:93
  207.6 7.0 %slice.504 = bf16[4,1088,816]{2,1,0:T(8,128)(2,1)} slice(bf16[4,1088,1088]{2,1,0:T(8,128)(2,1)} %bitcast.179), slice={[0:4], [0:1088], [0:816]} | slice | bytes 14204928 | tf_op jit(solution)/shard_map/slice | solution.py:403
  214.6 11.3 %copy.120 = bf16[4,1088,816]{1,2,0:T(8,128)(2,1)} copy(bf16[4,1088,816]{2,1,0:T(8,128)(2,1)} %slice.504) | data formatting | bytes 14204928
  225.9 14.2 %add_convert_fusion.q_ref.k_ref.v_ref.q_own.k_own.v_own = bf16[3264,1024]{1,0:T(8,128)(2,1)} fusion(bf16[3264,1088]{1,0:T(8,128)(2,1)} %bitcast.207, bf16[1024,1088]{1,0:T(8,128)(2,1)S(1)} %bitcast.246, f32[3264]{0:T(1024)S(1)} %concatenate.158), kind=kOutput, calls=%fused_computation.2 | convolution fusion | flops 7279607808 | bytes 16028416 | tf_op jit(solution)/shard_map/cdn,rd->cnr/dot_general | solution.py:140
  240.0 16.5 %attend.1 = (bf16[1088,256]{1,0:T(8,128)(2,1)S(1)}, f32[17,1,256]{2,1,0:T(1,128)S(1)}) custom-call(s32[1]{0:T(128)} %bitcast.4.z_ref, bf16[3264,1024]{1,0:T(8,128)(2,1)} %add_convert_fusion.q_ref.k_ref.v_ref.q_own.k_own.v_own, bf16[3264,1024]{1,0:T(8,128)(2,1)} %add_convert_fusion.q_ref.k_ref.v_ref.q_own.k_own.v_own, ...), custom_call_target="tpu_custom_call" | custom-call | flops 1140850688 | bytes 4456448 | tf_op jit(solution)/shard_map/attend/pallas_call | solution.py:262
  273.9 6.4 pad_maximum_fusion.4
  280.3 8.8 %reorder_blocks.2 = bf16[16,136,1088]{2,1,0:T(8,128)(2,1)S(1)} custom-call(s32[16]{0:T(128)S(1)} %add.315.take_ref, bf16[16,136,1088]{2,1,0:T(8,128)(2,1)} %bitcast.224), custom_call_target="tpu_custom_call" | custom-call | bytes 9469952 | tf_op jit(solution)/shard_map/reorder_blocks/pallas_call | solution.py:114
  289.1 3.4 convolution_add_fusion.3
  292.6 3.4 convolution_add_fusion.2
  296.0 3.2 convolution_convert_fusion.1
  299.3 3.9 convert_reduce_fusion.2
  303.2 3.3 convert_reduce_fusion.3
  306.6 5.1 fusion.107
  311.7 2.9 convolution_convert_fusion
  315.5 6.5 fusion.121
  324.1 7.8 %fusion = bf16[2176,1088]{0,1:T(8,128)(2,1)} fusion(f32[2176,1088]{0,1:T(8,128)} %fusion.121, bf16[256,1088]{0,1:T(8,128)(2,1)} %collective-permute-done.15, bf16[256,2176]{1,0:T(8,128)(2,1)} %copy-done.65), kind=kOutput, calls=%fused_computation.3 | convolution fusion | flops 1216888832 | bytes 15876096 | tf_op jit(solution)/shard_map/rn,rd->nd/dot_general | solution.py:140
  331.9 8.3 %copy.117 = bf16[2176,1088]{1,0:T(8,128)(2,1)} copy(bf16[2176,1088]{0,1:T(8,128)(2,1)} %fusion) | data formatting | bytes 9469952 | tf_op jit(solution)/shard_map/convert_element_type | solution.py:47
  340.2 3.6 slice.578
  345.7 5.4 fusion.1
  352.1 4.1 fusion.114
  356.2 6.7 copy.118
  362.9 5.5 copy.119
  370.5 5.4 multiply_reduce_fusion
  382.6 5.0 fusion.14
  391.8 2.7 convert_multiply_fusion
  408.7 15.2 %collective-permute-done.45 = f32[4,1088]{1,0:T(4,128)S(1)} collective-permute-done((f32[4,1088]{1,0:T(4,128)S(1)}, f32[4,1088]{1,0:T(4,128)S(1)}, u32[]{:S(2)}, u32[]{:S(2)}) %collective-permute-start.45) | collective-permute-done | bytes 17440 | tf_op jit(solution)/shard_map/ppermute | solution.py:28
  430.5 24.0 %collective-permute-done.19 = bf16[1,1,1088,256]{3,2,1,0:T(8,128)(2,1)S(1)} collective-permute-done((bf16[1,1,1088,256]{3,2,1,0:T(8,128)(2,1)S(1)}, bf16[1,1,1088,256]{3,2,1,0:T(8,128)(2,1)S(1)}, u32[]{:S(2)}, u32[]{:S(2)}) %collective-permute-start.19) | collective-permute-done | bytes 557088 | tf_op jit(solution)/shard_map/ppermute | solution.py:28
  469.4 12.5 %collective-permute-done.20 = bf16[2,1,1088,256]{3,2,1,0:T(8,128)(2,1)} collective-permute-done((bf16[2,1,1088,256]{3,2,1,0:T(8,128)(2,1)}, bf16[2,1,1088,256]{3,2,1,0:T(8,128)(2,1)}, u32[]{:S(2)}, u32[]{:S(2)}) %collective-permute-start.20) | collective-permute-done | bytes 1114144 | tf_op jit(solution)/shard_map/ppermute | solution.py:28
  483.4 30.8 %attend_back.1 = bf16[3,1088,256]{2,1,0:T(8,128)(2,1)S(1)} custom-call(s32[1]{0:T(128)} %bitcast.4.z_ref, bf16[3264,1024]{1,0:T(8,128)(2,1)} %add_convert_fusion.q_ref.k_ref.v_ref.q_own.k_own.v_own, bf16[3264,1024]{1,0:T(8,128)(2,1)} %add_convert_fusion.q_ref.k_ref.v_ref.q_own.k_own.v_own, ...), custom_call_target="tpu_custom_call" | custom-call | flops 2281701376 | bytes 8912896 | tf_op jit(solution)/shard_map/attend_back/pallas_call | solution.py:293
  517.2 2.3 convolution_add_fusion.6
  519.5 2.3 convolution_add_fusion.5
  521.8 2.3 fusion.42
  529.0 3.5 collective-permute-done.27
  533.3 3.1 collective-permute-done.28
  544.6 2.7 add_convert_fusion.2
  553.7 21.0 %collective-permute-done.48 = bf16[1,1,2,2,136,1088]{5,4,3,2,1,0:T(8,128)(2,1)S(1)} collective-permute-done((bf16[1,1,2,2,136,1088]{5,4,3,2,1,0:T(8,128)(2,1)S(1)}, bf16[1,1,2,2,136,1088]{5,4,3,2,1,0:T(8,128)(2,1)S(1)}, u32[]{:S(2)}, u32[]{:S(2)}) %collective-permute-start.48) | collective-permute-done | bytes 1183776 | tf_op jit(solution)/shard_map/ppermute | solution.py:28
  580.8 23.2 %fusion.4 = bf16[2176,1088]{1,0:T(8,128)(2,1)} fusion(bf16[544,272]{1,0:T(8,128)(2,1)S(1)} %copy-done.61, bf16[544,816]{1,0:T(8,128)(2,1)S(1)} %add_convert_fusion.6, bf16[544,272]{1,0:T(8,128)(2,1)S(1)} %copy-done.62, bf16[544,816]{1,0:T(8,128)(2,1)S(1)} %add_convert_fusion.7, bf16[544,272]{1,0:T(8,128)(2,1)S(1)} %copy-done.63, ...), kind=kLoop, calls=%fused_computation.10 | loop fusion | flops 37879808 | bytes 9469952 | tf_op jit(solution)/shard_map/concatenate | solution.py:493
  603.9 8.8 %reorder_blocks.3 = bf16[16,136,1088]{2,1,0:T(8,128)(2,1)S(1)} custom-call(s32[16]{0:T(128)S(1)} %add.315.take_ref, bf16[16,136,1088]{2,1,0:T(8,128)(2,1)} %bitcast.204), custom_call_target="tpu_custom_call" | custom-call | bytes 9469952 | tf_op jit(solution)/shard_map/reorder_blocks/pallas_call | solution.py:114
  616.9 3.0 collective-permute-start.50
  620.1 17.2 %collective-permute-done.50 = bf16[1,1,1,1,136,1088]{5,4,3,2,1,0:T(8,128)(2,1)S(1)} collective-permute-done((bf16[1,1,1,1,136,1088]{5,4,3,2,1,0:T(8,128)(2,1)S(1)}, bf16[1,1,1,1,136,1088]{5,4,3,2,1,0:T(8,128)(2,1)S(1)}, u32[]{:S(2)}, u32[]{:S(2)}) %collective-permute-start.50) | collective-permute-done | bytes 295968 | tf_op jit(solution)/shard_map/ppermute | solution.py:28
  639.4 5.5 collective-permute-done.38
  646.6 8.4 %collective-permute-done.35 = bf16[1,1,2,2,64,1088]{5,4,3,2,1,0:T(8,128)(2,1)S(1)} collective-permute-done((bf16[1,1,2,2,64,1088]{5,4,3,2,1,0:T(8,128)(2,1)S(1)}, bf16[1,1,2,2,64,1088]{5,4,3,2,1,0:T(8,128)(2,1)S(1)}, u32[]{:S(2)}, u32[]{:S(2)}) %collective-permute-start.35) | collective-permute-done | bytes 557088 | tf_op jit(solution)/shard_map/ppermute | solution.py:28
  657.0 3.4 collective-permute-start.40
  660.4 6.4 collective-permute-done.36
  667.7 2.7 collective-permute-done.40
  672.1 6.5 collective-permute-done.37
  (454 shorter events, 157.2 us)
Async XLA Ops:
  7.2 144.5 %all-gather.5.cloned.1.call-start = ((), (), s32[]{:S(2)}) async-start(), calls=%async_computation | async-start | bytes 3041280 | tf_op jit(solution)/shard_map/all_gather | solution.py:377
  8.3 41.2 %copy-start.18 = (bf16[1,1,1,1,64,1088]{5,4,3,2,1,0:T(8,128)(2,1)}, bf16[1,1,1,1,64,1088]{5,4,3,2,1,0:T(8,128)(2,1)S(1)}, u32[]{:S(2)}) copy-start(bf16[1,1,1,1,64,1088]{5,4,3,2,1,0:T(8,128)(2,1)S(1)} %fusion.82) | copy-start | bytes 417796
  8.3 15.9 %collective-permute-start.1 = (bf16[1,1,1,1,64,1088]{5,4,3,2,1,0:T(8,128)(2,1)S(1)}, bf16[1,1,1,1,64,1088]{5,4,3,2,1,0:T(8,128)(2,1)S(1)}, u32[]{:S(2)}, u32[]{:S(2)}) collective-permute-start(bf16[1,1,1,1,64,1088]{5,4,3,2,1,0:T(8,128)(2,1)S(1)} %fusion.82), channel_id=1, source_target_pairs={{0,4},{2,6},{4,0},{6,2},{1,5},{3,7},{5,1},{7,3},{8,12},{10,14},{12... | collective-permute-start | bytes 417800 | tf_op jit(solution)/shard_map/ppermute | solution.py:28
  14.2 13.2 %collective-permute-start.5 = (bf16[1,1,1,1,80,1088]{5,4,3,2,1,0:T(8,128)(2,1)S(1)}, bf16[1,1,1,1,80,1088]{5,4,3,2,1,0:T(8,128)(2,1)S(1)}, u32[]{:S(2)}, u32[]{:S(2)}) collective-permute-start(bf16[1,1,1,1,80,1088]{5,4,3,2,1,0:T(8,128)(2,1)S(1)} %fusion.77), channel_id=1, source_target_pairs={{0,4},{2,6},{4,0},{6,2},{1,5},{3,7},{5,1},{7,3},{8,12},{10,14},{12... | collective-permute-start | bytes 522248 | tf_op jit(solution)/shard_map/ppermute | solution.py:28
  24.3 10.0 %collective-permute-start.2 = (bf16[1,1,2,1,64,1088]{5,4,3,2,1,0:T(8,128)(2,1)S(1)}, bf16[1,1,2,1,64,1088]{5,4,3,2,1,0:T(8,128)(2,1)S(1)}, u32[]{:S(2)}, u32[]{:S(2)}) collective-permute-start(bf16[1,1,2,1,64,1088]{5,4,3,2,1,0:T(8,128)(2,1)S(1)} %pad_maximum_fusion.26), channel_id=1, source_target_pairs={{0,2},{2,0},{4,6},{6,4},{1,3},{3,1},{5,7},{7,5},{8,10},{10,8},{12,... | collective-permute-start | bytes 835592 | tf_op jit(solution)/shard_map/ppermute | solution.py:28
  26.5 25.5 %collective-permute-start = (bf16[520,1088]{1,0:T(8,128)(2,1)}, bf16[520,1088]{1,0:T(8,128)(2,1)}, u32[]{:S(2)}, u32[]{:S(2)}) collective-permute-start(bf16[520,1088]{1,0:T(8,128)(2,1)} %copy.106), channel_id=1, source_target_pairs={{0,1},{1,0},{2,3},{3,2},{4,5},{5,4},{6,7},{7,6},{8,9},{9,8},{10,11... | collective-permute-start | bytes 3394568 | tf_op jit(solution)/shard_map/ppermute | solution.py:24
  28.2 13.3 %collective-permute-start.6 = (bf16[1,1,2,1,80,1088]{5,4,3,2,1,0:T(8,128)(2,1)}, bf16[1,1,2,1,80,1088]{5,4,3,2,1,0:T(8,128)(2,1)S(1)}, u32[]{:S(2)}, u32[]{:S(2)}) collective-permute-start(bf16[1,1,2,1,80,1088]{5,4,3,2,1,0:T(8,128)(2,1)} %pad_maximum_fusion.25), channel_id=1, source_target_pairs={{0,2},{2,0},{4,6},{6,4},{1,3},{3,1},{5,7},{7,5},{8,10},{10,8},{12,... | collective-permute-start | bytes 1044488 | tf_op jit(solution)/shard_map/ppermute | solution.py:28
  35.2 14.3 %collective-permute-start.3 = (bf16[1,1,2,2,64,1088]{5,4,3,2,1,0:T(8,128)(2,1)}, bf16[1,1,2,2,64,1088]{5,4,3,2,1,0:T(8,128)(2,1)S(1)}, u32[]{:S(2)}, u32[]{:S(2)}) collective-permute-start(bf16[1,1,2,2,64,1088]{5,4,3,2,1,0:T(8,128)(2,1)} %pad_maximum_fusion.15), channel_id=1, source_target_pairs={{0,16},{8,24},{16,0},{24,8},{1,17},{9,25},{17,1},{25,9},{2,18},{10... | collective-permute-start | bytes 1671176 | tf_op jit(solution)/shard_map/ppermute | solution.py:28
  42.5 19.7 %collective-permute-start.7 = (bf16[1,1,2,2,80,1088]{5,4,3,2,1,0:T(8,128)(2,1)}, bf16[1,1,2,2,80,1088]{5,4,3,2,1,0:T(8,128)(2,1)}, u32[]{:S(2)}, u32[]{:S(2)}) collective-permute-start(bf16[1,1,2,2,80,1088]{5,4,3,2,1,0:T(8,128)(2,1)} %pad_maximum_fusion.13), channel_id=1, source_target_pairs={{0,8},{8,0},{16,24},{24,16},{1,9},{9,1},{17,25},{25,17},{2,10},{10... | collective-permute-start | bytes 2088968 | tf_op jit(solution)/shard_map/ppermute | solution.py:28
  50.8 35.2 %collective-permute-start.4 = (bf16[2,1,2,2,64,1088]{5,4,3,2,1,0:T(8,128)(2,1)}, bf16[2,1,2,2,64,1088]{5,4,3,2,1,0:T(8,128)(2,1)}, u32[]{:S(2)}, u32[]{:S(2)}) collective-permute-start(bf16[2,1,2,2,64,1088]{5,4,3,2,1,0:T(8,128)(2,1)} %pad_maximum_fusion.11), channel_id=1, source_target_pairs={{0,8},{8,0},{16,24},{24,16},{1,9},{9,1},{17,25},{25,17},{2,10},{10... | collective-permute-start | bytes 3342344 | tf_op jit(solution)/shard_map/ppermute | solution.py:28
  64.9 31.6 %collective-permute-start.8 = (bf16[1,2,2,2,80,1088]{5,4,3,2,1,0:T(8,128)(2,1)}, bf16[1,2,2,2,80,1088]{5,4,3,2,1,0:T(8,128)(2,1)}, u32[]{:S(2)}, u32[]{:S(2)}) collective-permute-start(bf16[1,2,2,2,80,1088]{5,4,3,2,1,0:T(8,128)(2,1)} %pad_maximum_fusion.9), channel_id=1, source_target_pairs={{0,16},{8,24},{16,0},{24,8},{1,17},{9,25},{17,1},{25,9},{2,18},{10... | collective-permute-start | bytes 4177928 | tf_op jit(solution)/shard_map/ppermute | solution.py:28
  67.8 212.5 %all-gather.7.cloned.1.call-start = ((), (), s32[]{:S(2)}) async-start(), calls=%async_computation.1 | async-start | bytes 5326848 | tf_op jit(solution)/shard_map/all_gather | solution.py:391
  99.7 33.2 %copy-start.45 = (bf16[128,1088]{0,1:T(8,128)(2,1)S(1)}, bf16[128,1088]{0,1:T(8,128)(2,1)}, u32[]{:S(2)}) copy-start(bf16[128,1088]{0,1:T(8,128)(2,1)} %get-tuple-element.102) | copy-start | bytes 835588
  99.7 31.5 %collective-permute-start.11 = (bf16[1,1,1,1,136,1088]{5,4,3,2,1,0:T(8,128)(2,1)S(1)}, bf16[1,1,1,1,136,1088]{5,4,3,2,1,0:T(8,128)(2,1)S(1)}, u32[]{:S(2)}, u32[]{:S(2)}) collective-permute-start(bf16[1,1,1,1,136,1088]{5,4,3,2,1,0:T(8,128)(2,1)S(1)} %bitcast.231), channel_id=1, source_target_pairs={{0,4},{2,6},{4,0},{6,2},{1,5},{3,7},{5,1},{7,3},{8,12},{10,14},{12... | collective-permute-start | bytes 887816 | tf_op jit(solution)/shard_map/ppermute | solution.py:28
  132.8 15.0 %collective-permute-start.12 = (bf16[1,1,2,1,136,1088]{5,4,3,2,1,0:T(8,128)(2,1)}, bf16[1,1,2,1,136,1088]{5,4,3,2,1,0:T(8,128)(2,1)}, u32[]{:S(2)}, u32[]{:S(2)}) collective-permute-start(bf16[1,1,2,1,136,1088]{5,4,3,2,1,0:T(8,128)(2,1)} %pad_maximum_fusion.14), channel_id=1, source_target_pairs={{0,2},{2,0},{4,6},{6,4},{1,3},{3,1},{5,7},{7,5},{8,10},{10,8},{12,... | collective-permute-start | bytes 1775624 | tf_op jit(solution)/shard_map/ppermute | solution.py:28
  134.4 50.3 %collective-permute-start.9 = (bf16[16,64,1088]{2,1,0:T(8,128)(2,1)S(1)}, bf16[16,64,1088]{2,1,0:T(8,128)(2,1)}, u32[]{:S(2)}, u32[]{:S(2)}) collective-permute-start(bf16[16,64,1088]{2,1,0:T(8,128)(2,1)S(1)} %bitcast.166), channel_id=1, source_target_pairs={{0,1},{1,0},{2,3},{3,2},{4,5},{5,4},{6,7},{7,6},{8,9},{9,8},{10,11... | collective-permute-start | bytes 6684680 | tf_op jit(solution)/shard_map/ppermute | solution.py:24
  134.4 50.3 %collective-permute-start.10 = (bf16[16,80,1088]{2,1,0:T(8,128)(2,1)}, bf16[16,80,1088]{2,1,0:T(8,128)(2,1)}, u32[]{:S(2)}, u32[]{:S(2)}) collective-permute-start(bf16[16,80,1088]{2,1,0:T(8,128)(2,1)} %bitcast.9.high_mine), channel_id=1, source_target_pairs={{0,1},{1,0},{2,3},{3,2},{4,5},{5,4},{6,7},{7,6},{8,9},{9,8},{10,11... | collective-permute-start | bytes 8355848 | tf_op jit(solution)/shard_map/ppermute | solution.py:24
  150.2 29.8 %collective-permute-start.13 = (bf16[1,1,2,2,136,1088]{5,4,3,2,1,0:T(8,128)(2,1)}, bf16[1,1,2,2,136,1088]{5,4,3,2,1,0:T(8,128)(2,1)}, u32[]{:S(2)}, u32[]{:S(2)}) collective-permute-start(bf16[1,1,2,2,136,1088]{5,4,3,2,1,0:T(8,128)(2,1)} %pad_maximum_fusion.10), channel_id=1, source_target_pairs={{0,8},{8,0},{16,24},{24,16},{1,9},{9,1},{17,25},{25,17},{2,10},{10... | collective-permute-start | bytes 3551240 | tf_op jit(solution)/shard_map/ppermute | solution.py:28
  183.3 90.6 %collective-permute-start.14 = (bf16[1,2,2,2,136,1088]{5,4,3,2,1,0:T(8,128)(2,1)}, bf16[1,2,2,2,136,1088]{5,4,3,2,1,0:T(8,128)(2,1)}, u32[]{:S(2)}, u32[]{:S(2)}) collective-permute-start(bf16[1,2,2,2,136,1088]{5,4,3,2,1,0:T(8,128)(2,1)} %pad_maximum_fusion.6), channel_id=1, source_target_pairs={{0,16},{8,24},{16,0},{24,8},{1,17},{9,25},{17,1},{25,9},{2,18},{10... | collective-permute-start | bytes 7102472 | tf_op jit(solution)/shard_map/ppermute | solution.py:28
  256.6 12.5 %collective-permute-start.21 = (f32[1,1,17,1,256]{4,3,2,1,0:T(1,128)S(1)}, f32[1,1,17,1,256]{4,3,2,1,0:T(1,128)S(1)}, u32[]{:S(2)}, u32[]{:S(2)}) collective-permute-start(f32[1,1,17,1,256]{4,3,2,1,0:T(1,128)S(1)} %bitcast.176), channel_id=1, source_target_pairs={{0,4},{2,6},{4,0},{6,2},{1,5},{3,7},{5,1},{7,3},{8,12},{10,14},{12... | collective-permute-start | bytes 52232 | tf_op jit(solution)/shard_map/ppermute | solution.py:28
  258.3 14.8 %collective-permute-start.32 = (bf16[1088,256]{1,0:T(8,128)(2,1)S(1)}, bf16[1088,256]{1,0:T(8,128)(2,1)S(1)}, u32[]{:S(2)}, u32[]{:S(2)}) collective-permute-start(bf16[1088,256]{1,0:T(8,128)(2,1)S(1)} %get-tuple-element.25), channel_id=1, source_target_pairs={{0,1},{1,0},{2,3},{3,2},{4,5},{5,4},{6,7},{7,6},{8,9},{9,8},{10,11... | collective-permute-start | bytes 1671176 | tf_op jit(solution)/shard_map/ppermute | solution.py:24
  268.5 24.1 %collective-permute-start.15 = (bf16[256,1088]{0,1:T(8,128)(2,1)}, bf16[256,1088]{0,1:T(8,128)(2,1)}, u32[]{:S(2)}, u32[]{:S(2)}) collective-permute-start(bf16[256,1088]{0,1:T(8,128)(2,1)} %add_convert_fusion.17), channel_id=1, source_target_pairs={{0,1},{1,0},{2,3},{3,2},{4,5},{5,4},{6,7},{7,6},{8,9},{9,8},{10,11... | collective-permute-start | bytes 1671176 | tf_op jit(solution)/shard_map/ppermute | solution.py:24
  269.1 4.0 collective-permute-start.22
  311.6 70.9 %collective-permute-start.16 = (bf16[256,1088]{0,1:T(8,128)(2,1)}, bf16[256,1088]{0,1:T(8,128)(2,1)}, u32[]{:S(2)}, u32[]{:S(2)}) collective-permute-start(bf16[256,1088]{0,1:T(8,128)(2,1)} %convolution_convert_fusion.1), channel_id=1, source_target_pairs={{0,1},{1,0},{2,3},{3,2},{4,5},{5,4},{6,7},{7,6},{8,9},{9,8},{10,11... | collective-permute-start | bytes 1671176 | tf_op jit(solution)/shard_map/ppermute | solution.py:24
  314.6 55.9 %collective-permute-start.18 = (bf16[256,1088]{0,1:T(8,128)(2,1)}, bf16[256,1088]{0,1:T(8,128)(2,1)}, u32[]{:S(2)}, u32[]{:S(2)}) collective-permute-start(bf16[256,1088]{0,1:T(8,128)(2,1)} %convolution_convert_fusion), channel_id=1, source_target_pairs={{0,1},{1,0},{2,3},{3,2},{4,5},{5,4},{6,7},{7,6},{8,9},{9,8},{10,11... | collective-permute-start | bytes 1671176 | tf_op jit(solution)/shard_map/ppermute | solution.py:24
  315.3 6.9 %collective-permute-start.51 = (f32[2,4,136]{2,1,0:T(4,128)S(1)}, f32[2,4,136]{2,1,0:T(4,128)S(1)}, u32[]{:S(2)}, u32[]{:S(2)}) collective-permute-start(f32[2,4,136]{2,1,0:T(4,128)S(1)} %slice.481), channel_id=1, source_target_pairs={{0,16},{8,24},{16,0},{24,8},{1,17},{9,25},{17,1},{25,9},{2,18},{10... | collective-permute-start | bytes 13064 | tf_op jit(solution)/shard_map/ppermute | solution.py:28
  322.2 21.7 %collective-permute-start.52 = (f32[1,4,136]{2,1,0:T(4,128)S(1)}, f32[1,4,136]{2,1,0:T(4,128)S(1)}, u32[]{:S(2)}, u32[]{:S(2)}) collective-permute-start(f32[1,4,136]{2,1,0:T(4,128)S(1)} %slice.588), channel_id=1, source_target_pairs={{0,8},{8,0},{16,24},{24,16},{1,9},{9,1},{17,25},{25,17},{2,10},{10... | collective-permute-start | bytes 6536 | tf_op jit(solution)/shard_map/ppermute | solution.py:28
  343.8 200.9 %collective-permute-start.47 = (bf16[2,1,2,2,136,1088]{5,4,3,2,1,0:T(8,128)(2,1)}, bf16[2,1,2,2,136,1088]{5,4,3,2,1,0:T(8,128)(2,1)}, u32[]{:S(2)}, u32[]{:S(2)}) collective-permute-start(bf16[2,1,2,2,136,1088]{5,4,3,2,1,0:T(8,128)(2,1)} %slice.578), channel_id=1, source_target_pairs={{0,8},{8,0},{16,24},{24,16},{1,9},{9,1},{17,25},{25,17},{2,10},{10... | collective-permute-start | bytes 7102472 | tf_op jit(solution)/shard_map/ppermute | solution.py:28
  343.9 7.1 %collective-permute-start.53 = (f32[1,2,136]{2,1,0:T(2,128)S(1)}, f32[1,2,136]{2,1,0:T(2,128)S(1)}, u32[]{:S(2)}, u32[]{:S(2)}) collective-permute-start(f32[1,2,136]{2,1,0:T(2,128)S(1)} %slice.590), channel_id=1, source_target_pairs={{0,4},{2,6},{4,0},{6,2},{1,5},{3,7},{5,1},{7,3},{8,12},{10,14},{12... | collective-permute-start | bytes 3272 | tf_op jit(solution)/shard_map/ppermute | solution.py:28
  351.1 18.8 %collective-permute-start.54 = (f32[1,1,136]{2,1,0:T(1,128)S(1)}, f32[1,1,136]{2,1,0:T(1,128)S(1)}, u32[]{:S(2)}, u32[]{:S(2)}) collective-permute-start(f32[1,1,136]{2,1,0:T(1,128)S(1)} %slice.592), channel_id=1, source_target_pairs={{0,2},{2,0},{4,6},{6,4},{1,3},{3,1},{5,7},{7,5},{8,10},{10,8},{12,... | collective-permute-start | bytes 1640 | tf_op jit(solution)/shard_map/ppermute | solution.py:28
  368.4 180.6 %collective-permute-start.55 = (bf16[1,2,2,2,136,1088]{5,4,3,2,1,0:T(8,128)(2,1)}, bf16[1,2,2,2,136,1088]{5,4,3,2,1,0:T(8,128)(2,1)}, u32[]{:S(2)}, u32[]{:S(2)}) collective-permute-start(bf16[1,2,2,2,136,1088]{5,4,3,2,1,0:T(8,128)(2,1)} %bitcast.245), channel_id=1, source_target_pairs={{0,16},{8,24},{16,0},{24,8},{1,17},{9,25},{17,1},{25,9},{2,18},{10... | collective-permute-start | bytes 7102472 | tf_op jit(solution)/shard_map/ppermute | solution.py:28
  394.5 2.7 collective-permute-start.42
  397.2 33.2 %copy-start.57 = (bf16[256,1088]{0,1:T(8,128)(2,1)S(1)}, bf16[256,1088]{0,1:T(8,128)(2,1)}, u32[]{:S(2)}) copy-start(bf16[256,1088]{0,1:T(8,128)(2,1)} %copy-done.56) | copy-start | bytes 1671172
  397.3 4.9 collective-permute-start.43
  399.6 30.9 %collective-permute-start.17 = (bf16[128,1088]{0,1:T(8,128)(2,1)}, bf16[128,1088]{0,1:T(8,128)(2,1)S(1)}, u32[]{:S(2)}, u32[]{:S(2)}) collective-permute-start(bf16[128,1088]{0,1:T(8,128)(2,1)} %broadcast_select_fusion.8), channel_id=1, source_target_pairs={{0,1},{1,0},{2,3},{3,2},{4,5},{5,4},{6,7},{7,6},{8,9},{9,8},{10,11... | collective-permute-start | bytes 835592 | tf_op jit(solution)/shard_map/ppermute | solution.py:24
  399.9 4.8 collective-permute-start.23
  402.2 3.8 collective-permute-start.44
  404.7 19.3 %collective-permute-start.24 = (f32[2,1,17,1,256]{4,3,2,1,0:T(1,128)S(1)}, f32[2,1,17,1,256]{4,3,2,1,0:T(1,128)S(1)}, u32[]{:S(2)}, u32[]{:S(2)}) collective-permute-start(f32[2,1,17,1,256]{4,3,2,1,0:T(1,128)S(1)} %constant_dynamic-update-slice_fusion), channel_id=1, source_target_pairs={{0,2},{2,0},{4,6},{6,4},{1,3},{3,1},{5,7},{7,5},{8,10},{10,8},{12,... | collective-permute-start | bytes 104456 | tf_op jit(solution)/shard_map/ppermute | solution.py:28
  406.1 17.9 %collective-permute-start.45 = (f32[4,1088]{1,0:T(4,128)S(1)}, f32[4,1088]{1,0:T(4,128)S(1)}, u32[]{:S(2)}, u32[]{:S(2)}) collective-permute-start(f32[4,1088]{1,0:T(4,128)S(1)} %add.377), channel_id=1, source_target_pairs={{0,16},{8,24},{16,0},{24,8},{1,17},{9,25},{17,1},{25,9},{2,18},{10... | collective-permute-start | bytes 52232 | tf_op jit(solution)/shard_map/ppermute | solution.py:28
  424.0 32.6 %collective-permute-start.33 = (bf16[256,1088]{0,1:T(8,128)(2,1)S(1)}, bf16[256,1088]{0,1:T(8,128)(2,1)S(1)}, u32[]{:S(2)}, u32[]{:S(2)}) collective-permute-start(bf16[256,1088]{0,1:T(8,128)(2,1)S(1)} %copy-done.9), channel_id=1, source_target_pairs={{0,1},{1,0},{2,3},{3,2},{4,5},{5,4},{6,7},{7,6},{8,9},{9,8},{10,11... | collective-permute-start | bytes 1671176 | tf_op jit(solution)/shard_map/ppermute | solution.py:24
  424.0 3.8 collective-permute-start.46
  427.8 26.7 %collective-permute-start.19 = (bf16[1,1,1088,256]{3,2,1,0:T(8,128)(2,1)S(1)}, bf16[1,1,1088,256]{3,2,1,0:T(8,128)(2,1)S(1)}, u32[]{:S(2)}, u32[]{:S(2)}) collective-permute-start(bf16[1,1,1088,256]{3,2,1,0:T(8,128)(2,1)S(1)} %bitcast.236), channel_id=1, source_target_pairs={{0,4},{2,6},{4,0},{6,2},{1,5},{3,7},{5,1},{7,3},{8,12},{10,14},{12... | collective-permute-start | bytes 1671176 | tf_op jit(solution)/shard_map/ppermute | solution.py:28
  455.8 26.2 %collective-permute-start.20 = (bf16[2,1,1088,256]{3,2,1,0:T(8,128)(2,1)}, bf16[2,1,1088,256]{3,2,1,0:T(8,128)(2,1)}, u32[]{:S(2)}, u32[]{:S(2)}) collective-permute-start(bf16[2,1,1088,256]{3,2,1,0:T(8,128)(2,1)} %pad_maximum_fusion.12), channel_id=1, source_target_pairs={{0,2},{2,0},{4,6},{6,4},{1,3},{3,1},{5,7},{7,5},{8,10},{10,8},{12,... | collective-permute-start | bytes 3342344 | tf_op jit(solution)/shard_map/ppermute | solution.py:28
  517.1 60.7 %collective-permute-start.31 = (bf16[3264,256]{1,0:T(8,128)(2,1)S(1)}, bf16[3264,256]{1,0:T(8,128)(2,1)S(1)}, u32[]{:S(2)}, u32[]{:S(2)}) collective-permute-start(bf16[3264,256]{1,0:T(8,128)(2,1)S(1)} %bitcast.158), channel_id=1, source_target_pairs={{0,1},{1,0},{2,3},{3,2},{4,5},{5,4},{6,7},{7,6},{8,9},{9,8},{10,11... | collective-permute-start | bytes 5013512 | tf_op jit(solution)/shard_map/ppermute | solution.py:24
  526.1 1.7 collective-permute-start.26
  527.8 4.7 collective-permute-start.27
  532.6 3.8 collective-permute-start.28
  536.4 3.8 collective-permute-start.29
  538.4 14.4 %collective-permute-start.25 = (bf16[128,1088]{0,1:T(8,128)(2,1)S(1)}, bf16[128,1088]{0,1:T(8,128)(2,1)S(1)}, u32[]{:S(2)}, u32[]{:S(2)}) collective-permute-start(bf16[128,1088]{0,1:T(8,128)(2,1)S(1)} %broadcast_select_fusion.6), channel_id=1, source_target_pairs={{0,1},{1,0},{2,3},{3,2},{4,5},{5,4},{6,7},{7,6},{8,9},{9,8},{10,11... | collective-permute-start | bytes 835592 | tf_op jit(solution)/shard_map/ppermute | solution.py:24
  540.2 3.8 collective-permute-start.30
  547.4 27.2 %collective-permute-start.48 = (bf16[1,1,2,2,136,1088]{5,4,3,2,1,0:T(8,128)(2,1)S(1)}, bf16[1,1,2,2,136,1088]{5,4,3,2,1,0:T(8,128)(2,1)S(1)}, u32[]{:S(2)}, u32[]{:S(2)}) collective-permute-start(bf16[1,1,2,2,136,1088]{5,4,3,2,1,0:T(8,128)(2,1)S(1)} %slice.580), channel_id=1, source_target_pairs={{0,16},{8,24},{16,0},{24,8},{1,17},{9,25},{17,1},{25,9},{2,18},{10... | collective-permute-start | bytes 3551240 | tf_op jit(solution)/shard_map/ppermute | solution.py:28
  551.3 26.0 %collective-permute-start.56 = (bf16[1,1,2,2,136,1088]{5,4,3,2,1,0:T(8,128)(2,1)S(1)}, bf16[1,1,2,2,136,1088]{5,4,3,2,1,0:T(8,128)(2,1)S(1)}, u32[]{:S(2)}, u32[]{:S(2)}) collective-permute-start(bf16[1,1,2,2,136,1088]{5,4,3,2,1,0:T(8,128)(2,1)S(1)} %slice.596), channel_id=1, source_target_pairs={{0,8},{8,0},{16,24},{24,16},{1,9},{9,1},{17,25},{25,17},{2,10},{10... | collective-permute-start | bytes 3551240 | tf_op jit(solution)/shard_map/ppermute | solution.py:28
  575.0 41.7 %collective-permute-start.49 = (bf16[1,1,2,1,136,1088]{5,4,3,2,1,0:T(8,128)(2,1)S(1)}, bf16[1,1,2,1,136,1088]{5,4,3,2,1,0:T(8,128)(2,1)S(1)}, u32[]{:S(2)}, u32[]{:S(2)}) collective-permute-start(bf16[1,1,2,1,136,1088]{5,4,3,2,1,0:T(8,128)(2,1)S(1)} %slice.582), channel_id=1, source_target_pairs={{0,2},{2,0},{4,6},{6,4},{1,3},{3,1},{5,7},{7,5},{8,10},{10,8},{12,... | collective-permute-start | bytes 1775624 | tf_op jit(solution)/shard_map/ppermute | solution.py:28
  577.6 42.2 %collective-permute-start.57 = (bf16[1,1,2,1,136,1088]{5,4,3,2,1,0:T(8,128)(2,1)S(1)}, bf16[1,1,2,1,136,1088]{5,4,3,2,1,0:T(8,128)(2,1)S(1)}, u32[]{:S(2)}, u32[]{:S(2)}) collective-permute-start(bf16[1,1,2,1,136,1088]{5,4,3,2,1,0:T(8,128)(2,1)S(1)} %slice.598), channel_id=1, source_target_pairs={{0,2},{2,0},{4,6},{6,4},{1,3},{3,1},{5,7},{7,5},{8,10},{10,8},{12,... | collective-permute-start | bytes 1775624 | tf_op jit(solution)/shard_map/ppermute | solution.py:28
  613.3 24.9 %collective-permute-start.34 = (bf16[1,2,2,2,64,1088]{5,4,3,2,1,0:T(8,128)(2,1)S(1)}, bf16[1,2,2,2,64,1088]{5,4,3,2,1,0:T(8,128)(2,1)S(1)}, u32[]{:S(2)}, u32[]{:S(2)}) collective-permute-start(bf16[1,2,2,2,64,1088]{5,4,3,2,1,0:T(8,128)(2,1)S(1)} %bitcast.247), channel_id=1, source_target_pairs={{0,16},{8,24},{16,0},{24,8},{1,17},{9,25},{17,1},{25,9},{2,18},{10... | collective-permute-start | bytes 3342344 | tf_op jit(solution)/shard_map/ppermute | solution.py:28
  615.1 29.8 %collective-permute-start.38 = (bf16[2,1,2,2,72,1088]{5,4,3,2,1,0:T(8,128)(2,1)S(1)}, bf16[2,1,2,2,72,1088]{5,4,3,2,1,0:T(8,128)(2,1)S(1)}, u32[]{:S(2)}, u32[]{:S(2)}) collective-permute-start(bf16[2,1,2,2,72,1088]{5,4,3,2,1,0:T(8,128)(2,1)S(1)} %slice.563), channel_id=1, source_target_pairs={{0,8},{8,0},{16,24},{24,16},{1,9},{9,1},{17,25},{25,17},{2,10},{10... | collective-permute-start | bytes 3760136 | tf_op jit(solution)/shard_map/ppermute | solution.py:28
  616.9 20.5 %collective-permute-start.50 = (bf16[1,1,1,1,136,1088]{5,4,3,2,1,0:T(8,128)(2,1)S(1)}, bf16[1,1,1,1,136,1088]{5,4,3,2,1,0:T(8,128)(2,1)S(1)}, u32[]{:S(2)}, u32[]{:S(2)}) collective-permute-start(bf16[1,1,1,1,136,1088]{5,4,3,2,1,0:T(8,128)(2,1)S(1)} %slice.584), channel_id=1, source_target_pairs={{0,4},{2,6},{4,0},{6,2},{1,5},{3,7},{5,1},{7,3},{8,12},{10,14},{12... | collective-permute-start | bytes 887816 | tf_op jit(solution)/shard_map/ppermute | solution.py:28
  620.1 25.6 %collective-permute-start.58 = (bf16[1,1,1,1,136,1088]{5,4,3,2,1,0:T(8,128)(2,1)S(1)}, bf16[1,1,1,1,136,1088]{5,4,3,2,1,0:T(8,128)(2,1)S(1)}, u32[]{:S(2)}, u32[]{:S(2)}) collective-permute-start(bf16[1,1,1,1,136,1088]{5,4,3,2,1,0:T(8,128)(2,1)S(1)} %slice.600), channel_id=1, source_target_pairs={{0,4},{2,6},{4,0},{6,2},{1,5},{3,7},{5,1},{7,3},{8,12},{10,14},{12... | collective-permute-start | bytes 887816 | tf_op jit(solution)/shard_map/ppermute | solution.py:28
  638.6 16.4 %collective-permute-start.35 = (bf16[1,1,2,2,64,1088]{5,4,3,2,1,0:T(8,128)(2,1)S(1)}, bf16[1,1,2,2,64,1088]{5,4,3,2,1,0:T(8,128)(2,1)S(1)}, u32[]{:S(2)}, u32[]{:S(2)}) collective-permute-start(bf16[1,1,2,2,64,1088]{5,4,3,2,1,0:T(8,128)(2,1)S(1)} %slice.556), channel_id=1, source_target_pairs={{0,8},{8,0},{16,24},{24,16},{1,9},{9,1},{17,25},{25,17},{2,10},{10... | collective-permute-start | bytes 1671176 | tf_op jit(solution)/shard_map/ppermute | solution.py:28
  645.3 11.5 %collective-permute-start.39 = (bf16[1,1,2,2,72,1088]{5,4,3,2,1,0:T(8,128)(2,1)S(1)}, bf16[1,1,2,2,72,1088]{5,4,3,2,1,0:T(8,128)(2,1)S(1)}, u32[]{:S(2)}, u32[]{:S(2)}) collective-permute-start(bf16[1,1,2,2,72,1088]{5,4,3,2,1,0:T(8,128)(2,1)S(1)} %slice.565), channel_id=1, source_target_pairs={{0,16},{8,24},{16,0},{24,8},{1,17},{9,25},{17,1},{25,9},{2,18},{10... | collective-permute-start | bytes 1880072 | tf_op jit(solution)/shard_map/ppermute | solution.py:28
  655.2 11.6 %collective-permute-start.36 = (bf16[1,1,2,1,64,1088]{5,4,3,2,1,0:T(8,128)(2,1)S(1)}, bf16[1,1,2,1,64,1088]{5,4,3,2,1,0:T(8,128)(2,1)S(1)}, u32[]{:S(2)}, u32[]{:S(2)}) collective-permute-start(bf16[1,1,2,1,64,1088]{5,4,3,2,1,0:T(8,128)(2,1)S(1)} %slice.558), channel_id=1, source_target_pairs={{0,2},{2,0},{4,6},{6,4},{1,3},{3,1},{5,7},{7,5},{8,10},{10,8},{12,... | collective-permute-start | bytes 835592 | tf_op jit(solution)/shard_map/ppermute | solution.py:28
  657.0 13.3 %collective-permute-start.40 = (bf16[1,1,2,1,72,1088]{5,4,3,2,1,0:T(8,128)(2,1)S(1)}, bf16[1,1,2,1,72,1088]{5,4,3,2,1,0:T(8,128)(2,1)S(1)}, u32[]{:S(2)}, u32[]{:S(2)}) collective-permute-start(bf16[1,1,2,1,72,1088]{5,4,3,2,1,0:T(8,128)(2,1)S(1)} %slice.567), channel_id=1, source_target_pairs={{0,2},{2,0},{4,6},{6,4},{1,3},{3,1},{5,7},{7,5},{8,10},{10,8},{12,... | collective-permute-start | bytes 940040 | tf_op jit(solution)/shard_map/ppermute | solution.py:28
  666.9 11.8 %collective-permute-start.37 = (bf16[1,1,1,1,64,1088]{5,4,3,2,1,0:T(8,128)(2,1)S(1)}, bf16[1,1,1,1,64,1088]{5,4,3,2,1,0:T(8,128)(2,1)S(1)}, u32[]{:S(2)}, u32[]{:S(2)}) collective-permute-start(bf16[1,1,1,1,64,1088]{5,4,3,2,1,0:T(8,128)(2,1)S(1)} %slice.560), channel_id=1, source_target_pairs={{0,4},{2,6},{4,0},{6,2},{1,5},{3,7},{5,1},{7,3},{8,12},{10,14},{12... | collective-permute-start | bytes 417800 | tf_op jit(solution)/shard_map/ppermute | solution.py:28
  670.5 9.9 %collective-permute-start.41 = (bf16[1,1,1,1,72,1088]{5,4,3,2,1,0:T(8,128)(2,1)S(1)}, bf16[1,1,1,1,72,1088]{5,4,3,2,1,0:T(8,128)(2,1)S(1)}, u32[]{:S(2)}, u32[]{:S(2)}) collective-permute-start(bf16[1,1,1,1,72,1088]{5,4,3,2,1,0:T(8,128)(2,1)S(1)} %slice.569), channel_id=1, source_target_pairs={{0,4},{2,6},{4,0},{6,2},{1,5},{3,7},{5,1},{7,3},{8,12},{10,14},{12... | collective-permute-start | bytes 470024 | tf_op jit(solution)/shard_map/ppermute | solution.py:28
  (86 other events, 848.9 us)
Sparse Core Ops, SparseCore 0:
  67.9 65.0 all-gather.4
  151.9 101.9 all-gather.6

commit v3 on v2

--- a/solution.py
+++ b/solution.py
@@ -478,7 +478,7 @@
     h1_other = normalize(x_other.astype(F32), ln1_gain, ln1_bias).astype(BF16)
     h1_mine, h1_mine_other = my_columns(h1_own), my_columns(h1_other)
     att_mine, att_mine_other = my_rows(att_t), my_rows(att_other_t)
-    pair_parts = []
+    qkv_parts, proj_parts = [], []
     for i in range(dp):
         span = slice(i * qkv_cols, (i + 1) * qkv_cols)
         qkv_part = contract("ra,nr->an", h1_mine, dj_t[span]) + contract(
@@ -488,12 +488,13 @@
         proj_part = contract("ar,rn->an", att_mine, d_branch[:, span]) + contract(
             "ar,rn->an", att_mine_other, d_branch_other[:, span]
         )
-        pair_parts.append(jnp.concatenate([qkv_part.astype(BF16), proj_part.astype(BF16)], 1))
-    pair_sent = reorder_blocks(
-        take, jnp.concatenate(pair_parts, 0).reshape(dp * nz, shard_rows, qkv_cols + proj_cols)
-    )
-    pair_grad = jnp.concatenate(
-        [halved(pair_sent[:, :cut], shrink[0]), halved(pair_sent[:, cut:], shrink[1])], 0
+        qkv_parts.append(qkv_part.astype(BF16))
+        proj_parts.append(proj_part.astype(BF16))
+    qkv_sent = reorder_blocks(take, jnp.concatenate(qkv_parts, 0).reshape(dp * nz, shard_rows, -1))
+    proj_sent = reorder_blocks(take, jnp.concatenate(proj_parts, 0).reshape(dp * nz, shard_rows, -1))
+    proj_grad = halved(proj_sent, shrink[0])
+    qkv_grad = jnp.concatenate(
+        [halved(qkv_sent[:, :cut], shrink[0]), halved(qkv_sent[:, cut:], shrink[1])], 0
     )
 
     _, ln1_back = jax.vjp(normalize, x_f, ln1_gain, ln1_bias)
@@ -517,10 +518,10 @@
         placed(input_grad),
         late_sum[0],
         late_sum[1],
-        pair_grad[:, :qkv_cols].astype(F32),
+        qkv_grad.astype(F32),
         late_sum[2],
         late_sum[3],
-        pair_grad[:, qkv_cols:].astype(F32),
+        proj_grad.astype(F32),
         early_sum[1],
         early_sum[2],
         early_sum[3],

time: 696 us -> 685 us (0.984)
  other arithmetic: 90 us -> 75.7 us
  starting transfers between devices: 61.3 us -> 68.9 us
    concatenate x1, other arithmetic: 23.2 us -> 9.53 us  [local(): jnp.concatenate(qkv_parts, 0).reshape(dp * nz, shard_rows, -1)]
    ppermute x48 -> x52, starting transfers between devices: 59.1 us -> 66.9 us  [exchanged(): lax.ppermute(value, axis, [(i, i ^ bit) for i in range(lax.axis_size(axis...]
    ppermute x48 -> x52, waiting for transfers between devices: 257 us -> 254 us  [exchanged(): lax.ppermute(value, axis, [(i, i ^ bit) for i in range(lax.axis_size(axis...]
    unnamed x185 -> x165, local copies, waits for them, and re-layouts: 16.8 us -> 14.3 us
    pallas_call x2 -> x3, Pallas kernels: 17.7 us -> 18.6 us  [reorder_blocks(): pl.pallas_call(copy_kernel, grid_spec=pltpu.PrefetchScalarGridSpec(num_sc...]
  transfers between devices with their start and end apart: 61 -> 65, of which waited for: 32 -> 32; matrix products, arithmetic and copies ran while one was open for 35% -> 34% of each run, Pallas kernels for 13% -> 13%
where the time goes in v3:
time: 685 us; the launch traced here: 678 us
  waiting for transfers between devices  254 us (37%)
  matrix products  112 us (16%)
  Pallas kernels  88.7 us (13%)
  other arithmetic  75.7 us (11%)
  starting transfers between devices  68.9 us (10%)
  local copies, waits for them, and re-layouts  63.4 us (9%)
  between operations  16 us (2%)
    ppermute x52, waiting for transfers between devices, exchanged(): lax.ppermute(value, axis, [(i, i ^ bit) for i in range(lax.axis_size(axis...  254 us
    dot_general x41, matrix products, contract(): return jnp.einsum(spec, left, right, preferred_element_type=F32)  112 us
    ppermute x52, starting transfers between devices, exchanged(): lax.ppermute(value, axis, [(i, i ^ bit) for i in range(lax.axis_size(axis...  66.9 us
    pallas_call x1, Pallas kernels, attend_back(): pl.pallas_call(backward_kernel, grid_spec=pltpu.PrefetchScalarGridSpec(nu...  30.7 us
    concatenate x12, other arithmetic, doubled(): held = jnp.concatenate([held, exchanged(held, *bits[place])], place)  24.2 us
    pallas_call x1, Pallas kernels, reorder_weights(): pl.pallas_call(reorder_kernel, grid_spec=pltpu.PrefetchScalarGridSpec(num...  22.9 us
    pallas_call x3, Pallas kernels, reorder_blocks(): pl.pallas_call(copy_kernel, grid_spec=pltpu.PrefetchScalarGridSpec(num_sc...  18.6 us
    pallas_call x1, Pallas kernels, attend(): pl.pallas_call(forward_kernel, grid_spec=pltpu.PrefetchScalarGridSpec(num...  16.5 us
  transfers between devices with their start and end apart: 65, of which 32 were waited for; matrix products, arithmetic and copies ran while one was open for 34% of the time, Pallas kernels for 13%

profile of v3, /device:TPU:0, one launch (start us, length us, event | category | flops | bytes accessed | tf_op | source)
XLA Modules:
  0.0 678.0 jit_solution(3477536015943171797)
XLA Ops:
  8.3 4.1 collective-permute-start.1
  15.7 8.5 %collective-permute-done.1 = bf16[1,1,1,1,64,1088]{5,4,3,2,1,0:T(8,128)(2,1)S(1)} collective-permute-done((bf16[1,1,1,1,64,1088]{5,4,3,2,1,0:T(8,128)(2,1)S(1)}, bf16[1,1,1,1,64,1088]{5,4,3,2,1,0:T(8,128)(2,1)S(1)}, u32[]{:S(2)}, u32[]{:S(2)}) %collective-permute-start.1) | collective-permute-done | bytes 139296 | tf_op jit(solution)/shard_map/ppermute | solution.py:28
  29.4 4.9 collective-permute-done.2
  37.1 4.5 collective-permute-done.6
  44.1 5.4 collective-permute-done.3
  52.1 2.4 copy.67
  57.4 4.9 collective-permute-done.7
  62.3 2.5 pad_maximum_fusion.6
  69.7 16.3 %collective-permute-done.4 = bf16[2,1,2,2,64,1088]{5,4,3,2,1,0:T(8,128)(2,1)} collective-permute-done((bf16[2,1,2,2,64,1088]{5,4,3,2,1,0:T(8,128)(2,1)}, bf16[2,1,2,2,64,1088]{5,4,3,2,1,0:T(8,128)(2,1)}, u32[]{:S(2)}, u32[]{:S(2)}) %collective-permute-start.4) | collective-permute-done | bytes 1114144 | tf_op jit(solution)/shard_map/ppermute | solution.py:28
  87.8 8.7 %collective-permute-done.8 = bf16[1,2,2,2,80,1088]{5,4,3,2,1,0:T(8,128)(2,1)} collective-permute-done((bf16[1,2,2,2,80,1088]{5,4,3,2,1,0:T(8,128)(2,1)}, bf16[1,2,2,2,80,1088]{5,4,3,2,1,0:T(8,128)(2,1)}, u32[]{:S(2)}, u32[]{:S(2)}) %collective-permute-start.8) | collective-permute-done | bytes 1392672 | tf_op jit(solution)/shard_map/ppermute | solution.py:28
  96.5 3.1 pad_maximum_fusion.2
  99.7 2.9 collective-permute-start.11
  102.8 28.4 %collective-permute-done.11 = bf16[1,1,1,1,136,1088]{5,4,3,2,1,0:T(8,128)(2,1)S(1)} collective-permute-done((bf16[1,1,1,1,136,1088]{5,4,3,2,1,0:T(8,128)(2,1)S(1)}, bf16[1,1,1,1,136,1088]{5,4,3,2,1,0:T(8,128)(2,1)S(1)}, u32[]{:S(2)}, u32[]{:S(2)}) %collective-permute-start.11) | collective-permute-done | bytes 295968 | tf_op jit(solution)/shard_map/ppermute | solution.py:28
  136.5 11.4 %collective-permute-done.12 = bf16[1,1,2,1,136,1088]{5,4,3,2,1,0:T(8,128)(2,1)} collective-permute-done((bf16[1,1,2,1,136,1088]{5,4,3,2,1,0:T(8,128)(2,1)}, bf16[1,1,2,1,136,1088]{5,4,3,2,1,0:T(8,128)(2,1)}, u32[]{:S(2)}, u32[]{:S(2)}) %collective-permute-start.12) | collective-permute-done | bytes 591904 | tf_op jit(solution)/shard_map/ppermute | solution.py:28
  154.0 2.5 fusion.4
  158.8 21.3 %collective-permute-done.13 = bf16[1,1,2,2,136,1088]{5,4,3,2,1,0:T(8,128)(2,1)} collective-permute-done((bf16[1,1,2,2,136,1088]{5,4,3,2,1,0:T(8,128)(2,1)}, bf16[1,1,2,2,136,1088]{5,4,3,2,1,0:T(8,128)(2,1)}, u32[]{:S(2)}, u32[]{:S(2)}) %collective-permute-start.13) | collective-permute-done | bytes 1183776 | tf_op jit(solution)/shard_map/ppermute | solution.py:28
  180.0 3.3 pad_maximum_fusion.3
  184.8 22.9 %reorder_weights.1 = bf16[32,136,1088]{2,1,0:T(8,128)(2,1)} custom-call(s32[17]{0:T(128)S(1)} %pad_add_fusion.take_ref, bf16[16,64,1088]{2,1,0:T(8,128)(2,1)S(1)} %bitcast.176, bf16[16,80,1088]{2,1,0:T(8,128)(2,1)} %bitcast.9.high_mine, bf16[16,64,1088]{2,1,0:T(8,128)(2,1)} %collective-permute-done.9.low_other, ...), custom_call_target="tpu_custom_call" | custom-call | bytes 28409856 | tf_op jit(solution)/shard_map/reorder_weights/pallas_call | solution.py:93
  207.7 7.0 %slice.533 = bf16[4,1088,816]{2,1,0:T(8,128)(2,1)} slice(bf16[4,1088,1088]{2,1,0:T(8,128)(2,1)} %bitcast.189), slice={[0:4], [0:1088], [0:816]} | slice | bytes 14204928 | tf_op jit(solution)/shard_map/slice | solution.py:403
  214.7 11.3 %copy.77 = bf16[4,1088,816]{1,2,0:T(8,128)(2,1)} copy(bf16[4,1088,816]{2,1,0:T(8,128)(2,1)} %slice.533) | data formatting | bytes 14204928
  226.0 14.2 %add_convert_fusion.q_ref.k_ref.v_ref.q_own.k_own.v_own = bf16[3264,1024]{1,0:T(8,128)(2,1)} fusion(bf16[3264,1088]{1,0:T(8,128)(2,1)} %bitcast.217, bf16[1024,1088]{1,0:T(8,128)(2,1)S(1)} %bitcast.254, f32[3264]{0:T(1024)S(1)} %concatenate.149), kind=kOutput, calls=%fused_computation.2 | convolution fusion | flops 7279607808 | bytes 16028416 | tf_op jit(solution)/shard_map/cdn,rd->cnr/dot_general | solution.py:140
  240.2 16.5 %attend.1 = (bf16[1088,256]{1,0:T(8,128)(2,1)S(1)}, f32[17,1,256]{2,1,0:T(1,128)S(1)}) custom-call(s32[1]{0:T(128)} %bitcast.4.z_ref, bf16[3264,1024]{1,0:T(8,128)(2,1)} %add_convert_fusion.q_ref.k_ref.v_ref.q_own.k_own.v_own, bf16[3264,1024]{1,0:T(8,128)(2,1)} %add_convert_fusion.q_ref.k_ref.v_ref.q_own.k_own.v_own, ...), custom_call_target="tpu_custom_call" | custom-call | flops 1140850688 | bytes 4456448 | tf_op jit(solution)/shard_map/attend/pallas_call | solution.py:262
  274.0 6.3 pad_maximum_fusion
  280.3 8.8 %reorder_blocks.3 = bf16[16,136,1088]{2,1,0:T(8,128)(2,1)S(1)} custom-call(s32[16]{0:T(128)S(1)} %add.327.take_ref, bf16[16,136,1088]{2,1,0:T(8,128)(2,1)} %bitcast.234), custom_call_target="tpu_custom_call" | custom-call | bytes 9469952 | tf_op jit(solution)/shard_map/reorder_blocks/pallas_call | solution.py:114
  289.2 3.4 convolution_add_fusion.3
  292.7 3.4 convolution_add_fusion.2
  296.1 3.2 convolution_convert_fusion.1
  299.4 3.9 convert_reduce_fusion.2
  303.3 3.3 convert_reduce_fusion.3
  306.6 5.1 fusion.104
  311.7 2.9 convolution_convert_fusion
  315.7 6.5 fusion.119
  324.2 7.8 %fusion = bf16[2176,1088]{0,1:T(8,128)(2,1)} fusion(f32[2176,1088]{0,1:T(8,128)} %fusion.119, bf16[256,1088]{0,1:T(8,128)(2,1)} %collective-permute-done.15, bf16[256,2176]{1,0:T(8,128)(2,1)} %copy-done.55), kind=kOutput, calls=%fused_computation.3 | convolution fusion | flops 1216888832 | bytes 15876096 | tf_op jit(solution)/shard_map/rn,rd->nd/dot_general | solution.py:140
  332.0 8.3 %copy.74 = bf16[2176,1088]{1,0:T(8,128)(2,1)} copy(bf16[2176,1088]{0,1:T(8,128)(2,1)} %fusion) | data formatting | bytes 9469952 | tf_op jit(solution)/shard_map/convert_element_type | solution.py:47
  340.3 3.6 slice.613
  345.8 5.4 fusion.1
  352.2 4.1 fusion.110
  356.3 6.7 copy.75
  363.0 5.5 copy.76
  369.1 5.4 multiply_reduce_fusion
  382.3 2.9 convert_multiply_fusion
  393.6 5.8 fusion.11
  402.6 12.3 %collective-permute-done.47 = f32[4,1088]{1,0:T(4,128)S(1)} collective-permute-done((f32[4,1088]{1,0:T(4,128)S(1)}, f32[4,1088]{1,0:T(4,128)S(1)}, u32[]{:S(2)}, u32[]{:S(2)}) %collective-permute-start.47) | collective-permute-done | bytes 17440 | tf_op jit(solution)/shard_map/ppermute | solution.py:28
  422.0 3.4 concatenate.171
  433.2 16.5 %collective-permute-done.49 = f32[4,1088]{1,0:T(4,128)S(1)} collective-permute-done((f32[4,1088]{1,0:T(4,128)S(1)}, f32[4,1088]{1,0:T(4,128)S(1)}, u32[]{:S(2)}, u32[]{:S(2)}) %collective-permute-start.49) | collective-permute-done | bytes 17440 | tf_op jit(solution)/shard_map/ppermute | solution.py:28
  460.6 6.8 %collective-permute-done.43 = bf16[1,1,2,2,136,272]{5,4,3,2,1,0:T(8,128)(2,1)S(1)} collective-permute-done((bf16[1,1,2,2,136,272]{5,4,3,2,1,0:T(8,128)(2,1)S(1)}, bf16[1,1,2,2,136,272]{5,4,3,2,1,0:T(8,128)(2,1)S(1)}, u32[]{:S(2)}, u32[]{:S(2)}) %collective-permute-start.43) | collective-permute-done | bytes 295968 | tf_op jit(solution)/shard_map/ppermute | solution.py:28
  469.4 20.7 %collective-permute-done.44 = bf16[1,1,2,1,136,272]{5,4,3,2,1,0:T(8,128)(2,1)S(1)} collective-permute-done((bf16[1,1,2,1,136,272]{5,4,3,2,1,0:T(8,128)(2,1)S(1)}, bf16[1,1,2,1,136,272]{5,4,3,2,1,0:T(8,128)(2,1)S(1)}, u32[]{:S(2)}, u32[]{:S(2)}) %collective-permute-start.44) | collective-permute-done | bytes 148000 | tf_op jit(solution)/shard_map/ppermute | solution.py:28
  490.1 2.5 collective-permute-start.45
  493.5 4.1 collective-permute-done.45
  499.8 30.7 %attend_back.1 = bf16[3,1088,256]{2,1,0:T(8,128)(2,1)S(1)} custom-call(s32[1]{0:T(128)} %bitcast.4.z_ref, bf16[3264,1024]{1,0:T(8,128)(2,1)} %add_convert_fusion.q_ref.k_ref.v_ref.q_own.k_own.v_own, bf16[3264,1024]{1,0:T(8,128)(2,1)} %add_convert_fusion.q_ref.k_ref.v_ref.q_own.k_own.v_own, ...), custom_call_target="tpu_custom_call" | custom-call | flops 2281701376 | bytes 8912896 | tf_op jit(solution)/shard_map/attend_back/pallas_call | solution.py:293
  545.5 3.5 collective-permute-done.27
  550.0 2.8 collective-permute-done.28
  554.0 2.6 collective-permute-done.29
  557.2 3.2 collective-permute-done.30
  561.1 2.7 add_convert_fusion.2
  566.7 23.5 %collective-permute-done.52 = bf16[1,1,2,2,136,1088]{5,4,3,2,1,0:T(8,128)(2,1)S(1)} collective-permute-done((bf16[1,1,2,2,136,1088]{5,4,3,2,1,0:T(8,128)(2,1)S(1)}, bf16[1,1,2,2,136,1088]{5,4,3,2,1,0:T(8,128)(2,1)S(1)}, u32[]{:S(2)}, u32[]{:S(2)}) %collective-permute-start.52) | collective-permute-done | bytes 1183776 | tf_op jit(solution)/shard_map/ppermute | solution.py:28
  595.1 9.5 %pad_maximum_fusion.1 = bf16[2176,816]{1,0:T(8,128)(2,1)} fusion(bf16[544,816]{1,0:T(8,128)(2,1)S(1)} %add_convert_fusion.6, bf16[544,816]{1,0:T(8,128)(2,1)S(1)} %add_convert_fusion.7, bf16[544,816]{1,0:T(8,128)(2,1)S(1)} %add_convert_fusion.8, bf16[544,816]{1,0:T(8,128)(2,1)S(1)} %add_convert_fusion.9), kind=kLoop, calls=%fused_computation.18 | loop fusion | flops 14204928 | bytes 7102464 | tf_op jit(solution)/shard_map/concatenate | solution.py:493
  604.6 8.7 %reorder_blocks.4 = bf16[16,136,816]{2,1,0:T(8,128)(2,1)S(1)} custom-call(s32[16]{0:T(128)S(1)} %add.327.take_ref, bf16[16,136,816]{2,1,0:T(8,128)(2,1)} %bitcast.214), custom_call_target="tpu_custom_call" | custom-call | bytes 7102464 | tf_op jit(solution)/shard_map/reorder_blocks/pallas_call | solution.py:114
  619.4 17.9 %collective-permute-done.54 = bf16[1,1,1,1,136,1088]{5,4,3,2,1,0:T(8,128)(2,1)S(1)} collective-permute-done((bf16[1,1,1,1,136,1088]{5,4,3,2,1,0:T(8,128)(2,1)S(1)}, bf16[1,1,1,1,136,1088]{5,4,3,2,1,0:T(8,128)(2,1)S(1)}, u32[]{:S(2)}, u32[]{:S(2)}) %collective-permute-start.54) | collective-permute-done | bytes 295968 | tf_op jit(solution)/shard_map/ppermute | solution.py:28
  639.4 2.5 collective-permute-start.37
  643.0 4.6 collective-permute-done.33
  651.8 5.8 collective-permute-done.34
  660.7 3.1 collective-permute-start.39
  663.9 4.8 collective-permute-done.35
  (448 shorter events, 160.4 us)
Async XLA Ops:
  7.2 144.5 %all-gather.5.cloned.1.call-start = ((), (), s32[]{:S(2)}) async-start(), calls=%async_computation | async-start | bytes 3041280 | tf_op jit(solution)/shard_map/all_gather | solution.py:377
  8.3 15.9 %collective-permute-start.1 = (bf16[1,1,1,1,64,1088]{5,4,3,2,1,0:T(8,128)(2,1)S(1)}, bf16[1,1,1,1,64,1088]{5,4,3,2,1,0:T(8,128)(2,1)S(1)}, u32[]{:S(2)}, u32[]{:S(2)}) collective-permute-start(bf16[1,1,1,1,64,1088]{5,4,3,2,1,0:T(8,128)(2,1)S(1)} %fusion.76), channel_id=1, source_target_pairs={{0,4},{2,6},{4,0},{6,2},{1,5},{3,7},{5,1},{7,3},{8,12},{10,14},{12... | collective-permute-start | bytes 417800 | tf_op jit(solution)/shard_map/ppermute | solution.py:28
  14.2 13.2 %collective-permute-start.5 = (bf16[1,1,1,1,80,1088]{5,4,3,2,1,0:T(8,128)(2,1)S(1)}, bf16[1,1,1,1,80,1088]{5,4,3,2,1,0:T(8,128)(2,1)S(1)}, u32[]{:S(2)}, u32[]{:S(2)}) collective-permute-start(bf16[1,1,1,1,80,1088]{5,4,3,2,1,0:T(8,128)(2,1)S(1)} %fusion.73), channel_id=1, source_target_pairs={{0,4},{2,6},{4,0},{6,2},{1,5},{3,7},{5,1},{7,3},{8,12},{10,14},{12... | collective-permute-start | bytes 522248 | tf_op jit(solution)/shard_map/ppermute | solution.py:28
  24.3 10.0 %collective-permute-start.2 = (bf16[1,1,2,1,64,1088]{5,4,3,2,1,0:T(8,128)(2,1)S(1)}, bf16[1,1,2,1,64,1088]{5,4,3,2,1,0:T(8,128)(2,1)S(1)}, u32[]{:S(2)}, u32[]{:S(2)}) collective-permute-start(bf16[1,1,2,1,64,1088]{5,4,3,2,1,0:T(8,128)(2,1)S(1)} %pad_maximum_fusion.23), channel_id=1, source_target_pairs={{0,2},{2,0},{4,6},{6,4},{1,3},{3,1},{5,7},{7,5},{8,10},{10,8},{12,... | collective-permute-start | bytes 835592 | tf_op jit(solution)/shard_map/ppermute | solution.py:28
  26.5 25.5 %collective-permute-start = (bf16[520,1088]{1,0:T(8,128)(2,1)}, bf16[520,1088]{1,0:T(8,128)(2,1)}, u32[]{:S(2)}, u32[]{:S(2)}) collective-permute-start(bf16[520,1088]{1,0:T(8,128)(2,1)} %copy.66), channel_id=1, source_target_pairs={{0,1},{1,0},{2,3},{3,2},{4,5},{5,4},{6,7},{7,6},{8,9},{9,8},{10,11... | collective-permute-start | bytes 3394568 | tf_op jit(solution)/shard_map/ppermute | solution.py:24
  28.2 13.3 %collective-permute-start.6 = (bf16[1,1,2,1,80,1088]{5,4,3,2,1,0:T(8,128)(2,1)}, bf16[1,1,2,1,80,1088]{5,4,3,2,1,0:T(8,128)(2,1)S(1)}, u32[]{:S(2)}, u32[]{:S(2)}) collective-permute-start(bf16[1,1,2,1,80,1088]{5,4,3,2,1,0:T(8,128)(2,1)} %pad_maximum_fusion.22), channel_id=1, source_target_pairs={{0,2},{2,0},{4,6},{6,4},{1,3},{3,1},{5,7},{7,5},{8,10},{10,8},{12,... | collective-permute-start | bytes 1044488 | tf_op jit(solution)/shard_map/ppermute | solution.py:28
  35.2 14.3 %collective-permute-start.3 = (bf16[1,1,2,2,64,1088]{5,4,3,2,1,0:T(8,128)(2,1)}, bf16[1,1,2,2,64,1088]{5,4,3,2,1,0:T(8,128)(2,1)S(1)}, u32[]{:S(2)}, u32[]{:S(2)}) collective-permute-start(bf16[1,1,2,2,64,1088]{5,4,3,2,1,0:T(8,128)(2,1)} %pad_maximum_fusion.12), channel_id=1, source_target_pairs={{0,16},{8,24},{16,0},{24,8},{1,17},{9,25},{17,1},{25,9},{2,18},{10... | collective-permute-start | bytes 1671176 | tf_op jit(solution)/shard_map/ppermute | solution.py:28
  42.6 19.7 %collective-permute-start.7 = (bf16[1,1,2,2,80,1088]{5,4,3,2,1,0:T(8,128)(2,1)}, bf16[1,1,2,2,80,1088]{5,4,3,2,1,0:T(8,128)(2,1)}, u32[]{:S(2)}, u32[]{:S(2)}) collective-permute-start(bf16[1,1,2,2,80,1088]{5,4,3,2,1,0:T(8,128)(2,1)} %pad_maximum_fusion.10), channel_id=1, source_target_pairs={{0,8},{8,0},{16,24},{24,16},{1,9},{9,1},{17,25},{25,17},{2,10},{10... | collective-permute-start | bytes 2088968 | tf_op jit(solution)/shard_map/ppermute | solution.py:28
  50.8 35.2 %collective-permute-start.4 = (bf16[2,1,2,2,64,1088]{5,4,3,2,1,0:T(8,128)(2,1)}, bf16[2,1,2,2,64,1088]{5,4,3,2,1,0:T(8,128)(2,1)}, u32[]{:S(2)}, u32[]{:S(2)}) collective-permute-start(bf16[2,1,2,2,64,1088]{5,4,3,2,1,0:T(8,128)(2,1)} %pad_maximum_fusion.8), channel_id=1, source_target_pairs={{0,8},{8,0},{16,24},{24,16},{1,9},{9,1},{17,25},{25,17},{2,10},{10... | collective-permute-start | bytes 3342344 | tf_op jit(solution)/shard_map/ppermute | solution.py:28
  64.9 31.6 %collective-permute-start.8 = (bf16[1,2,2,2,80,1088]{5,4,3,2,1,0:T(8,128)(2,1)}, bf16[1,2,2,2,80,1088]{5,4,3,2,1,0:T(8,128)(2,1)}, u32[]{:S(2)}, u32[]{:S(2)}) collective-permute-start(bf16[1,2,2,2,80,1088]{5,4,3,2,1,0:T(8,128)(2,1)} %pad_maximum_fusion.6), channel_id=1, source_target_pairs={{0,16},{8,24},{16,0},{24,8},{1,17},{9,25},{17,1},{25,9},{2,18},{10... | collective-permute-start | bytes 4177928 | tf_op jit(solution)/shard_map/ppermute | solution.py:28
  67.8 212.6 %all-gather.7.cloned.1.call-start = ((), (), s32[]{:S(2)}) async-start(), calls=%async_computation.1 | async-start | bytes 5326848 | tf_op jit(solution)/shard_map/all_gather | solution.py:391
  99.7 31.5 %collective-permute-start.11 = (bf16[1,1,1,1,136,1088]{5,4,3,2,1,0:T(8,128)(2,1)S(1)}, bf16[1,1,1,1,136,1088]{5,4,3,2,1,0:T(8,128)(2,1)S(1)}, u32[]{:S(2)}, u32[]{:S(2)}) collective-permute-start(bf16[1,1,1,1,136,1088]{5,4,3,2,1,0:T(8,128)(2,1)S(1)} %bitcast.241), channel_id=1, source_target_pairs={{0,4},{2,6},{4,0},{6,2},{1,5},{3,7},{5,1},{7,3},{8,12},{10,14},{12... | collective-permute-start | bytes 887816 | tf_op jit(solution)/shard_map/ppermute | solution.py:28
  132.8 15.0 %collective-permute-start.12 = (bf16[1,1,2,1,136,1088]{5,4,3,2,1,0:T(8,128)(2,1)}, bf16[1,1,2,1,136,1088]{5,4,3,2,1,0:T(8,128)(2,1)}, u32[]{:S(2)}, u32[]{:S(2)}) collective-permute-start(bf16[1,1,2,1,136,1088]{5,4,3,2,1,0:T(8,128)(2,1)} %pad_maximum_fusion.11), channel_id=1, source_target_pairs={{0,2},{2,0},{4,6},{6,4},{1,3},{3,1},{5,7},{7,5},{8,10},{10,8},{12,... | collective-permute-start | bytes 1775624 | tf_op jit(solution)/shard_map/ppermute | solution.py:28
  135.0 49.8 %collective-permute-start.9 = (bf16[16,64,1088]{2,1,0:T(8,128)(2,1)S(1)}, bf16[16,64,1088]{2,1,0:T(8,128)(2,1)}, u32[]{:S(2)}, u32[]{:S(2)}) collective-permute-start(bf16[16,64,1088]{2,1,0:T(8,128)(2,1)S(1)} %bitcast.175), channel_id=1, source_target_pairs={{0,1},{1,0},{2,3},{3,2},{4,5},{5,4},{6,7},{7,6},{8,9},{9,8},{10,11... | collective-permute-start | bytes 6684680 | tf_op jit(solution)/shard_map/ppermute | solution.py:24
  135.0 49.8 %collective-permute-start.10 = (bf16[16,80,1088]{2,1,0:T(8,128)(2,1)}, bf16[16,80,1088]{2,1,0:T(8,128)(2,1)}, u32[]{:S(2)}, u32[]{:S(2)}) collective-permute-start(bf16[16,80,1088]{2,1,0:T(8,128)(2,1)} %bitcast.9.high_mine), channel_id=1, source_target_pairs={{0,1},{1,0},{2,3},{3,2},{4,5},{5,4},{6,7},{7,6},{8,9},{9,8},{10,11... | collective-permute-start | bytes 8355848 | tf_op jit(solution)/shard_map/ppermute | solution.py:24
  150.2 29.8 %collective-permute-start.13 = (bf16[1,1,2,2,136,1088]{5,4,3,2,1,0:T(8,128)(2,1)}, bf16[1,1,2,2,136,1088]{5,4,3,2,1,0:T(8,128)(2,1)}, u32[]{:S(2)}, u32[]{:S(2)}) collective-permute-start(bf16[1,1,2,2,136,1088]{5,4,3,2,1,0:T(8,128)(2,1)} %pad_maximum_fusion.7), channel_id=1, source_target_pairs={{0,8},{8,0},{16,24},{24,16},{1,9},{9,1},{17,25},{25,17},{2,10},{10... | collective-permute-start | bytes 3551240 | tf_op jit(solution)/shard_map/ppermute | solution.py:28
  183.3 90.7 %collective-permute-start.14 = (bf16[1,2,2,2,136,1088]{5,4,3,2,1,0:T(8,128)(2,1)}, bf16[1,2,2,2,136,1088]{5,4,3,2,1,0:T(8,128)(2,1)}, u32[]{:S(2)}, u32[]{:S(2)}) collective-permute-start(bf16[1,2,2,2,136,1088]{5,4,3,2,1,0:T(8,128)(2,1)} %pad_maximum_fusion.3), channel_id=1, source_target_pairs={{0,16},{8,24},{16,0},{24,8},{1,17},{9,25},{17,1},{25,9},{2,18},{10... | collective-permute-start | bytes 7102472 | tf_op jit(solution)/shard_map/ppermute | solution.py:28
  256.7 12.5 %collective-permute-start.21 = (f32[1,1,17,1,256]{4,3,2,1,0:T(1,128)S(1)}, f32[1,1,17,1,256]{4,3,2,1,0:T(1,128)S(1)}, u32[]{:S(2)}, u32[]{:S(2)}) collective-permute-start(f32[1,1,17,1,256]{4,3,2,1,0:T(1,128)S(1)} %bitcast.186), channel_id=1, source_target_pairs={{0,4},{2,6},{4,0},{6,2},{1,5},{3,7},{5,1},{7,3},{8,12},{10,14},{12... | collective-permute-start | bytes 52232 | tf_op jit(solution)/shard_map/ppermute | solution.py:28
  258.4 14.8 %collective-permute-start.40 = (bf16[1088,256]{1,0:T(8,128)(2,1)S(1)}, bf16[1088,256]{1,0:T(8,128)(2,1)S(1)}, u32[]{:S(2)}, u32[]{:S(2)}) collective-permute-start(bf16[1088,256]{1,0:T(8,128)(2,1)S(1)} %get-tuple-element.25), channel_id=1, source_target_pairs={{0,1},{1,0},{2,3},{3,2},{4,5},{5,4},{6,7},{7,6},{8,9},{9,8},{10,11... | collective-permute-start | bytes 1671176 | tf_op jit(solution)/shard_map/ppermute | solution.py:24
  268.6 24.0 %collective-permute-start.15 = (bf16[256,1088]{0,1:T(8,128)(2,1)}, bf16[256,1088]{0,1:T(8,128)(2,1)}, u32[]{:S(2)}, u32[]{:S(2)}) collective-permute-start(bf16[256,1088]{0,1:T(8,128)(2,1)} %add_convert_fusion.15), channel_id=1, source_target_pairs={{0,1},{1,0},{2,3},{3,2},{4,5},{5,4},{6,7},{7,6},{8,9},{9,8},{10,11... | collective-permute-start | bytes 1671176 | tf_op jit(solution)/shard_map/ppermute | solution.py:24
  269.2 4.0 collective-permute-start.22
  311.7 81.7 %collective-permute-start.16 = (bf16[256,1088]{0,1:T(8,128)(2,1)}, bf16[256,1088]{0,1:T(8,128)(2,1)}, u32[]{:S(2)}, u32[]{:S(2)}) collective-permute-start(bf16[256,1088]{0,1:T(8,128)(2,1)} %convolution_convert_fusion.1), channel_id=1, source_target_pairs={{0,1},{1,0},{2,3},{3,2},{4,5},{5,4},{6,7},{7,6},{8,9},{9,8},{10,11... | collective-permute-start | bytes 1671176 | tf_op jit(solution)/shard_map/ppermute | solution.py:24
  314.7 54.4 %collective-permute-start.18 = (bf16[256,1088]{0,1:T(8,128)(2,1)}, bf16[256,1088]{0,1:T(8,128)(2,1)}, u32[]{:S(2)}, u32[]{:S(2)}) collective-permute-start(bf16[256,1088]{0,1:T(8,128)(2,1)} %convolution_convert_fusion), channel_id=1, source_target_pairs={{0,1},{1,0},{2,3},{3,2},{4,5},{5,4},{6,7},{7,6},{8,9},{9,8},{10,11... | collective-permute-start | bytes 1671176 | tf_op jit(solution)/shard_map/ppermute | solution.py:24
  315.3 6.9 %collective-permute-start.55 = (f32[2,4,136]{2,1,0:T(4,128)S(1)}, f32[2,4,136]{2,1,0:T(4,128)S(1)}, u32[]{:S(2)}, u32[]{:S(2)}) collective-permute-start(f32[2,4,136]{2,1,0:T(4,128)S(1)} %slice.510), channel_id=1, source_target_pairs={{0,16},{8,24},{16,0},{24,8},{1,17},{9,25},{17,1},{25,9},{2,18},{10... | collective-permute-start | bytes 13064 | tf_op jit(solution)/shard_map/ppermute | solution.py:28
  322.3 21.8 %collective-permute-start.56 = (f32[1,4,136]{2,1,0:T(4,128)S(1)}, f32[1,4,136]{2,1,0:T(4,128)S(1)}, u32[]{:S(2)}, u32[]{:S(2)}) collective-permute-start(f32[1,4,136]{2,1,0:T(4,128)S(1)} %slice.623), channel_id=1, source_target_pairs={{0,8},{8,0},{16,24},{24,16},{1,9},{9,1},{17,25},{25,17},{2,10},{10... | collective-permute-start | bytes 6536 | tf_op jit(solution)/shard_map/ppermute | solution.py:28
  343.9 217.2 %collective-permute-start.51 = (bf16[2,1,2,2,136,1088]{5,4,3,2,1,0:T(8,128)(2,1)}, bf16[2,1,2,2,136,1088]{5,4,3,2,1,0:T(8,128)(2,1)}, u32[]{:S(2)}, u32[]{:S(2)}) collective-permute-start(bf16[2,1,2,2,136,1088]{5,4,3,2,1,0:T(8,128)(2,1)} %slice.613), channel_id=1, source_target_pairs={{0,8},{8,0},{16,24},{24,16},{1,9},{9,1},{17,25},{25,17},{2,10},{10... | collective-permute-start | bytes 7102472 | tf_op jit(solution)/shard_map/ppermute | solution.py:28
  344.1 7.1 %collective-permute-start.57 = (f32[1,2,136]{2,1,0:T(2,128)S(1)}, f32[1,2,136]{2,1,0:T(2,128)S(1)}, u32[]{:S(2)}, u32[]{:S(2)}) collective-permute-start(f32[1,2,136]{2,1,0:T(2,128)S(1)} %slice.625), channel_id=1, source_target_pairs={{0,4},{2,6},{4,0},{6,2},{1,5},{3,7},{5,1},{7,3},{8,12},{10,14},{12... | collective-permute-start | bytes 3272 | tf_op jit(solution)/shard_map/ppermute | solution.py:28
  351.2 17.3 %collective-permute-start.58 = (f32[1,1,136]{2,1,0:T(1,128)S(1)}, f32[1,1,136]{2,1,0:T(1,128)S(1)}, u32[]{:S(2)}, u32[]{:S(2)}) collective-permute-start(f32[1,1,136]{2,1,0:T(1,128)S(1)} %slice.627), channel_id=1, source_target_pairs={{0,2},{2,0},{4,6},{6,4},{1,3},{3,1},{5,7},{7,5},{8,10},{10,8},{12,... | collective-permute-start | bytes 1640 | tf_op jit(solution)/shard_map/ppermute | solution.py:28
  378.9 36.1 %collective-permute-start.41 = (bf16[256,1088]{0,1:T(8,128)(2,1)}, bf16[256,1088]{0,1:T(8,128)(2,1)}, u32[]{:S(2)}, u32[]{:S(2)}) collective-permute-start(bf16[256,1088]{0,1:T(8,128)(2,1)} %get-tuple-element.50), channel_id=1, source_target_pairs={{0,1},{1,0},{2,3},{3,2},{4,5},{5,4},{6,7},{7,6},{8,9},{9,8},{10,11... | collective-permute-start | bytes 1671176 | tf_op jit(solution)/shard_map/ppermute | solution.py:24
  385.2 72.2 %collective-permute-start.19 = (bf16[1,1,1088,256]{3,2,1,0:T(8,128)(2,1)}, bf16[1,1,1088,256]{3,2,1,0:T(8,128)(2,1)}, u32[]{:S(2)}, u32[]{:S(2)}) collective-permute-start(bf16[1,1,1088,256]{3,2,1,0:T(8,128)(2,1)} %bitcast.26), channel_id=1, source_target_pairs={{0,4},{2,6},{4,0},{6,2},{1,5},{3,7},{5,1},{7,3},{8,12},{10,14},{12... | collective-permute-start | bytes 1671176 | tf_op jit(solution)/shard_map/ppermute | solution.py:28
  388.5 41.9 %collective-permute-start.23 = (f32[1,1,17,1,256]{4,3,2,1,0:T(1,128)S(1)}, f32[1,1,17,1,256]{4,3,2,1,0:T(1,128)S(1)}, u32[]{:S(2)}, u32[]{:S(2)}) collective-permute-start(f32[1,1,17,1,256]{4,3,2,1,0:T(1,128)S(1)} %reshape_broadcast_in_dim.3), channel_id=1, source_target_pairs={{0,4},{2,6},{4,0},{6,2},{1,5},{3,7},{5,1},{7,3},{8,12},{10,14},{12... | collective-permute-start | bytes 52232 | tf_op jit(solution)/shard_map/ppermute | solution.py:28
  393.5 7.1 %collective-permute-start.46 = (f32[4,1088]{1,0:T(4,128)S(1)}, f32[4,1088]{1,0:T(4,128)S(1)}, u32[]{:S(2)}, u32[]{:S(2)}) collective-permute-start(f32[4,1088]{1,0:T(4,128)S(1)} %pad_maximum_fusion.28), channel_id=1, source_target_pairs={{0,1},{1,0},{2,3},{3,2},{4,5},{5,4},{6,7},{7,6},{8,9},{9,8},{10,11... | collective-permute-start | bytes 52232 | tf_op jit(solution)/shard_map/ppermute | solution.py:28
  400.6 14.2 %collective-permute-start.47 = (f32[4,1088]{1,0:T(4,128)S(1)}, f32[4,1088]{1,0:T(4,128)S(1)}, u32[]{:S(2)}, u32[]{:S(2)}) collective-permute-start(f32[4,1088]{1,0:T(4,128)S(1)} %fusion.101), channel_id=1, source_target_pairs={{0,4},{2,6},{4,0},{6,2},{1,5},{3,7},{5,1},{7,3},{8,12},{10,14},{12... | collective-permute-start | bytes 52232 | tf_op jit(solution)/shard_map/ppermute | solution.py:28
  414.9 17.6 %collective-permute-start.48 = (f32[4,1088]{1,0:T(4,128)S(1)}, f32[4,1088]{1,0:T(4,128)S(1)}, u32[]{:S(2)}, u32[]{:S(2)}) collective-permute-start(f32[4,1088]{1,0:T(4,128)S(1)} %fusion.160), channel_id=1, source_target_pairs={{0,2},{2,0},{4,6},{6,4},{1,3},{3,1},{5,7},{7,5},{8,10},{10,8},{12,... | collective-permute-start | bytes 52232 | tf_op jit(solution)/shard_map/ppermute | solution.py:28
  428.9 26.1 %collective-permute-start.42 = (bf16[1,2,2,2,136,272]{5,4,3,2,1,0:T(8,128)(2,1)S(1)}, bf16[1,2,2,2,136,272]{5,4,3,2,1,0:T(8,128)(2,1)S(1)}, u32[]{:S(2)}, u32[]{:S(2)}) collective-permute-start(bf16[1,2,2,2,136,272]{5,4,3,2,1,0:T(8,128)(2,1)S(1)} %bitcast.256), channel_id=1, source_target_pairs={{0,16},{8,24},{16,0},{24,8},{1,17},{9,25},{17,1},{25,9},{2,18},{10... | collective-permute-start | bytes 1775624 | tf_op jit(solution)/shard_map/ppermute | solution.py:28
  430.4 20.7 %collective-permute-start.24 = (f32[2,1,17,1,256]{4,3,2,1,0:T(1,128)S(1)}, f32[2,1,17,1,256]{4,3,2,1,0:T(1,128)S(1)}, u32[]{:S(2)}, u32[]{:S(2)}) collective-permute-start(f32[2,1,17,1,256]{4,3,2,1,0:T(1,128)S(1)} %constant_dynamic-update-slice_fusion), channel_id=1, source_target_pairs={{0,2},{2,0},{4,6},{6,4},{1,3},{3,1},{5,7},{7,5},{8,10},{10,8},{12,... | collective-permute-start | bytes 104456 | tf_op jit(solution)/shard_map/ppermute | solution.py:28
  432.5 17.2 %collective-permute-start.49 = (f32[4,1088]{1,0:T(4,128)S(1)}, f32[4,1088]{1,0:T(4,128)S(1)}, u32[]{:S(2)}, u32[]{:S(2)}) collective-permute-start(f32[4,1088]{1,0:T(4,128)S(1)} %add.393), channel_id=1, source_target_pairs={{0,16},{8,24},{16,0},{24,8},{1,17},{9,25},{17,1},{25,9},{2,18},{10... | collective-permute-start | bytes 52232 | tf_op jit(solution)/shard_map/ppermute | solution.py:28
  449.7 114.9 %collective-permute-start.59 = (bf16[1,2,2,2,136,1088]{5,4,3,2,1,0:T(8,128)(2,1)S(1)}, bf16[1,2,2,2,136,1088]{5,4,3,2,1,0:T(8,128)(2,1)S(1)}, u32[]{:S(2)}, u32[]{:S(2)}) collective-permute-start(bf16[1,2,2,2,136,1088]{5,4,3,2,1,0:T(8,128)(2,1)S(1)} %bitcast.253), channel_id=1, source_target_pairs={{0,16},{8,24},{16,0},{24,8},{1,17},{9,25},{17,1},{25,9},{2,18},{10... | collective-permute-start | bytes 7102472 | tf_op jit(solution)/shard_map/ppermute | solution.py:28
  451.2 3.8 collective-permute-start.50
  455.0 14.4 %collective-permute-start.17 = (bf16[128,1088]{0,1:T(8,128)(2,1)S(1)}, bf16[128,1088]{0,1:T(8,128)(2,1)S(1)}, u32[]{:S(2)}, u32[]{:S(2)}) collective-permute-start(bf16[128,1088]{0,1:T(8,128)(2,1)S(1)} %broadcast_select_fusion.8), channel_id=1, source_target_pairs={{0,1},{1,0},{2,3},{3,2},{4,5},{5,4},{6,7},{7,6},{8,9},{9,8},{10,11... | collective-permute-start | bytes 835592 | tf_op jit(solution)/shard_map/ppermute | solution.py:24
  455.3 12.1 %collective-permute-start.43 = (bf16[1,1,2,2,136,272]{5,4,3,2,1,0:T(8,128)(2,1)S(1)}, bf16[1,1,2,2,136,272]{5,4,3,2,1,0:T(8,128)(2,1)S(1)}, u32[]{:S(2)}, u32[]{:S(2)}) collective-permute-start(bf16[1,1,2,2,136,272]{5,4,3,2,1,0:T(8,128)(2,1)S(1)} %slice.604), channel_id=1, source_target_pairs={{0,8},{8,0},{16,24},{24,16},{1,9},{9,1},{17,25},{25,17},{2,10},{10... | collective-permute-start | bytes 887816 | tf_op jit(solution)/shard_map/ppermute | solution.py:28
  458.8 39.5 %collective-permute-start.20 = (bf16[2,1,1088,256]{3,2,1,0:T(8,128)(2,1)S(1)}, bf16[2,1,1088,256]{3,2,1,0:T(8,128)(2,1)S(1)}, u32[]{:S(2)}, u32[]{:S(2)}) collective-permute-start(bf16[2,1,1088,256]{3,2,1,0:T(8,128)(2,1)S(1)} %pad_maximum_fusion.9), channel_id=1, source_target_pairs={{0,2},{2,0},{4,6},{6,4},{1,3},{3,1},{5,7},{7,5},{8,10},{10,8},{12,... | collective-permute-start | bytes 3342344 | tf_op jit(solution)/shard_map/ppermute | solution.py:28
  467.5 22.5 %collective-permute-start.44 = (bf16[1,1,2,1,136,272]{5,4,3,2,1,0:T(8,128)(2,1)S(1)}, bf16[1,1,2,1,136,272]{5,4,3,2,1,0:T(8,128)(2,1)S(1)}, u32[]{:S(2)}, u32[]{:S(2)}) collective-permute-start(bf16[1,1,2,1,136,272]{5,4,3,2,1,0:T(8,128)(2,1)S(1)} %slice.606), channel_id=1, source_target_pairs={{0,2},{2,0},{4,6},{6,4},{1,3},{3,1},{5,7},{7,5},{8,10},{10,8},{12,... | collective-permute-start | bytes 443912 | tf_op jit(solution)/shard_map/ppermute | solution.py:28
  490.1 7.5 %collective-permute-start.45 = (bf16[1,1,1,1,136,272]{5,4,3,2,1,0:T(8,128)(2,1)S(1)}, bf16[1,1,1,1,136,272]{5,4,3,2,1,0:T(8,128)(2,1)S(1)}, u32[]{:S(2)}, u32[]{:S(2)}) collective-permute-start(bf16[1,1,1,1,136,272]{5,4,3,2,1,0:T(8,128)(2,1)S(1)} %slice.608), channel_id=1, source_target_pairs={{0,4},{2,6},{4,0},{6,2},{1,5},{3,7},{5,1},{7,3},{8,12},{10,14},{12... | collective-permute-start | bytes 221960 | tf_op jit(solution)/shard_map/ppermute | solution.py:28
  533.3 59.8 %collective-permute-start.31 = (bf16[3264,256]{1,0:T(8,128)(2,1)S(1)}, bf16[3264,256]{1,0:T(8,128)(2,1)S(1)}, u32[]{:S(2)}, u32[]{:S(2)}) collective-permute-start(bf16[3264,256]{1,0:T(8,128)(2,1)S(1)} %bitcast.167), channel_id=1, source_target_pairs={{0,1},{1,0},{2,3},{3,2},{4,5},{5,4},{6,7},{7,6},{8,9},{9,8},{10,11... | collective-permute-start | bytes 5013512 | tf_op jit(solution)/shard_map/ppermute | solution.py:24
  544.0 5.0 collective-permute-start.27
  549.0 3.8 collective-permute-start.28
  552.9 3.8 collective-permute-start.29
  554.0 11.8 %collective-permute-start.25 = (bf16[128,1088]{0,1:T(8,128)(2,1)S(1)}, bf16[128,1088]{0,1:T(8,128)(2,1)S(1)}, u32[]{:S(2)}, u32[]{:S(2)}) collective-permute-start(bf16[128,1088]{0,1:T(8,128)(2,1)S(1)} %broadcast_select_fusion.6), channel_id=1, source_target_pairs={{0,1},{1,0},{2,3},{3,2},{4,5},{5,4},{6,7},{7,6},{8,9},{9,8},{10,11... | collective-permute-start | bytes 835592 | tf_op jit(solution)/shard_map/ppermute | solution.py:24
  556.6 3.8 collective-permute-start.30
  563.9 26.4 %collective-permute-start.52 = (bf16[1,1,2,2,136,1088]{5,4,3,2,1,0:T(8,128)(2,1)S(1)}, bf16[1,1,2,2,136,1088]{5,4,3,2,1,0:T(8,128)(2,1)S(1)}, u32[]{:S(2)}, u32[]{:S(2)}) collective-permute-start(bf16[1,1,2,2,136,1088]{5,4,3,2,1,0:T(8,128)(2,1)S(1)} %slice.615), channel_id=1, source_target_pairs={{0,16},{8,24},{16,0},{24,8},{1,17},{9,25},{17,1},{25,9},{2,18},{10... | collective-permute-start | bytes 3551240 | tf_op jit(solution)/shard_map/ppermute | solution.py:28
  565.3 26.9 %collective-permute-start.60 = (bf16[1,1,2,2,136,1088]{5,4,3,2,1,0:T(8,128)(2,1)S(1)}, bf16[1,1,2,2,136,1088]{5,4,3,2,1,0:T(8,128)(2,1)S(1)}, u32[]{:S(2)}, u32[]{:S(2)}) collective-permute-start(bf16[1,1,2,2,136,1088]{5,4,3,2,1,0:T(8,128)(2,1)S(1)} %slice.631), channel_id=1, source_target_pairs={{0,8},{8,0},{16,24},{24,16},{1,9},{9,1},{17,25},{25,17},{2,10},{10... | collective-permute-start | bytes 3551240 | tf_op jit(solution)/shard_map/ppermute | solution.py:28
  590.6 25.2 %collective-permute-start.53 = (bf16[1,1,2,1,136,1088]{5,4,3,2,1,0:T(8,128)(2,1)S(1)}, bf16[1,1,2,1,136,1088]{5,4,3,2,1,0:T(8,128)(2,1)S(1)}, u32[]{:S(2)}, u32[]{:S(2)}) collective-permute-start(bf16[1,1,2,1,136,1088]{5,4,3,2,1,0:T(8,128)(2,1)S(1)} %slice.617), channel_id=1, source_target_pairs={{0,2},{2,0},{4,6},{6,4},{1,3},{3,1},{5,7},{7,5},{8,10},{10,8},{12,... | collective-permute-start | bytes 1775624 | tf_op jit(solution)/shard_map/ppermute | solution.py:28
  592.6 25.4 %collective-permute-start.61 = (bf16[1,1,2,1,136,1088]{5,4,3,2,1,0:T(8,128)(2,1)S(1)}, bf16[1,1,2,1,136,1088]{5,4,3,2,1,0:T(8,128)(2,1)S(1)}, u32[]{:S(2)}, u32[]{:S(2)}) collective-permute-start(bf16[1,1,2,1,136,1088]{5,4,3,2,1,0:T(8,128)(2,1)S(1)} %slice.633), channel_id=1, source_target_pairs={{0,2},{2,0},{4,6},{6,4},{1,3},{3,1},{5,7},{7,5},{8,10},{10,8},{12,... | collective-permute-start | bytes 1775624 | tf_op jit(solution)/shard_map/ppermute | solution.py:28
  613.7 25.4 %collective-permute-start.36 = (bf16[2,1,2,2,72,816]{5,4,3,2,1,0:T(8,128)(2,1)S(1)}, bf16[2,1,2,2,72,816]{5,4,3,2,1,0:T(8,128)(2,1)S(1)}, u32[]{:S(2)}, u32[]{:S(2)}) collective-permute-start(bf16[2,1,2,2,72,816]{5,4,3,2,1,0:T(8,128)(2,1)S(1)} %slice.584), channel_id=1, source_target_pairs={{0,8},{8,0},{16,24},{24,16},{1,9},{9,1},{17,25},{25,17},{2,10},{10... | collective-permute-start | bytes 2820104 | tf_op jit(solution)/shard_map/ppermute | solution.py:28
  614.3 23.9 %collective-permute-start.32 = (bf16[1,2,2,2,64,816]{5,4,3,2,1,0:T(8,128)(2,1)S(1)}, bf16[1,2,2,2,64,816]{5,4,3,2,1,0:T(8,128)(2,1)S(1)}, u32[]{:S(2)}, u32[]{:S(2)}) collective-permute-start(bf16[1,2,2,2,64,816]{5,4,3,2,1,0:T(8,128)(2,1)S(1)} %bitcast.255), channel_id=1, source_target_pairs={{0,16},{8,24},{16,0},{24,8},{1,17},{9,25},{17,1},{25,9},{2,18},{10... | collective-permute-start | bytes 2506760 | tf_op jit(solution)/shard_map/ppermute | solution.py:28
  616.0 21.4 %collective-permute-start.54 = (bf16[1,1,1,1,136,1088]{5,4,3,2,1,0:T(8,128)(2,1)S(1)}, bf16[1,1,1,1,136,1088]{5,4,3,2,1,0:T(8,128)(2,1)S(1)}, u32[]{:S(2)}, u32[]{:S(2)}) collective-permute-start(bf16[1,1,1,1,136,1088]{5,4,3,2,1,0:T(8,128)(2,1)S(1)} %slice.619), channel_id=1, source_target_pairs={{0,4},{2,6},{4,0},{6,2},{1,5},{3,7},{5,1},{7,3},{8,12},{10,14},{12... | collective-permute-start | bytes 887816 | tf_op jit(solution)/shard_map/ppermute | solution.py:28
  618.2 24.0 %collective-permute-start.62 = (bf16[1,1,1,1,136,1088]{5,4,3,2,1,0:T(8,128)(2,1)S(1)}, bf16[1,1,1,1,136,1088]{5,4,3,2,1,0:T(8,128)(2,1)S(1)}, u32[]{:S(2)}, u32[]{:S(2)}) collective-permute-start(bf16[1,1,1,1,136,1088]{5,4,3,2,1,0:T(8,128)(2,1)S(1)} %slice.635), channel_id=1, source_target_pairs={{0,4},{2,6},{4,0},{6,2},{1,5},{3,7},{5,1},{7,3},{8,12},{10,14},{12... | collective-permute-start | bytes 887816 | tf_op jit(solution)/shard_map/ppermute | solution.py:28
  638.6 9.1 %collective-permute-start.33 = (bf16[1,1,2,2,64,816]{5,4,3,2,1,0:T(8,128)(2,1)S(1)}, bf16[1,1,2,2,64,816]{5,4,3,2,1,0:T(8,128)(2,1)S(1)}, u32[]{:S(2)}, u32[]{:S(2)}) collective-permute-start(bf16[1,1,2,2,64,816]{5,4,3,2,1,0:T(8,128)(2,1)S(1)} %slice.577), channel_id=1, source_target_pairs={{0,8},{8,0},{16,24},{24,16},{1,9},{9,1},{17,25},{25,17},{2,10},{10... | collective-permute-start | bytes 1253384 | tf_op jit(solution)/shard_map/ppermute | solution.py:28
  639.4 11.3 %collective-permute-start.37 = (bf16[1,1,2,2,72,816]{5,4,3,2,1,0:T(8,128)(2,1)S(1)}, bf16[1,1,2,2,72,816]{5,4,3,2,1,0:T(8,128)(2,1)S(1)}, u32[]{:S(2)}, u32[]{:S(2)}) collective-permute-start(bf16[1,1,2,2,72,816]{5,4,3,2,1,0:T(8,128)(2,1)S(1)} %slice.586), channel_id=1, source_target_pairs={{0,16},{8,24},{16,0},{24,8},{1,17},{9,25},{17,1},{25,9},{2,18},{10... | collective-permute-start | bytes 1410056 | tf_op jit(solution)/shard_map/ppermute | solution.py:28
  647.8 9.8 %collective-permute-start.34 = (bf16[1,1,2,1,64,816]{5,4,3,2,1,0:T(8,128)(2,1)S(1)}, bf16[1,1,2,1,64,816]{5,4,3,2,1,0:T(8,128)(2,1)S(1)}, u32[]{:S(2)}, u32[]{:S(2)}) collective-permute-start(bf16[1,1,2,1,64,816]{5,4,3,2,1,0:T(8,128)(2,1)S(1)} %slice.579), channel_id=1, source_target_pairs={{0,2},{2,0},{4,6},{6,4},{1,3},{3,1},{5,7},{7,5},{8,10},{10,8},{12,... | collective-permute-start | bytes 626696 | tf_op jit(solution)/shard_map/ppermute | solution.py:28
  650.9 9.7 %collective-permute-start.38 = (bf16[1,1,2,1,72,816]{5,4,3,2,1,0:T(8,128)(2,1)S(1)}, bf16[1,1,2,1,72,816]{5,4,3,2,1,0:T(8,128)(2,1)S(1)}, u32[]{:S(2)}, u32[]{:S(2)}) collective-permute-start(bf16[1,1,2,1,72,816]{5,4,3,2,1,0:T(8,128)(2,1)S(1)} %slice.588), channel_id=1, source_target_pairs={{0,2},{2,0},{4,6},{6,4},{1,3},{3,1},{5,7},{7,5},{8,10},{10,8},{12,... | collective-permute-start | bytes 705032 | tf_op jit(solution)/shard_map/ppermute | solution.py:28
  657.7 11.0 %collective-permute-start.35 = (bf16[1,1,1,1,64,816]{5,4,3,2,1,0:T(8,128)(2,1)S(1)}, bf16[1,1,1,1,64,816]{5,4,3,2,1,0:T(8,128)(2,1)S(1)}, u32[]{:S(2)}, u32[]{:S(2)}) collective-permute-start(bf16[1,1,1,1,64,816]{5,4,3,2,1,0:T(8,128)(2,1)S(1)} %slice.581), channel_id=1, source_target_pairs={{0,4},{2,6},{4,0},{6,2},{1,5},{3,7},{5,1},{7,3},{8,12},{10,14},{12... | collective-permute-start | bytes 313352 | tf_op jit(solution)/shard_map/ppermute | solution.py:28
  660.7 9.4 %collective-permute-start.39 = (bf16[1,1,1,1,72,816]{5,4,3,2,1,0:T(8,128)(2,1)S(1)}, bf16[1,1,1,1,72,816]{5,4,3,2,1,0:T(8,128)(2,1)S(1)}, u32[]{:S(2)}, u32[]{:S(2)}) collective-permute-start(bf16[1,1,1,1,72,816]{5,4,3,2,1,0:T(8,128)(2,1)S(1)} %slice.590), channel_id=1, source_target_pairs={{0,4},{2,6},{4,0},{6,2},{1,5},{3,7},{5,1},{7,3},{8,12},{10,14},{12... | collective-permute-start | bytes 352520 | tf_op jit(solution)/shard_map/ppermute | solution.py:28
  (80 other events, 836.9 us)
Sparse Core Ops, SparseCore 0:
  67.9 65.0 all-gather.4
  151.9 101.9 all-gather.6
